TPU v7x, 32 devices: a whole 2x2x4 slice. The times are simulated.
32 devices in a mesh: fsdp: 8 (over z, x), seq: 2 (over core), tensor: 2 (over y).
Axes of the slice: x: 2, y: 2, z: 4, core: 2. Of those that a mesh axis runs over, the one named last changes fastest.
Arguments:
- tokens: bfloat16 [4096, 768], P(('fsdp', 'seq', 'tensor')), may hold values from -6 to 6
- segments: int32 [4096], P('fsdp'), may hold values from 0 to 2, as said below
- grad_out: bfloat16 [4096, 768], P('fsdp'), may hold values from -6 to 6
- w_qkv: bfloat16 [3, 768, 768], P(None, 'fsdp', ('seq', 'tensor')), may hold values from -0.21875 to 0.21875
- b_qv: bfloat16 [2, 768], P(None, ('seq', 'tensor', 'fsdp')), may hold values from -3 to 3
- w_out: bfloat16 [768, 768], P(('seq', 'tensor'), 'fsdp'), may hold values from -0.875 to 0.875
- b_out: bfloat16 [768], P('fsdp'), may hold values from -2 to 2
- w_fc: bfloat16 [768, 3072], P('fsdp', ('seq', 'tensor')), may hold values from -0.21875 to 0.21875
- b_fc: bfloat16 [3072], P(('seq', 'tensor', 'fsdp')), may hold values from -3 to 3
- w_proj: bfloat16 [3072, 768], P(('seq', 'tensor'), 'fsdp'), may hold values from -0.109375 to 0.109375
- b_proj: bfloat16 [768], P('fsdp'), may hold values from -2 to 2
- ln1_gain: bfloat16 [768], P('fsdp'), may hold values from 0.5 to 1.5
- ln1_bias: bfloat16 [768], P('fsdp'), may hold values from -2 to 2
- ln2_gain: bfloat16 [768], P('fsdp'), may hold values from 0.5 to 1.5
- ln2_bias: bfloat16 [768], P('fsdp'), may hold values from -2 to 2
Outputs:
- output: bfloat16 [4096, 768], P(('fsdp', 'seq', 'tensor'))
- grad_tokens: float32 [4096, 768], P(('fsdp', 'seq', 'tensor'))
- grad_w_qkv: float32 [3, 768, 768], P(None, 'fsdp', ('seq', 'tensor'))
- grad_w_out: float32 [768, 768], P(('seq', 'tensor'), 'fsdp')
- grad_w_fc: float32 [768, 3072], P('fsdp', ('seq', 'tensor'))
- grad_w_proj: float32 [3072, 768], P(('seq', 'tensor'), 'fsdp')
- grad_b_qv: float32 [2, 768], P(None, ('seq', 'tensor', 'fsdp'))
- grad_b_out: float32 [768], P('fsdp')
- grad_b_fc: float32 [3072], P(('seq', 'tensor', 'fsdp'))
- grad_b_proj: float32 [768], P('fsdp')
- grad_ln1_gain: float32 [768], P('fsdp')
- grad_ln1_bias: float32 [768], P('fsdp')
- grad_ln2_gain: float32 [768], P('fsdp')
- grad_ln2_bias: float32 [768], P('fsdp')
Inputs may be any that keep to these rules, and one draw needn't show every extreme that they name: `segments`: each sequence of 512 tokens holds three documents numbered 0, 1, 2 in order, each of 64 tokens or more; document 1 covers positions 224 to 287.
All inputs are finite; a program needn't handle non-finite values.
Results may differ from a plain program's by a relative error of at most 0.018.
Values may be sent and summed in bfloat16 or wider, within the bound.
No kernel may reach another device: no remote copies, remote signals or barrier semaphores. Data moves between devices by JAX's collectives and lax.ppermute only.
A program may use at most 64 MiB of HBM per device.

v0:
```python
import jax
import jax.numpy as jnp
from jax import lax
from jax.sharding import PartitionSpec as P

HEAD_DIM = 64


def norm_rows(values, gain, shift):
    center = values - jnp.mean(values, axis=-1, keepdims=True)
    spread = jnp.mean(center * center, axis=-1, keepdims=True)
    return center * lax.rsqrt(spread + 1e-05) * gain + shift


def gelu_tanh(values):
    return jax.nn.gelu(values, approximate=True)


def block_scores(q_block, keys_all, doc_block, doc_ids, offset):
    key_pos = jnp.arange(keys_all.shape[0], dtype=jnp.int32)
    query_pos = offset + jnp.arange(q_block.shape[0], dtype=jnp.int32)
    allowed = (doc_block[:, None] == doc_ids[None, :]) & (key_pos[None, :] <= query_pos[:, None])
    scores = (
        jnp.einsum("qhd,khd->hqk", q_block, keys_all, preferred_element_type=jnp.float32) * 0.125
    )
    return jnp.where(allowed[None], scores, -1e30)


def attend_forward(queries, keys_all, values_all, doc_ids):
    seq_rows = queries.shape[0]
    block_rows = min(512, seq_rows)

    def query_block(number):
        offset = number * block_rows
        scores = block_scores(queries, keys_all, doc_ids, doc_ids, offset)
        row_top = jnp.max(scores, axis=-1, keepdims=True)
        log_norm = row_top + jnp.log(jnp.sum(jnp.exp(scores - row_top), axis=-1, keepdims=True))
        probs = jnp.exp(scores - log_norm).astype(jnp.bfloat16)
        mixed = jnp.einsum("hqk,khd->qhd", probs, values_all, preferred_element_type=jnp.float32)
        return (mixed.astype(jnp.bfloat16), log_norm[..., 0])

    mixed, log_norm = lax.map(query_block, jnp.arange(seq_rows // block_rows, dtype=jnp.int32))
    return (mixed.reshape(seq_rows, -1), log_norm)


def attend_backward(queries, keys_all, values_all, doc_ids, log_norm, grad_mixed):
    seq_rows = queries.shape[0]
    block_rows = min(512, seq_rows)

    def query_block(carry, number):
        key_grad, value_grad = carry
        offset = number * block_rows
        scores = block_scores(queries, keys_all, doc_ids, doc_ids, offset)
        probs = jnp.exp(scores - log_norm[number][..., None])
        grad_probs = jnp.einsum(
            "qhd,khd->hqk", grad_mixed, values_all, preferred_element_type=jnp.float32
        )
        inner = jnp.sum(probs * grad_probs, axis=-1, keepdims=True)
        grad_scores = (probs * (grad_probs - inner)).astype(jnp.bfloat16)
        query_grad = (
            jnp.einsum("hqk,khd->qhd", grad_scores, keys_all, preferred_element_type=jnp.float32)
            * 0.125
        )
        key_grad = (
            key_grad
            + jnp.einsum("hqk,qhd->khd", grad_scores, queries, preferred_element_type=jnp.float32)
            * 0.125
        )
        value_grad = value_grad + jnp.einsum(
            "hqk,qhd->khd",
            probs.astype(jnp.bfloat16),
            grad_mixed,
            preferred_element_type=jnp.float32,
        )
        return ((key_grad, value_grad), query_grad)

    empty = jnp.zeros(keys_all.shape, jnp.float32)
    (key_grad, value_grad), query_grad = lax.scan(
        query_block, (empty, empty), jnp.arange(seq_rows // block_rows, dtype=jnp.int32)
    )
    return (query_grad.reshape(keys_all.shape), key_grad, value_grad)


def local(
    tokens,
    segments,
    grad_out,
    w_qkv,
    b_qv,
    w_out,
    b_out,
    w_fc,
    b_fc,
    w_proj,
    b_proj,
    ln1_gain,
    ln1_bias,
    ln2_gain,
    ln2_bias,
):
    (
        full_qkv,
        full_out,
        full_fc,
        full_proj,
        full_qv,
        full_bout,
        full_bfc,
        full_bproj,
        gain_one,
        shift_one,
        gain_two,
        shift_two,
    ) = (
        lax.all_gather(w_qkv, "fsdp", axis=1, tiled=True),
        lax.all_gather(w_out, "fsdp", axis=1, tiled=True),
        lax.all_gather(w_fc, "fsdp", axis=0, tiled=True),
        lax.all_gather(w_proj, "fsdp", axis=1, tiled=True),
        lax.all_gather(b_qv, "fsdp", axis=1, tiled=True),
        lax.all_gather(b_out, "fsdp", axis=0, tiled=True),
        lax.all_gather(b_fc, "fsdp", axis=0, tiled=True),
        lax.all_gather(b_proj, "fsdp", axis=0, tiled=True),
        lax.all_gather(ln1_gain, "fsdp", axis=0, tiled=True),
        lax.all_gather(ln1_bias, "fsdp", axis=0, tiled=True),
        lax.all_gather(ln2_gain, "fsdp", axis=0, tiled=True),
        lax.all_gather(ln2_bias, "fsdp", axis=0, tiled=True),
    )
    own_rows = tokens.shape[0]
    seq_rows = segments.shape[0]
    inputs = tokens.astype(jnp.float32)
    normed, ln_one_pull = jax.vjp(
        norm_rows, inputs, gain_one.astype(jnp.float32), shift_one.astype(jnp.float32)
    )
    seq_normed = lax.all_gather(normed.astype(jnp.bfloat16), ("seq", "tensor"), axis=0, tiled=True)
    projected = jnp.einsum("td,kde->kte", seq_normed, full_qkv, preferred_element_type=jnp.float32)
    bias_rows = jnp.stack([full_qv[0], jnp.zeros_like(full_qv[0]), full_qv[1]]).astype(jnp.float32)
    qkv_low = (projected + bias_rows[:, None, :]).astype(jnp.bfloat16)
    head_shape = (seq_rows, -1, HEAD_DIM)
    queries = qkv_low[0].reshape(head_shape)
    keys_all = qkv_low[1].reshape(head_shape)
    values_all = qkv_low[2].reshape(head_shape)
    mixed, log_norm = attend_forward(queries, keys_all, values_all, segments)
    middle = (
        inputs
        + lax.psum_scatter(
            jnp.dot(mixed, full_out, preferred_element_type=jnp.float32).astype(jnp.bfloat16),
            ("seq", "tensor"),
            scatter_dimension=0,
            tiled=True,
        ).astype(jnp.float32)
        + full_bout.astype(jnp.float32)
    )
    normed_two, ln_two_pull = jax.vjp(
        norm_rows, middle, gain_two.astype(jnp.float32), shift_two.astype(jnp.float32)
    )
    seq_normed_two = lax.all_gather(
        normed_two.astype(jnp.bfloat16), ("seq", "tensor"), axis=0, tiled=True
    )
    hidden = jnp.dot(seq_normed_two, full_fc, preferred_element_type=jnp.float32) + full_bfc.astype(
        jnp.float32
    )
    active, gelu_pull = jax.vjp(gelu_tanh, hidden)
    active_low = active.astype(jnp.bfloat16)
    result = (
        middle
        + lax.psum_scatter(
            jnp.dot(active_low, full_proj, preferred_element_type=jnp.float32).astype(jnp.bfloat16),
            ("seq", "tensor"),
            scatter_dimension=0,
            tiled=True,
        ).astype(jnp.float32)
        + full_bproj.astype(jnp.float32)
    )
    back_qkv, back_out, back_fc, back_proj = (
        lax.all_gather(w_qkv, "fsdp", axis=1, tiled=True),
        lax.all_gather(w_out, "fsdp", axis=1, tiled=True),
        lax.all_gather(w_fc, "fsdp", axis=0, tiled=True),
        lax.all_gather(w_proj, "fsdp", axis=1, tiled=True),
    )
    place = lax.axis_index("seq") * lax.axis_size("tensor") + lax.axis_index("tensor")
    cot_rows = lax.dynamic_slice_in_dim(grad_out, place * own_rows, own_rows, 0).astype(jnp.float32)
    grad_bproj = jnp.sum(cot_rows, axis=0)
    grad_wproj = jnp.einsum("tf,td->fd", active_low, grad_out, preferred_element_type=jnp.float32)
    grad_active = jnp.einsum("td,fd->tf", grad_out, back_proj, preferred_element_type=jnp.float32)
    grad_hidden = gelu_pull(grad_active)[0].astype(jnp.bfloat16)
    grad_bfc = jnp.sum(grad_hidden.astype(jnp.float32), axis=0)
    grad_wfc = jnp.einsum(
        "td,tf->df", seq_normed_two, grad_hidden, preferred_element_type=jnp.float32
    )
    grad_normed_two = lax.psum_scatter(
        jnp.einsum("tf,df->td", grad_hidden, back_fc, preferred_element_type=jnp.float32).astype(
            jnp.bfloat16
        ),
        ("seq", "tensor"),
        scatter_dimension=0,
        tiled=True,
    ).astype(jnp.float32)
    grad_mid_norm, grad_gain_two, grad_shift_two = ln_two_pull(grad_normed_two)
    grad_middle = cot_rows + grad_mid_norm
    grad_bout = jnp.sum(grad_middle, axis=0)
    seq_grad_mid = lax.all_gather(
        grad_middle.astype(jnp.bfloat16), ("seq", "tensor"), axis=0, tiled=True
    )
    grad_wout = jnp.einsum("te,td->ed", mixed, seq_grad_mid, preferred_element_type=jnp.float32)
    grad_attn = jnp.einsum(
        "td,ed->te", seq_grad_mid, back_out, preferred_element_type=jnp.float32
    ).astype(jnp.bfloat16)
    query_grad, key_grad, value_grad = attend_backward(
        queries, keys_all, values_all, segments, log_norm, grad_attn.reshape(head_shape)
    )
    grad_qkv = (
        jnp.stack([query_grad, key_grad, value_grad]).reshape(3, seq_rows, -1).astype(jnp.bfloat16)
    )
    grad_wqkv = jnp.einsum("td,kte->kde", seq_normed, grad_qkv, preferred_element_type=jnp.float32)
    grad_bqv = jnp.stack(
        [
            jnp.sum(grad_qkv[0].astype(jnp.float32), axis=0),
            jnp.sum(grad_qkv[2].astype(jnp.float32), axis=0),
        ]
    )
    grad_normed = lax.psum_scatter(
        jnp.einsum("kte,kde->td", grad_qkv, back_qkv, preferred_element_type=jnp.float32).astype(
            jnp.bfloat16
        ),
        ("seq", "tensor"),
        scatter_dimension=0,
        tiled=True,
    ).astype(jnp.float32)
    grad_in_norm, grad_gain_one, grad_shift_one = ln_one_pull(grad_normed)
    grad_inputs = grad_middle + grad_in_norm
    sum_bout, sum_bproj, sum_gain_one, sum_shift_one, sum_gain_two, sum_shift_two = lax.psum(
        (grad_bout, grad_bproj, grad_gain_one, grad_shift_one, grad_gain_two, grad_shift_two),
        ("seq", "tensor"),
    )
    owned = (
        lax.psum_scatter(grad_wqkv, "fsdp", scatter_dimension=1, tiled=True),
        lax.psum_scatter(grad_wout, "fsdp", scatter_dimension=1, tiled=True),
        lax.psum_scatter(grad_wfc, "fsdp", scatter_dimension=0, tiled=True),
        lax.psum_scatter(grad_wproj, "fsdp", scatter_dimension=1, tiled=True),
        lax.psum_scatter(grad_bqv, "fsdp", scatter_dimension=1, tiled=True),
        lax.psum_scatter(sum_bout, "fsdp", scatter_dimension=0, tiled=True),
        lax.psum_scatter(grad_bfc, "fsdp", scatter_dimension=0, tiled=True),
        lax.psum_scatter(sum_bproj, "fsdp", scatter_dimension=0, tiled=True),
        lax.psum_scatter(sum_gain_one, "fsdp", scatter_dimension=0, tiled=True),
        lax.psum_scatter(sum_shift_one, "fsdp", scatter_dimension=0, tiled=True),
        lax.psum_scatter(sum_gain_two, "fsdp", scatter_dimension=0, tiled=True),
        lax.psum_scatter(sum_shift_two, "fsdp", scatter_dimension=0, tiled=True),
    )
    return (
        result.astype(jnp.bfloat16),
        grad_inputs,
        owned[0],
        owned[1],
        owned[2],
        owned[3],
        owned[4],
        owned[5],
        owned[6],
        owned[7],
        owned[8],
        owned[9],
        owned[10],
        owned[11],
    )


def solution(mesh):
    in_specs = (
        P(("fsdp", "seq", "tensor"), None),
        P("fsdp"),
        P("fsdp", None),
        P(None, "fsdp", ("seq", "tensor")),
        P(None, ("seq", "tensor", "fsdp")),
        P(("seq", "tensor"), "fsdp"),
        P("fsdp"),
        P("fsdp", ("seq", "tensor")),
        P(("seq", "tensor", "fsdp")),
        P(("seq", "tensor"), "fsdp"),
        P("fsdp"),
        P("fsdp"),
        P("fsdp"),
        P("fsdp"),
        P("fsdp"),
    )
    out_specs = (
        P(("fsdp", "seq", "tensor"), None),
        P(("fsdp", "seq", "tensor"), None),
        P(None, "fsdp", ("seq", "tensor")),
        P(("seq", "tensor"), "fsdp"),
        P("fsdp", ("seq", "tensor")),
        P(("seq", "tensor"), "fsdp"),
        P(None, ("seq", "tensor", "fsdp")),
        P("fsdp"),
        P(("seq", "tensor", "fsdp")),
        P("fsdp"),
        P("fsdp"),
        P("fsdp"),
        P("fsdp"),
        P("fsdp"),
    )
    return jax.shard_map(local, mesh=mesh, in_specs=in_specs, out_specs=out_specs, check_vma=False)
```

profile of v0, /device:TPU:0, one launch (start us, length us, event | category | flops | bytes accessed | tf_op | source)
XLA Modules:
  0.0 644.1 jit_solution(5961437092864837091)
XLA Ops:
  18.7 39.4 %all-reduce.17 = (bf16[768]{0:T(1024)(128)(2,1)S(1)}, bf16[768]{0:T(1024)(128)(2,1)S(1)}, bf16[768]{0:T(1024)(128)(2,1)S(1)}, bf16[768]{0:T(1024)(128)(2,1)S(1)}...) all-reduce(bf16[768]{0:T(1024)(128)(2,1)S(1)} %dynamic-update-slice, ...), channel_id=1, replica_groups=mesh['fsdp'=8,'seq'=2,'tensor'=2] {'fsdp'}, use_global_device_ids=true, to_apply=%add.4 | all-reduce | flops 5376 | bytes 21504
  58.1 16.4 %all-gather = bf16[8,24,2]{1,2,0:T(2,128)(2,1)S(1)} all-gather(bf16[1,24,2]{1,2,0:T(2,128)(2,1)} %bitcast.103), channel_id=1, replica_groups=mesh['fsdp'=8,'seq'=2,'tensor'=2] {'fsdp'}, dimensions={0}, use_global_device_ids=true | all-gather | bytes 864 | tf_op jit(solution)/shard_map/all_gather | solution.py:119
  78.2 33.0 %all_gather.54 = bf16[192,768]{0,1:T(8,128)(2,1)} all-gather(bf16[192,96]{0,1:T(8,128)(2,1)S(1)} %copy.48), channel_id=1, replica_groups=mesh['fsdp'=8,'seq'=2,'tensor'=2] {'fsdp'}, dimensions={1}, use_global_device_ids=true | all-gather | bytes 331776 | tf_op jit(solution)/shard_map/all_gather | solution.py:116
  111.3 16.3 %all_gather.51 = bf16[512,768]{1,0:T(8,128)(2,1)S(1)} all-gather(bf16[128,768]{1,0:T(8,128)(2,1)S(1)} %fusion.23), channel_id=1, replica_groups=mesh['fsdp'=8,'seq'=2,'tensor'=2] {'seq','tensor'}, dimensions={0}, use_global_device_ids=true | all-gather | bytes 983040 | tf_op jit(solution)/shard_map/all_gather | solution.py:134
  127.6 36.0 %all_gather.52 = bf16[3,768,192]{2,0,1:T(4,128)(2,1)S(1)} all-gather(bf16[3,96,192]{2,0,1:T(4,128)(2,1)S(1)} %copy.44), channel_id=1, replica_groups=mesh['fsdp'=8,'seq'=2,'tensor'=2] {'fsdp'}, dimensions={1}, use_global_device_ids=true | all-gather | bytes 995328 | tf_op jit(solution)/shard_map/all_gather | solution.py:115
  171.9 20.9 %reduce-scatter.14.cloned.1.call-done = bf16[128,768]{1,0:T(8,128)(2,1)} async-done(((bf16[512,768]{1,0:T(8,128)(2,1)}), bf16[128,768]{1,0:T(8,128)(2,1)}) %reduce-scatter.14.cloned.1.call-update) | async-done | bytes 196624 | tf_op jit(solution)/shard_map/reduce_scatter | solution.py:145
  196.1 16.4 %all_gather.58 = bf16[512,768]{1,0:T(8,128)(2,1)} all-gather(bf16[128,768]{1,0:T(8,128)(2,1)S(1)} %add_convert_fusion.2), channel_id=1, replica_groups=mesh['fsdp'=8,'seq'=2,'tensor'=2] {'seq','tensor'}, dimensions={0}, use_global_device_ids=true | all-gather | bytes 983040 | tf_op jit(solution)/shard_map/all_gather | solution.py:156
  213.8 3.5 fusion.47
  217.3 38.9 %all-gather.4.cloned.1.call-done = bf16[768,768]{1,0:T(8,128)(2,1)} async-done(((bf16[96,768]{1,0:T(8,128)(2,1)}), bf16[768,768]{1,0:T(8,128)(2,1)}) %all-gather.4.cloned.1.call-update) | async-done | bytes 1179664 | tf_op jit(solution)/shard_map/all_gather | solution.py:117
  256.1 5.5 convert_reduce_fusion
  264.3 3.7 convolution_convert_fusion.1
  269.0 17.2 %reduce-scatter.18.cloned.1.call-done = bf16[128,768]{1,0:T(8,128)(2,1)} async-done(((bf16[512,768]{1,0:T(8,128)(2,1)}), bf16[128,768]{1,0:T(8,128)(2,1)}) %reduce-scatter.18.cloned.1.call-update) | async-done | bytes 196624 | tf_op jit(solution)/shard_map/reduce_scatter | solution.py:190
  286.2 1.7 convert_reduce_fusion.2
  289.1 1.8 fusion.28
  291.4 20.6 %reduce-scatter.16.cloned.1.call-done = bf16[128,768]{1,0:T(8,128)(2,1)} async-done(((bf16[512,768]{1,0:T(8,128)(2,1)}), bf16[128,768]{1,0:T(8,128)(2,1)}) %reduce-scatter.16.cloned.1.call-update) | async-done | bytes 196624 | tf_op jit(solution)/shard_map/reduce_scatter | solution.py:166
  312.0 2.7 fusion.42
  315.5 16.3 %all_gather.63 = bf16[512,768]{1,0:T(8,128)(2,1)S(1)} all-gather(bf16[128,768]{1,0:T(8,128)(2,1)S(1)} %convert_element_type.140), channel_id=1, replica_groups=mesh['fsdp'=8,'seq'=2,'tensor'=2] {'seq','tensor'}, dimensions={0}, use_global_device_ids=true | all-gather | bytes 983040 | tf_op jit(solution)/shard_map/all_gather | solution.py:201
  334.5 2.3 multiply_reduce_fusion
  340.7 1.8 bitcast_convert_fusion
  342.5 2.9 convolution_bitcast_fusion
  345.4 3.0 copy.58
  348.3 2.8 reshape.235
  352.3 3.9 fusion.40
  357.5 2.2 fusion.48
  361.5 35.5 %reduce-scatter.28.cloned.1.call-done = f32[96,192]{1,0:T(8,128)} async-done(((f32[768,192]{1,0:T(8,128)}), f32[96,192]{1,0:T(8,128)}) %reduce-scatter.28.cloned.1.call-update) | async-done | bytes 73744
  398.6 23.2 %reduce-scatter.20.cloned.1.call-done = bf16[128,768]{1,0:T(8,128)(2,1)} async-done(((bf16[512,768]{1,0:T(8,128)(2,1)}), bf16[128,768]{1,0:T(8,128)(2,1)}) %reduce-scatter.20.cloned.1.call-update) | async-done | bytes 196624 | tf_op jit(solution)/shard_map/reduce_scatter | solution.py:221
  424.3 37.7 %all-reduce.15 = (f32[2,192]{1,0:T(2,128)S(1)}, f32[768]{0:T(1024)S(1)}, f32[768]{0:T(1024)S(1)}, f32[768]{0:T(1024)S(1)}, f32[768]{0:T(1024)S(1)}, /*index=5*/f...) all-reduce(f32[2,192]{1,0:T(2,128)S(1)} %pad_maximum_fusion.3, ...), channel_id=10, replica_groups=mesh['fsdp'=8,'seq'=2,'tensor'=2] {'fsdp'}, use_global_device_ids=true, to_apply=%region_21.22.clone | all-reduce | flops 5760 | bytes 46080
  463.0 6.8 %all-reduce.16 = (f32[96]{0:T(128)}, f32[96]{0:T(128)}, f32[96]{0:T(128)}, f32[96]{0:T(128)}, f32[96]{0:T(128)}, /*index=5*/f32[96]{0:T(128)}) all-reduce(f32[96]{0:T(128)S(1)} %dynamic-slice.10, f32[96]{0:T(128)S(1)} %dynamic-slice.14, f32[96]{0:T(128)S(1)} %dynamic-slice.16, ...), channel_id=1, replica_groups=mesh['fsdp'=8,'seq'=2,'tensor'=2] {'seq','tensor'}, use_global_device_ids=true, to_apply=%region_23.24 | all-reduce | flops 576 | bytes 4608 | tf_op jit(solution)/shard_map/psum | solution.py:231
  470.4 1.9 add_add_fusion.2
  472.3 20.0 %reduce-scatter.26.cloned.1.call-done = f32[96,576]{1,0:T(8,128)} async-done(((f32[768,576]{1,0:T(8,128)}), f32[96,576]{1,0:T(8,128)}) %reduce-scatter.26.cloned.1.call-update) | async-done | bytes 221200
  494.2 70.8 %reduce-scatter.24.cloned.1.call-done = f32[768,96]{0,1:T(8,128)} async-done(((f32[768,768]{0,1:T(8,128)}), f32[768,96]{0,1:T(8,128)}) %reduce-scatter.24.cloned.1.call-update) | async-done | bytes 294928 | tf_op jit(solution)/shard_map/reduce_scatter | solution.py:239
  565.0 72.0 %reduce-scatter.22.cloned.1.call-done = f32[96,768]{1,0:T(8,128)} async-done(((f32[768,768]{1,0:T(8,128)}), f32[96,768]{1,0:T(8,128)}) %reduce-scatter.22.cloned.1.call-update) | async-done | bytes 294928 | tf_op jit(solution)/shard_map/reduce_scatter | solution.py:238
  (190 shorter events, 49.4 us)
Async XLA Ops:
  8.0 103.1 %copy-start = (bf16[128,768]{1,0:T(8,128)(2,1)S(1)}, bf16[128,768]{1,0:T(8,128)(2,1)}, u32[]{:S(2)}) copy-start(bf16[128,768]{1,0:T(8,128)(2,1)} %param.15) | copy-start | bytes 589828
  8.0 184.8 %reduce-scatter.14.cloned.1.call-start = ((), (), s32[]{:S(2)}) async-start(), calls=%async_computation.8 | async-start | bytes 983040 | tf_op jit(solution)/shard_map/reduce_scatter | solution.py:145
  9.2 118.4 %copy-start.34 = (f32[128]{0:T(128)}, f32[128]{0:T(128)S(1)}, u32[]{:S(2)}) copy-start(f32[128]{0:T(128)S(1)} %broadcast_multiply_fusion.1) | copy-start | bytes 1540
  10.8 116.8 %copy-start.37 = (f32[128]{0:T(128)}, f32[128]{0:T(128)S(1)}, u32[]{:S(2)}) copy-start(f32[128]{0:T(128)S(1)} %fusion.33) | copy-start | bytes 1540
  127.6 36.9 %copy-start.11 = (bf16[512,768]{1,0:T(8,128)(2,1)}, bf16[512,768]{1,0:T(8,128)(2,1)S(1)}, u32[]{:S(2)}) copy-start(bf16[512,768]{1,0:T(8,128)(2,1)S(1)} %all_gather.51) | copy-start | bytes 2359300
  165.5 2.2 copy-start.21
  170.7 43.1 %all-gather.6.cloned.1.call-start = ((), (), s32[]{:S(2)}) async-start(), calls=%async_computation.10 | async-start | bytes 1327104 | tf_op jit(solution)/shard_map/all_gather | solution.py:118
  171.3 84.8 %all-gather.4.cloned.1.call-start = ((), (), s32[]{:S(2)}) async-start(), calls=%async_computation.9 | async-start | bytes 1327104 | tf_op jit(solution)/shard_map/all_gather | solution.py:117
  171.9 114.3 %reduce-scatter.18.cloned.1.call-start = ((), (), s32[]{:S(2)}) async-start(), calls=%async_computation.12 | async-start | bytes 983040 | tf_op jit(solution)/shard_map/reduce_scatter | solution.py:190
  193.9 23.4 %copy-start.36 = (f32[128]{0:T(128)}, f32[128]{0:T(128)S(1)}, u32[]{:S(2)}) copy-start(f32[128]{0:T(128)S(1)} %broadcast_multiply_fusion) | copy-start | bytes 1540
  195.0 22.2 %copy-start.44 = (f32[128]{0:T(128)}, f32[128]{0:T(128)S(1)}, u32[]{:S(2)}) copy-start(f32[128]{0:T(128)S(1)} %multiply_reduce_fusion.1) | copy-start | bytes 1540
  195.0 22.2 %copy-start.39 = (f32[128]{0:T(128)}, f32[128]{0:T(128)S(1)}, u32[]{:S(2)}) copy-start(f32[128]{0:T(128)S(1)} %fusion.34) | copy-start | bytes 1540
  256.1 6.4 copy-start.45
  264.2 47.8 %reduce-scatter.16.cloned.1.call-start = ((), (), s32[]{:S(2)}) async-start(), calls=%async_computation.11 | async-start | bytes 983040 | tf_op jit(solution)/shard_map/reduce_scatter | solution.py:166
  264.3 21.9 %copy-start.1 = (bf16[128,768]{1,0:T(8,128)(2,1)S(1)}, bf16[128,768]{1,0:T(8,128)(2,1)}, u32[]{:S(2)}) copy-start(bf16[128,768]{1,0:T(8,128)(2,1)} %reduce-scatter.14.cloned.1.call-done) | copy-start | bytes 589828
  268.1 128.9 %reduce-scatter.28.cloned.1.call-start = ((), (), s32[]{:S(2)}) async-start(), calls=%async_computation.17 | async-start | bytes 884736
  312.0 19.8 %copy-start.10 = (bf16[192,768]{0,1:T(8,128)(2,1)S(1)}, bf16[192,768]{0,1:T(8,128)(2,1)}, u32[]{:S(2)}) copy-start(bf16[192,768]{0,1:T(8,128)(2,1)} %all_gather.54) | copy-start | bytes 884740
  314.8 18.2 %copy-start.18 = (bf16[3,64,512]{2,1,0:T(8,128)(2,1)S(1)}, bf16[3,64,512]{2,1,0:T(8,128)(2,1)}, u32[]{:S(2)}) copy-start(bf16[3,64,512]{2,1,0:T(8,128)(2,1)} %copy-done.17) | copy-start | bytes 589828
  334.4 87.5 %reduce-scatter.20.cloned.1.call-start = ((), (), s32[]{:S(2)}) async-start(), calls=%async_computation.13 | async-start | bytes 983040 | tf_op jit(solution)/shard_map/reduce_scatter | solution.py:221
  334.4 2.3 copy-start.3
  342.5 149.8 %reduce-scatter.26.cloned.1.call-start = ((), (), s32[]{:S(2)}) async-start(), calls=%async_computation.16 | async-start | bytes 2211840
  351.2 213.9 %reduce-scatter.24.cloned.1.call-start = ((), (), s32[]{:S(2)}) async-start(), calls=%async_computation.15 | async-start | bytes 2654208 | tf_op jit(solution)/shard_map/reduce_scatter | solution.py:239
  356.2 280.8 %reduce-scatter.22.cloned.1.call-start = ((), (), s32[]{:S(2)}) async-start(), calls=%async_computation.14 | async-start | bytes 2654208 | tf_op jit(solution)/shard_map/reduce_scatter | solution.py:238
  359.7 62.1 %copy-start.35 = (f32[128]{0:T(128)S(1)}, f32[128]{0:T(128)}, u32[]{:S(2)}) copy-start(f32[128]{0:T(128)} %copy-done.34) | copy-start | bytes 1540
  359.7 63.3 %copy-start.43 = (f32[128]{0:T(128)S(1)}, f32[128]{0:T(128)}, u32[]{:S(2)}) copy-start(f32[128]{0:T(128)} %copy-done.42) | copy-start | bytes 1540
  359.7 63.3 %copy-start.38 = (f32[128]{0:T(128)S(1)}, f32[128]{0:T(128)}, u32[]{:S(2)}) copy-start(f32[128]{0:T(128)} %copy-done.37) | copy-start | bytes 1540
  359.7 64.5 %copy-start.30 = (f32[768]{0:T(1024)S(1)}, f32[768]{0:T(1024)}, u32[]{:S(2)}) copy-start(f32[768]{0:T(1024)} %get-tuple-element.111) | copy-start | bytes 9220
  359.7 64.5 %copy-start.31 = (f32[768]{0:T(1024)S(1)}, f32[768]{0:T(1024)}, u32[]{:S(2)}) copy-start(f32[768]{0:T(1024)} %get-tuple-element.107) | copy-start | bytes 9220
  359.7 64.5 %copy-start.32 = (f32[768]{0:T(1024)S(1)}, f32[768]{0:T(1024)}, u32[]{:S(2)}) copy-start(f32[768]{0:T(1024)} %get-tuple-element.138) | copy-start | bytes 9220
  359.8 64.5 %copy-start.33 = (f32[768]{0:T(1024)S(1)}, f32[768]{0:T(1024)}, u32[]{:S(2)}) copy-start(f32[768]{0:T(1024)} %get-tuple-element.140) | copy-start | bytes 9220
  359.8 64.5 %copy-start.40 = (f32[768]{0:T(1024)S(1)}, f32[768]{0:T(1024)}, u32[]{:S(2)}) copy-start(f32[768]{0:T(1024)} %get-tuple-element.136) | copy-start | bytes 9220
  359.8 110.6 %copy-start.8 = (f32[128,768]{1,0:T(8,128)S(1)}, f32[128,768]{1,0:T(8,128)}, u32[]{:S(2)}) copy-start(f32[128,768]{1,0:T(8,128)} %copy-done.7) | copy-start | bytes 1179652
  (24 other events, 27.7 us)
Sparse Core Ops, SparseCore 0:
  170.8 21.9 reduce-scatter.13
  264.4 21.7 reduce-scatter.17
  288.7 23.2 reduce-scatter.15
Sparse Core Ops, SparseCore 1:
  173.6 40.2 all-gather.5
  216.1 40.0 all-gather.3
  334.5 62.5 reduce-scatter.27
  399.6 22.2 reduce-scatter.19
  425.7 66.5 reduce-scatter.25
  496.4 68.6 reduce-scatter.23
  569.0 68.0 reduce-scatter.21
where the time goes:
time: 645 us; the launch traced here: 644 us
  waiting for transfers between devices  321 us (50%)
  blocking collectives  218 us (34%)
  matrix products  35.5 us (6%)
  local copies, waits for them, and re-layouts  28.6 us (4%)
  other arithmetic  21.9 us (3%)
  between operations  18 us (3%)
    unnamed x2, blocking collectives  77.1 us
    reduce_scatter x1, waiting for transfers between devices, local(): lax.psum_scatter(grad_wfc, 'fsdp', scatter_dimension=0, tiled=True)  72 us
    reduce_scatter x1, waiting for transfers between devices, local(): lax.psum_scatter(grad_wproj, 'fsdp', scatter_dimension=1, tiled=True)  70.8 us
    unnamed x12, waiting for transfers between devices  56.7 us
    all_gather x1, waiting for transfers between devices, local(): lax.all_gather(w_fc, 'fsdp', axis=0, tiled=True)  38.9 us
    all_gather x1, blocking collectives, local(): lax.all_gather(w_qkv, 'fsdp', axis=1, tiled=True)  36 us
    all_gather x1, blocking collectives, local(): lax.all_gather(w_out, 'fsdp', axis=1, tiled=True)  33 us
    unnamed x123, local copies, waits for them, and re-layouts  27.6 us
  transfers between devices with their start and end apart: 10, of which 10 were waited for; matrix products, arithmetic and copies ran while one was open for 7% of the time, Pallas kernels for 0%

commit v1 on v0

v1 whole, which is shorter than its diff:
```python
import jax
import jax.numpy as jnp
from jax import lax
from jax.sharding import PartitionSpec as P

HEAD_DIM = 64
DIRECT_LIMIT = 8
LOW = jnp.bfloat16
F32 = jnp.float32


def norm_parts(values):
    center = values - jnp.mean(values, axis=-1, keepdims=True)
    spread = jnp.mean(center * center, axis=-1, keepdims=True)
    inverse = lax.rsqrt(spread + 1e-05)
    return center * inverse, inverse


def norm_back(cot, scaled, inverse, gain):
    inner = cot * gain
    first = jnp.mean(inner, axis=-1, keepdims=True)
    second = jnp.mean(inner * scaled, axis=-1, keepdims=True)
    return (inner - first - scaled * second) * inverse


def gelu_tanh(values):
    return jax.nn.gelu(values, approximate=True)


def dot(left, right, left_dim, right_dim):
    return lax.dot_general(
        left, right, (((left_dim,), (right_dim,)), ((), ())), preferred_element_type=F32
    )


def shifted(value, step):
    size = lax.axis_size("fsdp")
    return lax.ppermute(value, "fsdp", [(i, (i + step) % size) for i in range(size)])


def swap(value, axis):
    return lax.ppermute(value, axis, [(0, 1), (1, 0)])


def gather_chunks(chunk):
    size = lax.axis_size("fsdp")
    if size > DIRECT_LIMIT:
        return lax.all_gather(chunk, "fsdp", axis=0, tiled=False)
    return jnp.stack([chunk] + [shifted(chunk, -step) for step in range(1, size)])


def scatter_chunks(chunks):
    size = lax.axis_size("fsdp")
    if size > DIRECT_LIMIT:
        return lax.psum_scatter(chunks, "fsdp", scatter_dimension=0, tiled=False)
    total = chunks[0]
    low = chunks.astype(LOW)
    for step in range(1, size):
        total = total + shifted(low[step], step).astype(F32)
    return total


def turn(value, count, axis):
    return jnp.roll(value, -count, axis=axis)


def local(
    tokens,
    segments,
    grad_out,
    w_qkv,
    b_qv,
    w_out,
    b_out,
    w_fc,
    b_fc,
    w_proj,
    b_proj,
    ln1_gain,
    ln1_bias,
    ln2_gain,
    ln2_bias,
):
    size = lax.axis_size("fsdp")
    me = lax.axis_index("fsdp")
    chunk_rows = w_fc.shape[0]
    width = tokens.shape[1]
    own_rows = tokens.shape[0]
    seq_rows = segments.shape[0]
    hidden_cols = w_fc.shape[1]
    head_cols = w_out.shape[0]
    heads = head_cols // HEAD_DIM
    qkv_cols = 3 * head_cols
    offset = me * chunk_rows if size <= DIRECT_LIMIT else 0 * me
    place = lax.axis_index("seq") * 2 + lax.axis_index("tensor")

    vectors = jnp.concatenate(
        [b_out, b_proj, ln1_gain, ln1_bias, ln2_gain, ln2_bias, b_qv.reshape(-1), b_fc]
    )
    vector_rows = -(-vectors.shape[0] // qkv_cols)
    vectors = jnp.pad(vectors, (0, vector_rows * qkv_cols - vectors.shape[0]))
    first = jnp.concatenate(
        [w_qkv[0], w_qkv[1], w_qkv[2]], axis=1
    )
    first = jnp.concatenate([first, vectors.reshape(vector_rows, qkv_cols)], axis=0)
    second = jnp.concatenate([w_out.T, w_fc, w_proj.T], axis=1)
    own_tokens = turn(tokens, offset, 1)

    near = swap(own_tokens, "tensor")
    pair = jnp.concatenate([own_tokens, near])
    seq_tokens = jnp.concatenate([pair, swap(pair, "seq")])

    first_all = gather_chunks(first)
    second_all = gather_chunks(second)
    qkv_all = first_all[:, :chunk_rows].reshape(width, qkv_cols)
    vec_all = first_all[:, chunk_rows:].reshape(size, -1).astype(F32)
    d_vec = vec_all[:, : 6 * chunk_rows].reshape(size, 6, chunk_rows).transpose(1, 0, 2).reshape(6, width)
    bout_all, bproj_all, gain_one, shift_one, gain_two, shift_two = [d_vec[i] for i in range(6)]
    qv_count = b_qv.shape[1]
    rest = jnp.roll(vec_all[:, 6 * chunk_rows :], offset // chunk_rows, axis=0)
    qv_all = rest[:, : 2 * qv_count].reshape(size, 2, qv_count).transpose(1, 0, 2).reshape(2, head_cols)
    bfc_all = rest[:, 2 * qv_count : 2 * qv_count + chunk_rows * 0 + b_fc.shape[0]].reshape(hidden_cols)

    second_flat = second_all.reshape(width, -1)
    wo_own = second_flat[:, :head_cols]
    wf = second_flat[:, head_cols : head_cols + hidden_cols]
    wp = second_flat[:, head_cols + hidden_cols :]
    wo_pair = jnp.concatenate([wo_own, swap(wo_own, "tensor")], axis=1)
    wo_full = jnp.concatenate([wo_pair, swap(wo_pair, "seq")], axis=1)

    blocks = [place ^ b for b in range(4)]

    def in_order(value):
        return jnp.concatenate(
            [lax.dynamic_slice_in_dim(value, b * own_rows, own_rows, 0) for b in blocks]
        )

    docs = in_order(segments)
    cot = turn(in_order(grad_out), offset, 1)
    positions = jnp.concatenate([b * own_rows + jnp.arange(own_rows, dtype=jnp.int32) for b in blocks])
    allowed = (docs[:, None] == docs[None, :]) & (positions[None, :] <= positions[:, None])

    inputs = seq_tokens.astype(F32)
    scaled_one, inverse_one = norm_parts(inputs)
    normed = (scaled_one * gain_one + shift_one).astype(LOW)
    bias_row = jnp.concatenate([qv_all[0], jnp.zeros((head_cols,), F32), qv_all[1]])
    qkv_low = (dot(normed, qkv_all, 1, 0) + bias_row).astype(LOW)
    queries, keys, values = [
        qkv_low[:, i * head_cols : (i + 1) * head_cols].reshape(seq_rows, heads, HEAD_DIM)
        for i in range(3)
    ]
    scores = jnp.einsum("qhd,khd->hqk", queries, keys, preferred_element_type=F32) * 0.125
    scores = jnp.where(allowed[None], scores, -1e30)
    top = jnp.max(scores, axis=-1, keepdims=True)
    log_norm = top + jnp.log(jnp.sum(jnp.exp(scores - top), axis=-1, keepdims=True))
    probs = jnp.exp(scores - log_norm)
    probs_low = probs.astype(LOW)
    mixed = (
        jnp.einsum("hqk,khd->qhd", probs_low, values, preferred_element_type=F32)
        .astype(LOW)
        .reshape(seq_rows, head_cols)
    )

    def cross(value):
        part = value.reshape(4, own_rows, -1)
        return jnp.concatenate([part[1], part[0], part[3], part[2]])

    mixed_pair = jnp.concatenate([mixed, cross(swap(mixed, "tensor"))], axis=1)
    other_pair = swap(mixed_pair, "seq")
    half = 2 * own_rows
    other_pair = jnp.concatenate([other_pair[half:], other_pair[:half]])
    mixed_full = jnp.concatenate([mixed_pair, other_pair], axis=1)
    middle = inputs + dot(mixed_full, wo_full, 1, 1) + bout_all
    scaled_two, inverse_two = norm_parts(middle)
    normed_two = (scaled_two * gain_two + shift_two).astype(LOW)
    hidden = dot(normed_two, wf, 1, 0) + bfc_all
    active, gelu_pull = jax.vjp(gelu_tanh, hidden)
    active_low = active.astype(LOW)
    grad_hidden = gelu_pull(dot(cot, wp, 1, 0))[0].astype(LOW)

    def sum_half(partial):
        return partial[:half] + swap(partial[half:].astype(LOW), "seq").astype(F32)

    part_two = sum_half(dot(grad_hidden, wf, 1, 1))
    far = swap(part_two.astype(LOW), "tensor").astype(F32)
    grad_normed_two = part_two + jnp.concatenate([far[own_rows:], far[:own_rows]])
    cot_half = cot[:half].astype(F32)
    grad_middle = cot_half + norm_back(
        grad_normed_two, scaled_two[:half], inverse_two[:half], gain_two
    )
    grad_mid_half = grad_middle.astype(LOW)
    seq_grad_mid = jnp.concatenate([grad_mid_half, swap(grad_mid_half, "seq")])

    out_half = sum_half(dot(active_low, wp, 1, 1))
    out_own = out_half[:own_rows] + swap(out_half[own_rows:].astype(LOW), "tensor").astype(F32)
    result = turn((middle[:own_rows] + out_own + bproj_all).astype(LOW), width - offset, 1)

    grad_ff = jnp.concatenate([dot(normed_two, grad_hidden, 0, 0), dot(cot, active_low, 0, 0)], axis=1)
    sum_ff = scatter_chunks(grad_ff.reshape(size, chunk_rows, -1))

    grad_wo = dot(seq_grad_mid, mixed, 0, 0)
    grad_attn = dot(seq_grad_mid, wo_own, 1, 0).astype(LOW).reshape(seq_rows, heads, HEAD_DIM)
    grad_probs = jnp.einsum("qhd,khd->hqk", grad_attn, values, preferred_element_type=F32)
    inner = jnp.sum(probs * grad_probs, axis=-1, keepdims=True)
    grad_scores = (probs * (grad_probs - inner)).astype(LOW)
    query_grad = jnp.einsum("hqk,khd->qhd", grad_scores, keys, preferred_element_type=F32) * 0.125
    key_grad = jnp.einsum("hqk,qhd->khd", grad_scores, queries, preferred_element_type=F32) * 0.125
    value_grad = jnp.einsum("hqk,qhd->khd", probs_low, grad_attn, preferred_element_type=F32)
    grad_qkv = jnp.concatenate(
        [item.reshape(seq_rows, head_cols).astype(LOW) for item in (query_grad, key_grad, value_grad)],
        axis=1,
    )
    grad_wqkv = dot(normed, grad_qkv, 0, 0)
    part_normed = dot(grad_qkv, qkv_all, 1, 1)
    half_normed = sum_half(part_normed)
    grad_normed = half_normed[:own_rows] + swap(half_normed[own_rows:].astype(LOW), "tensor").astype(F32)
    own_scaled = scaled_one[:own_rows]
    grad_inputs = grad_middle[:own_rows] + norm_back(
        grad_normed, own_scaled, inverse_one[:own_rows], gain_one
    )
    grad_inputs = turn(grad_inputs, width - offset, 1)

    own_two = grad_normed_two[:own_rows]
    sums = jnp.stack(
        [
            jnp.sum(grad_middle[:own_rows], axis=0),
            jnp.sum(cot_half[:own_rows], axis=0),
            jnp.sum(part_normed * scaled_one, axis=0),
            jnp.sum(part_normed, axis=0),
            jnp.sum(own_two * scaled_two[:own_rows], axis=0),
            jnp.sum(own_two, axis=0),
        ]
    )
    sums = sums + swap(sums, "tensor")
    sums = sums + swap(sums, "seq")
    d_sums = sums.reshape(6, size, chunk_rows).transpose(1, 0, 2).reshape(size, -1)
    grad_qv = jnp.sum(grad_qkv.astype(F32), axis=0)
    qv_sums = (
        jnp.stack([grad_qv[:head_cols], grad_qv[2 * head_cols :]])
        .reshape(2, size, qv_count)
        .transpose(1, 0, 2)
        .reshape(size, -1)
    )
    fc_sums = jnp.sum(grad_hidden.astype(F32), axis=0).reshape(size, -1)
    rest_sums = jnp.roll(jnp.concatenate([qv_sums, fc_sums], axis=1), -(offset // chunk_rows), axis=0)
    vec_sums = jnp.concatenate([d_sums, rest_sums], axis=1)
    last_cols = qkv_cols + head_cols
    vec_count = vec_sums.shape[1]
    vec_rows = -(-vec_count // last_cols)
    vec_sums = jnp.pad(vec_sums, ((0, 0), (0, vec_rows * last_cols - vec_count)))
    last = jnp.concatenate([grad_wqkv, grad_wo], axis=1).reshape(size, chunk_rows, last_cols)
    last = jnp.concatenate([last, vec_sums.reshape(size, vec_rows, last_cols)], axis=1)
    sum_last = scatter_chunks(last)

    own_vec = sum_last[chunk_rows:].reshape(-1)
    d_own = own_vec[: 6 * chunk_rows].reshape(6, chunk_rows)
    qv_own = own_vec[6 * chunk_rows : 6 * chunk_rows + 2 * qv_count].reshape(2, qv_count)
    fc_own = own_vec[6 * chunk_rows + 2 * qv_count : vec_count]
    wqkv_own = jnp.stack(
        [sum_last[:chunk_rows, i * head_cols : (i + 1) * head_cols] for i in range(3)]
    )
    return (
        result,
        grad_inputs,
        wqkv_own,
        sum_last[:chunk_rows, qkv_cols:].T,
        sum_ff[:, :hidden_cols],
        sum_ff[:, hidden_cols:].T,
        qv_own,
        d_own[0],
        fc_own,
        d_own[1],
        d_own[2],
        d_own[3],
        d_own[4],
        d_own[5],
    )


def solution(mesh):
    in_specs = (
        P(("fsdp", "seq", "tensor"), None),
        P("fsdp"),
        P("fsdp", None),
        P(None, "fsdp", ("seq", "tensor")),
        P(None, ("seq", "tensor", "fsdp")),
        P(("seq", "tensor"), "fsdp"),
        P("fsdp"),
        P("fsdp", ("seq", "tensor")),
        P(("seq", "tensor", "fsdp")),
        P(("seq", "tensor"), "fsdp"),
        P("fsdp"),
        P("fsdp"),
        P("fsdp"),
        P("fsdp"),
        P("fsdp"),
    )
    out_specs = (
        P(("fsdp", "seq", "tensor"), None),
        P(("fsdp", "seq", "tensor"), None),
        P(None, "fsdp", ("seq", "tensor")),
        P(("seq", "tensor"), "fsdp"),
        P("fsdp", ("seq", "tensor")),
        P(("seq", "tensor"), "fsdp"),
        P(None, ("seq", "tensor", "fsdp")),
        P("fsdp"),
        P(("seq", "tensor", "fsdp")),
        P("fsdp"),
        P("fsdp"),
        P("fsdp"),
        P("fsdp"),
        P("fsdp"),
    )
    return jax.shard_map(local, mesh=mesh, in_specs=in_specs, out_specs=out_specs, check_vma=False)
```

time: 645 us -> 327 us (0.51)
  blocking collectives: 218 us -> 0 us
  waiting for transfers between devices: 321 us -> 157 us
  starting transfers between devices: 0.61 us -> 63.8 us
  local copies, waits for them, and re-layouts: 28.6 us -> 56 us
  between operations: 18 us -> 1.86 us
  matrix products: 35.5 us -> 22.6 us
    reduce_scatter x6 -> x0, waiting for transfers between devices: 225 us -> none  [the longest x1 72 us: local(): lax.psum_scatter(grad_wfc, 'fsdp', scatter_dimension=0, tiled=True)]
    ppermute x0 -> x43, waiting for transfers between devices: none -> 157 us  [the longest x28 141 us: shifted(): lax.ppermute(value, 'fsdp', [(i, (i + step) % size) for i in range(size)])]
    all_gather x6 -> x0, blocking collectives: 134 us -> none  [the longest x1 36 us: local(): lax.all_gather(w_qkv, 'fsdp', axis=1, tiled=True)]
    unnamed x2 -> x0, blocking collectives: 77.1 us -> none
    ppermute x0 -> x43, starting transfers between devices: none -> 63.8 us  [the longest x28 55.7 us: shifted(): lax.ppermute(value, 'fsdp', [(i, (i + step) % size) for i in range(size)])]
    unnamed x12 -> x0, waiting for transfers between devices: 56.7 us -> none
    all_gather x2 -> x0, waiting for transfers between devices: 40.1 us -> none  [the longest x1 38.9 us: local(): lax.all_gather(w_fc, 'fsdp', axis=0, tiled=True)]
    slice x2 -> x23, local copies, waits for them, and re-layouts: 0.05 us -> 11 us  [the longest x1 2.29 us: scatter_chunks(): total = total + shifted(low[step], step).astype(F32)]
  transfers between devices with their start and end apart: 10 -> 43, of which waited for: 10 -> 20; matrix products, arithmetic and copies ran while one was open for 7% -> 25% of each run, Pallas kernels for 0% -> 0%
where the time goes in v1:
time: 327 us; the launch traced here: 326 us
  waiting for transfers between devices  157 us (48%)
  starting transfers between devices  63.8 us (20%)
  local copies, waits for them, and re-layouts  56 us (17%)
  other arithmetic  24.3 us (7%)
  matrix products  22.6 us (7%)
    ppermute x28, waiting for transfers between devices, shifted(): lax.ppermute(value, 'fsdp', [(i, (i + step) % size) for i in range(size)])  141 us
    ppermute x28, starting transfers between devices, shifted(): lax.ppermute(value, 'fsdp', [(i, (i + step) % size) for i in range(size)])  55.7 us
    unnamed x137, local copies, waits for them, and re-layouts  19.1 us
    dot_general x12, matrix products, dot(): lax.dot_general(left, right, (((left_dim,), (right_dim,)), ((), ())), pre...  17.8 us
    ppermute x15, waiting for transfers between devices, swap(): return lax.ppermute(value, axis, [(0, 1), (1, 0)])  16.5 us
    ppermute x15, starting transfers between devices, swap(): return lax.ppermute(value, axis, [(0, 1), (1, 0)])  8.17 us
  transfers between devices with their start and end apart: 43, of which 20 were waited for; matrix products, arithmetic and copies ran while one was open for 25% of the time, Pallas kernels for 0%

profile of v1, /device:TPU:0, one launch (start us, length us, event | category | flops | bytes accessed | tf_op | source)
XLA Modules:
  0.0 325.9 jit_solution(16837624599436861152)
XLA Ops:
  3.6 6.0 %collective-permute-start.11 = (bf16[96,1728]{1,0:T(8,128)(2,1)}, bf16[96,1728]{1,0:T(8,128)(2,1)}, u32[]{:S(2)}, u32[]{:S(2)}) collective-permute-start(bf16[96,1728]{1,0:T(8,128)(2,1)} %concatenate.108), channel_id=1, source_target_pairs={{0,28},{4,0},{8,4},{12,8},{16,12},{20,16},{24,20},{28,24},{1,29},{... | collective-permute-start | bytes 995336 | tf_op jit(solution)/shard_map/ppermute | solution.py:38
  10.0 3.0 collective-permute-start.14
  13.7 4.8 %concatenate.98 = bf16[720]{0:T(1024)(128)(2,1)S(1)} concatenate(bf16[96]{0:T(256)(128)(2,1)} %param.23, bf16[96]{0:T(256)(128)(2,1)} %param.27, bf16[96]{0:T(256)(128)(2,1)} %param.28, bf16[96]{0:T(256)(128)(2,1)} %param.29, bf16[96]{0:T(256)(128)(2,1)} %param.30, bf16[96]{0:T(256)(128)(2,1)} %param.31, bf16[48]{0:T(256)(128)(2,1)S(1)} %reshape.309, bf16[96]{0:T(256)(128)(2,1)} %param.25), dimensions={0} | concatenate | bytes 2880 | tf_op jit(solution)/shard_map/concatenate | solution.py:97
  24.3 18.2 %collective-permute-done.2 = bf16[98,576]{1,0:T(8,128)(2,1)S(1)} collective-permute-done((bf16[98,576]{1,0:T(8,128)(2,1)S(1)}, bf16[98,576]{1,0:T(8,128)(2,1)S(1)}, u32[]{:S(2)}, u32[]{:S(2)}) %collective-permute-start.2) | collective-permute-done | bytes 112928 | tf_op jit(solution)/shard_map/ppermute | solution.py:38
  42.6 14.1 %collective-permute-done.3 = bf16[98,576]{1,0:T(8,128)(2,1)S(1)} collective-permute-done((bf16[98,576]{1,0:T(8,128)(2,1)S(1)}, bf16[98,576]{1,0:T(8,128)(2,1)S(1)}, u32[]{:S(2)}, u32[]{:S(2)}) %collective-permute-start.3) | collective-permute-done | bytes 112928 | tf_op jit(solution)/shard_map/ppermute | solution.py:38
  56.7 7.2 %collective-permute-start.4 = (bf16[98,576]{1,0:T(8,128)(2,1)S(1)}, bf16[98,576]{1,0:T(8,128)(2,1)S(1)}, u32[]{:S(2)}, u32[]{:S(2)}) collective-permute-start(bf16[98,576]{1,0:T(8,128)(2,1)S(1)} %get-tuple-element.63), channel_id=1, source_target_pairs={{0,20},{4,24},{8,28},{12,0},{16,4},{20,8},{24,12},{28,16},{1,21},{... | collective-permute-start | bytes 338696 | tf_op jit(solution)/shard_map/ppermute | solution.py:38
  63.9 4.0 %collective-permute-done.4 = bf16[98,576]{1,0:T(8,128)(2,1)S(1)} collective-permute-done((bf16[98,576]{1,0:T(8,128)(2,1)S(1)}, bf16[98,576]{1,0:T(8,128)(2,1)S(1)}, u32[]{:S(2)}, u32[]{:S(2)}) %collective-permute-start.4) | collective-permute-done | bytes 112928 | tf_op jit(solution)/shard_map/ppermute | solution.py:38
  67.9 3.1 collective-permute-start.5
  71.0 3.9 %collective-permute-done.5 = bf16[98,576]{1,0:T(8,128)(2,1)S(1)} collective-permute-done((bf16[98,576]{1,0:T(8,128)(2,1)S(1)}, bf16[98,576]{1,0:T(8,128)(2,1)S(1)}, u32[]{:S(2)}, u32[]{:S(2)}) %collective-permute-start.5) | collective-permute-done | bytes 112928 | tf_op jit(solution)/shard_map/ppermute | solution.py:38
  74.9 4.0 %collective-permute-start.6 = (bf16[98,576]{1,0:T(8,128)(2,1)S(1)}, bf16[98,576]{1,0:T(8,128)(2,1)S(1)}, u32[]{:S(2)}, u32[]{:S(2)}) collective-permute-start(bf16[98,576]{1,0:T(8,128)(2,1)S(1)} %get-tuple-element.63), channel_id=1, source_target_pairs={{0,12},{4,16},{8,20},{12,24},{16,28},{20,0},{24,4},{28,8},{1,13},{... | collective-permute-start | bytes 338696 | tf_op jit(solution)/shard_map/ppermute | solution.py:38
  78.9 4.0 %collective-permute-done.6 = bf16[98,576]{1,0:T(8,128)(2,1)S(1)} collective-permute-done((bf16[98,576]{1,0:T(8,128)(2,1)S(1)}, bf16[98,576]{1,0:T(8,128)(2,1)S(1)}, u32[]{:S(2)}, u32[]{:S(2)}) %collective-permute-start.6) | collective-permute-done | bytes 112928 | tf_op jit(solution)/shard_map/ppermute | solution.py:38
  82.9 3.5 %collective-permute-start.7 = (bf16[98,576]{1,0:T(8,128)(2,1)S(1)}, bf16[98,576]{1,0:T(8,128)(2,1)S(1)}, u32[]{:S(2)}, u32[]{:S(2)}) collective-permute-start(bf16[98,576]{1,0:T(8,128)(2,1)S(1)} %get-tuple-element.63), channel_id=1, source_target_pairs={{0,8},{4,12},{8,16},{12,20},{16,24},{20,28},{24,0},{28,4},{1,9},{5... | collective-permute-start | bytes 338696 | tf_op jit(solution)/shard_map/ppermute | solution.py:38
  86.4 3.9 %collective-permute-done.7 = bf16[98,576]{1,0:T(8,128)(2,1)S(1)} collective-permute-done((bf16[98,576]{1,0:T(8,128)(2,1)S(1)}, bf16[98,576]{1,0:T(8,128)(2,1)S(1)}, u32[]{:S(2)}, u32[]{:S(2)}) %collective-permute-start.7) | collective-permute-done | bytes 112928 | tf_op jit(solution)/shard_map/ppermute | solution.py:38
  90.3 5.1 %collective-permute-start.8 = (bf16[98,576]{1,0:T(8,128)(2,1)S(1)}, bf16[98,576]{1,0:T(8,128)(2,1)S(1)}, u32[]{:S(2)}, u32[]{:S(2)}) collective-permute-start(bf16[98,576]{1,0:T(8,128)(2,1)S(1)} %get-tuple-element.63), channel_id=1, source_target_pairs={{0,4},{4,8},{8,12},{12,16},{16,20},{20,24},{24,28},{28,0},{1,5},{5... | collective-permute-start | bytes 338696 | tf_op jit(solution)/shard_map/ppermute | solution.py:38
  95.5 2.5 collective-permute-done.8
  101.1 2.6 collective-permute-done
  103.8 4.0 %collective-permute-start.16 = (bf16[96,1728]{1,0:T(8,128)(2,1)}, bf16[96,1728]{1,0:T(8,128)(2,1)S(1)}, u32[]{:S(2)}, u32[]{:S(2)}) collective-permute-start(bf16[96,1728]{1,0:T(8,128)(2,1)} %concatenate.108), channel_id=1, source_target_pairs={{0,8},{4,12},{8,16},{12,20},{16,24},{20,28},{24,0},{28,4},{1,9},{5... | collective-permute-start | bytes 995336 | tf_op jit(solution)/shard_map/ppermute | solution.py:38
  112.8 16.0 %collective-permute-done.15 = bf16[96,1728]{1,0:T(8,128)(2,1)S(1)} collective-permute-done((bf16[96,1728]{1,0:T(8,128)(2,1)}, bf16[96,1728]{1,0:T(8,128)(2,1)S(1)}, u32[]{:S(2)}, u32[]{:S(2)}) %collective-permute-start.15) | collective-permute-done | bytes 331808 | tf_op jit(solution)/shard_map/ppermute | solution.py:38
  138.5 3.6 %collective-permute-done.9 = bf16[512,192]{0,1:T(8,128)(2,1)S(1)} collective-permute-done((bf16[512,192]{0,1:T(8,128)(2,1)S(1)}, bf16[512,192]{0,1:T(8,128)(2,1)S(1)}, u32[]{:S(2)}, u32[]{:S(2)}) %collective-permute-start.9) | collective-permute-done | bytes 196640 | tf_op jit(solution)/shard_map/ppermute | solution.py:42
  143.0 6.6 %collective-permute-done.18 = bf16[768,192]{1,0:T(8,128)(2,1)S(1)} collective-permute-done((bf16[768,192]{1,0:T(8,128)(2,1)S(1)}, bf16[768,192]{1,0:T(8,128)(2,1)S(1)}, u32[]{:S(2)}, u32[]{:S(2)}) %collective-permute-start.18) | collective-permute-done | bytes 294944 | tf_op jit(solution)/shard_map/ppermute | solution.py:42
  150.8 4.0 %fusion.35 = bf16[512,768]{1,0:T(8,128)(2,1)} fusion(s32[]{:T(128)S(6)} %select_n.92, bf16[128,768]{1,0:T(8,128)(2,1)S(1)} %get-tuple-element.85, bf16[128,768]{1,0:T(8,128)(2,1)S(1)} %get-tuple-element.84, bf16[128,768]{1,0:T(8,128)(2,1)S(1)} %get-tuple-element.86, bf16[128,768]{1,0:T(8,128)(2,1)S(1)} %get-tuple-element.83), kind=kLoop, calls=%fused_computation.74 | loop fusion | flops 6291456 | bytes 1572868 | tf_op jit(solution)/shard_map/jit(_roll_dynamic)/concatenate | solution.py:64
  162.5 2.8 fusion.107
  180.0 3.3 collective-permute-start.39
  183.3 6.6 %collective-permute-done.42 = bf16[96,1536]{0,1:T(8,128)(2,1)} collective-permute-done((bf16[96,1536]{0,1:T(8,128)(2,1)}, bf16[96,1536]{0,1:T(8,128)(2,1)}, u32[]{:S(2)}, u32[]{:S(2)}) %collective-permute-start.42) | collective-permute-done | bytes 294944 | tf_op jit(solution)/shard_map/ppermute | solution.py:38
  189.9 10.1 %collective-permute-done.41 = bf16[96,1536]{0,1:T(8,128)(2,1)} collective-permute-done((bf16[96,1536]{0,1:T(8,128)(2,1)}, bf16[96,1536]{0,1:T(8,128)(2,1)}, u32[]{:S(2)}, u32[]{:S(2)}) %collective-permute-start.41) | collective-permute-done | bytes 294944 | tf_op jit(solution)/shard_map/ppermute | solution.py:38
  200.0 3.1 fusion.25
  207.7 30.3 %collective-permute-done.39 = bf16[96,1536]{0,1:T(8,128)(2,1)} collective-permute-done((bf16[96,1536]{0,1:T(8,128)(2,1)}, bf16[96,1536]{0,1:T(8,128)(2,1)}, u32[]{:S(2)}, u32[]{:S(2)}) %collective-permute-start.39) | collective-permute-done | bytes 294944 | tf_op jit(solution)/shard_map/ppermute | solution.py:38
  238.5 8.2 %collective-permute-done.38 = bf16[96,1536]{0,1:T(8,128)(2,1)} collective-permute-done((bf16[96,1536]{0,1:T(8,128)(2,1)}, bf16[96,1536]{0,1:T(8,128)(2,1)}, u32[]{:S(2)}, u32[]{:S(2)}) %collective-permute-start.38) | collective-permute-done | bytes 294944 | tf_op jit(solution)/shard_map/ppermute | solution.py:38
  269.5 2.7 fusion.97
  283.1 2.5 collective-permute-done.27
  290.5 5.0 %collective-permute-start.33 = (bf16[97,768]{1,0:T(8,128)(2,1)S(1)}, bf16[97,768]{1,0:T(8,128)(2,1)S(1)}, u32[]{:S(2)}, u32[]{:S(2)}) collective-permute-start(bf16[97,768]{1,0:T(8,128)(2,1)S(1)} %get-tuple-element.74), channel_id=1, source_target_pairs={{0,20},{4,24},{8,28},{12,0},{16,4},{20,8},{24,12},{28,16},{1,21},{... | collective-permute-start | bytes 446984 | tf_op jit(solution)/shard_map/ppermute | solution.py:38
  303.8 17.8 %collective-permute-done.32 = bf16[97,768]{1,0:T(8,128)(2,1)S(1)} collective-permute-done((bf16[97,768]{1,0:T(8,128)(2,1)S(1)}, bf16[97,768]{1,0:T(8,128)(2,1)S(1)}, u32[]{:S(2)}, u32[]{:S(2)}) %collective-permute-start.32) | collective-permute-done | bytes 149024 | tf_op jit(solution)/shard_map/ppermute | solution.py:38
  (331 shorter events, 107.7 us)
Async XLA Ops:
  3.6 100.2 %collective-permute-start.11 = (bf16[96,1728]{1,0:T(8,128)(2,1)}, bf16[96,1728]{1,0:T(8,128)(2,1)}, u32[]{:S(2)}, u32[]{:S(2)}) collective-permute-start(bf16[96,1728]{1,0:T(8,128)(2,1)} %concatenate.108), channel_id=1, source_target_pairs={{0,28},{4,0},{8,4},{12,8},{16,12},{20,16},{24,20},{28,24},{1,29},{... | collective-permute-start | bytes 995336 | tf_op jit(solution)/shard_map/ppermute | solution.py:38
  9.5 100.0 %collective-permute-start.12 = (bf16[96,1728]{1,0:T(8,128)(2,1)}, bf16[96,1728]{1,0:T(8,128)(2,1)}, u32[]{:S(2)}, u32[]{:S(2)}) collective-permute-start(bf16[96,1728]{1,0:T(8,128)(2,1)} %concatenate.108), channel_id=1, source_target_pairs={{0,24},{4,28},{8,0},{12,4},{16,8},{20,12},{24,16},{28,20},{1,25},{... | collective-permute-start | bytes 995336 | tf_op jit(solution)/shard_map/ppermute | solution.py:38
  10.0 101.3 %collective-permute-start.13 = (bf16[96,1728]{1,0:T(8,128)(2,1)}, bf16[96,1728]{1,0:T(8,128)(2,1)S(1)}, u32[]{:S(2)}, u32[]{:S(2)}) collective-permute-start(bf16[96,1728]{1,0:T(8,128)(2,1)} %concatenate.108), channel_id=1, source_target_pairs={{0,20},{4,24},{8,28},{12,0},{16,4},{20,8},{24,12},{28,16},{1,21},{... | collective-permute-start | bytes 995336 | tf_op jit(solution)/shard_map/ppermute | solution.py:38
  10.0 102.0 %collective-permute-start.14 = (bf16[96,1728]{1,0:T(8,128)(2,1)}, bf16[96,1728]{1,0:T(8,128)(2,1)S(1)}, u32[]{:S(2)}, u32[]{:S(2)}) collective-permute-start(bf16[96,1728]{1,0:T(8,128)(2,1)} %concatenate.108), channel_id=1, source_target_pairs={{0,16},{4,20},{8,24},{12,28},{16,0},{20,4},{24,8},{28,12},{1,17},{... | collective-permute-start | bytes 995336 | tf_op jit(solution)/shard_map/ppermute | solution.py:38
  19.6 22.9 %collective-permute-start.2 = (bf16[98,576]{1,0:T(8,128)(2,1)S(1)}, bf16[98,576]{1,0:T(8,128)(2,1)S(1)}, u32[]{:S(2)}, u32[]{:S(2)}) collective-permute-start(bf16[98,576]{1,0:T(8,128)(2,1)S(1)} %get-tuple-element.63), channel_id=1, source_target_pairs={{0,28},{4,0},{8,4},{12,8},{16,12},{20,16},{24,20},{28,24},{1,29},{... | collective-permute-start | bytes 338696 | tf_op jit(solution)/shard_map/ppermute | solution.py:38
  42.5 14.2 %collective-permute-start.3 = (bf16[98,576]{1,0:T(8,128)(2,1)S(1)}, bf16[98,576]{1,0:T(8,128)(2,1)S(1)}, u32[]{:S(2)}, u32[]{:S(2)}) collective-permute-start(bf16[98,576]{1,0:T(8,128)(2,1)S(1)} %get-tuple-element.63), channel_id=1, source_target_pairs={{0,24},{4,28},{8,0},{12,4},{16,8},{20,12},{24,16},{28,20},{1,25},{... | collective-permute-start | bytes 338696 | tf_op jit(solution)/shard_map/ppermute | solution.py:38
  56.7 11.2 %collective-permute-start.4 = (bf16[98,576]{1,0:T(8,128)(2,1)S(1)}, bf16[98,576]{1,0:T(8,128)(2,1)S(1)}, u32[]{:S(2)}, u32[]{:S(2)}) collective-permute-start(bf16[98,576]{1,0:T(8,128)(2,1)S(1)} %get-tuple-element.63), channel_id=1, source_target_pairs={{0,20},{4,24},{8,28},{12,0},{16,4},{20,8},{24,12},{28,16},{1,21},{... | collective-permute-start | bytes 338696 | tf_op jit(solution)/shard_map/ppermute | solution.py:38
  103.7 25.1 %collective-permute-start.15 = (bf16[96,1728]{1,0:T(8,128)(2,1)}, bf16[96,1728]{1,0:T(8,128)(2,1)S(1)}, u32[]{:S(2)}, u32[]{:S(2)}) collective-permute-start(bf16[96,1728]{1,0:T(8,128)(2,1)} %concatenate.108), channel_id=1, source_target_pairs={{0,12},{4,16},{8,20},{12,24},{16,28},{20,0},{24,4},{28,8},{1,13},{... | collective-permute-start | bytes 995336 | tf_op jit(solution)/shard_map/ppermute | solution.py:38
  103.8 25.8 %collective-permute-start.16 = (bf16[96,1728]{1,0:T(8,128)(2,1)}, bf16[96,1728]{1,0:T(8,128)(2,1)S(1)}, u32[]{:S(2)}, u32[]{:S(2)}) collective-permute-start(bf16[96,1728]{1,0:T(8,128)(2,1)} %concatenate.108), channel_id=1, source_target_pairs={{0,8},{4,12},{8,16},{12,20},{16,24},{20,28},{24,0},{28,4},{1,9},{5... | collective-permute-start | bytes 995336 | tf_op jit(solution)/shard_map/ppermute | solution.py:38
  109.5 26.6 %collective-permute-start.17 = (bf16[96,1728]{1,0:T(8,128)(2,1)}, bf16[96,1728]{1,0:T(8,128)(2,1)S(1)}, u32[]{:S(2)}, u32[]{:S(2)}) collective-permute-start(bf16[96,1728]{1,0:T(8,128)(2,1)} %concatenate.108), channel_id=1, source_target_pairs={{0,4},{4,8},{8,12},{12,16},{16,20},{20,24},{24,28},{28,0},{1,5},{5... | collective-permute-start | bytes 995336 | tf_op jit(solution)/shard_map/ppermute | solution.py:38
  111.3 19.1 %collective-permute-start.1 = (bf16[256,768]{1,0:T(8,128)(2,1)S(1)}, bf16[256,768]{1,0:T(8,128)(2,1)S(1)}, u32[]{:S(2)}, u32[]{:S(2)}) collective-permute-start(bf16[256,768]{1,0:T(8,128)(2,1)S(1)} %pad_maximum_fusion.9), channel_id=1, source_target_pairs={{0,2},{2,0},{1,3},{3,1},{4,6},{6,4},{5,7},{7,5},{8,10},{10,8},{9,1... | collective-permute-start | bytes 1179656 | tf_op jit(solution)/shard_map/ppermute | solution.py:42
  138.0 11.6 %collective-permute-start.18 = (bf16[768,192]{1,0:T(8,128)(2,1)S(1)}, bf16[768,192]{1,0:T(8,128)(2,1)S(1)}, u32[]{:S(2)}, u32[]{:S(2)}) collective-permute-start(bf16[768,192]{1,0:T(8,128)(2,1)S(1)} %slice.413), channel_id=1, source_target_pairs={{0,1},{1,0},{2,3},{3,2},{4,5},{5,4},{6,7},{7,6},{8,9},{9,8},{10,11... | collective-permute-start | bytes 884744 | tf_op jit(solution)/shard_map/ppermute | solution.py:42
  143.0 18.4 %collective-permute-start.10 = (bf16[512,384]{0,1:T(8,128)(2,1)}, bf16[512,384]{0,1:T(8,128)(2,1)}, u32[]{:S(2)}, u32[]{:S(2)}) collective-permute-start(bf16[512,384]{0,1:T(8,128)(2,1)} %maximum_maximum_fusion), channel_id=1, source_target_pairs={{0,2},{2,0},{1,3},{3,1},{4,6},{6,4},{5,7},{7,5},{8,10},{10,8},{9,1... | collective-permute-start | bytes 1179656 | tf_op jit(solution)/shard_map/ppermute | solution.py:42
  150.6 11.8 %collective-permute-start.19 = (bf16[768,384]{1,0:T(8,128)(2,1)}, bf16[768,384]{1,0:T(8,128)(2,1)}, u32[]{:S(2)}, u32[]{:S(2)}) collective-permute-start(bf16[768,384]{1,0:T(8,128)(2,1)} %pad_maximum_fusion.5), channel_id=1, source_target_pairs={{0,2},{2,0},{1,3},{3,1},{4,6},{6,4},{5,7},{7,5},{8,10},{10,8},{9,1... | collective-permute-start | bytes 1769480 | tf_op jit(solution)/shard_map/ppermute | solution.py:42
  175.1 24.9 %collective-permute-start.22 = (bf16[256,768]{1,0:T(8,128)(2,1)}, bf16[256,768]{1,0:T(8,128)(2,1)}, u32[]{:S(2)}, u32[]{:S(2)}) collective-permute-start(bf16[256,768]{1,0:T(8,128)(2,1)} %slice.604), channel_id=1, source_target_pairs={{0,2},{2,0},{1,3},{3,1},{4,6},{6,4},{5,7},{7,5},{8,10},{10,8},{9,1... | collective-permute-start | bytes 1179656 | tf_op jit(solution)/shard_map/ppermute | solution.py:42
  178.1 11.8 %collective-permute-start.42 = (bf16[96,1536]{0,1:T(8,128)(2,1)}, bf16[96,1536]{0,1:T(8,128)(2,1)}, u32[]{:S(2)}, u32[]{:S(2)}) collective-permute-start(bf16[96,1536]{0,1:T(8,128)(2,1)} %get-tuple-element.65), channel_id=1, source_target_pairs={{0,28},{4,0},{8,4},{12,8},{16,12},{20,16},{24,20},{28,24},{1,29},{... | collective-permute-start | bytes 884744 | tf_op jit(solution)/shard_map/ppermute | solution.py:38
  178.1 21.8 %collective-permute-start.41 = (bf16[96,1536]{0,1:T(8,128)(2,1)}, bf16[96,1536]{0,1:T(8,128)(2,1)}, u32[]{:S(2)}, u32[]{:S(2)}) collective-permute-start(bf16[96,1536]{0,1:T(8,128)(2,1)} %get-tuple-element.66), channel_id=1, source_target_pairs={{0,24},{4,28},{8,0},{12,4},{16,8},{20,12},{24,16},{28,20},{1,25},{... | collective-permute-start | bytes 884744 | tf_op jit(solution)/shard_map/ppermute | solution.py:38
  180.0 27.7 %collective-permute-start.40 = (bf16[96,1536]{0,1:T(8,128)(2,1)}, bf16[96,1536]{0,1:T(8,128)(2,1)}, u32[]{:S(2)}, u32[]{:S(2)}) collective-permute-start(bf16[96,1536]{0,1:T(8,128)(2,1)} %get-tuple-element.67), channel_id=1, source_target_pairs={{0,20},{4,24},{8,28},{12,0},{16,4},{20,8},{24,12},{28,16},{1,21},{... | collective-permute-start | bytes 884744 | tf_op jit(solution)/shard_map/ppermute | solution.py:38
  180.0 58.0 %collective-permute-start.39 = (bf16[96,1536]{0,1:T(8,128)(2,1)}, bf16[96,1536]{0,1:T(8,128)(2,1)}, u32[]{:S(2)}, u32[]{:S(2)}) collective-permute-start(bf16[96,1536]{0,1:T(8,128)(2,1)} %get-tuple-element.68), channel_id=1, source_target_pairs={{0,16},{4,20},{8,24},{12,28},{16,0},{20,4},{24,8},{28,12},{1,17},{... | collective-permute-start | bytes 884744 | tf_op jit(solution)/shard_map/ppermute | solution.py:38
  189.9 56.9 %collective-permute-start.38 = (bf16[96,1536]{0,1:T(8,128)(2,1)}, bf16[96,1536]{0,1:T(8,128)(2,1)}, u32[]{:S(2)}, u32[]{:S(2)}) collective-permute-start(bf16[96,1536]{0,1:T(8,128)(2,1)} %get-tuple-element.69), channel_id=1, source_target_pairs={{0,12},{4,16},{8,20},{12,24},{16,28},{20,0},{24,4},{28,8},{1,13},{... | collective-permute-start | bytes 884744 | tf_op jit(solution)/shard_map/ppermute | solution.py:38
  199.9 46.8 %collective-permute-start.37 = (bf16[96,1536]{0,1:T(8,128)(2,1)}, bf16[96,1536]{0,1:T(8,128)(2,1)}, u32[]{:S(2)}, u32[]{:S(2)}) collective-permute-start(bf16[96,1536]{0,1:T(8,128)(2,1)} %get-tuple-element.70), channel_id=1, source_target_pairs={{0,8},{4,12},{8,16},{12,20},{16,24},{20,28},{24,0},{28,4},{1,9},{5... | collective-permute-start | bytes 884744 | tf_op jit(solution)/shard_map/ppermute | solution.py:38
  199.9 46.8 %collective-permute-start.36 = (bf16[96,1536]{0,1:T(8,128)(2,1)}, bf16[96,1536]{0,1:T(8,128)(2,1)}, u32[]{:S(2)}, u32[]{:S(2)}) collective-permute-start(bf16[96,1536]{0,1:T(8,128)(2,1)} %get-tuple-element.64), channel_id=1, source_target_pairs={{0,4},{4,8},{8,12},{12,16},{16,20},{20,24},{24,28},{28,0},{1,5},{5... | collective-permute-start | bytes 884744 | tf_op jit(solution)/shard_map/ppermute | solution.py:38
  207.7 50.5 %collective-permute-start.20 = (bf16[256,768]{1,0:T(8,128)(2,1)}, bf16[256,768]{1,0:T(8,128)(2,1)}, u32[]{:S(2)}, u32[]{:S(2)}) collective-permute-start(bf16[256,768]{1,0:T(8,128)(2,1)} %slice.605), channel_id=1, source_target_pairs={{0,2},{2,0},{1,3},{3,1},{4,6},{6,4},{5,7},{7,5},{8,10},{10,8},{9,1... | collective-permute-start | bytes 1179656 | tf_op jit(solution)/shard_map/ppermute | solution.py:42
  238.0 15.8 %collective-permute-start.23 = (bf16[256,768]{1,0:T(8,128)(2,1)}, bf16[256,768]{1,0:T(8,128)(2,1)}, u32[]{:S(2)}, u32[]{:S(2)}) collective-permute-start(bf16[256,768]{1,0:T(8,128)(2,1)} %fusion.61), channel_id=1, source_target_pairs={{0,1},{1,0},{2,3},{3,2},{4,5},{5,4},{6,7},{7,6},{8,9},{9,8},{10,11... | collective-permute-start | bytes 1179656 | tf_op jit(solution)/shard_map/ppermute | solution.py:42
  260.6 28.8 %collective-permute-start.21 = (bf16[128,768]{1,0:T(8,128)(2,1)}, bf16[128,768]{1,0:T(8,128)(2,1)}, u32[]{:S(2)}, u32[]{:S(2)}) collective-permute-start(bf16[128,768]{1,0:T(8,128)(2,1)} %slice.607), channel_id=1, source_target_pairs={{0,1},{1,0},{2,3},{3,2},{4,5},{5,4},{6,7},{7,6},{8,9},{9,8},{10,11... | collective-permute-start | bytes 589832 | tf_op jit(solution)/shard_map/ppermute | solution.py:42
  288.3 9.6 %collective-permute-start.35 = (bf16[97,768]{1,0:T(8,128)(2,1)S(1)}, bf16[97,768]{1,0:T(8,128)(2,1)S(1)}, u32[]{:S(2)}, u32[]{:S(2)}) collective-permute-start(bf16[97,768]{1,0:T(8,128)(2,1)S(1)} %get-tuple-element.72), channel_id=1, source_target_pairs={{0,28},{4,0},{8,4},{12,8},{16,12},{20,16},{24,20},{28,24},{1,29},{... | collective-permute-start | bytes 446984 | tf_op jit(solution)/shard_map/ppermute | solution.py:38
  288.4 11.6 %collective-permute-start.34 = (bf16[97,768]{1,0:T(8,128)(2,1)S(1)}, bf16[97,768]{1,0:T(8,128)(2,1)S(1)}, u32[]{:S(2)}, u32[]{:S(2)}) collective-permute-start(bf16[97,768]{1,0:T(8,128)(2,1)S(1)} %get-tuple-element.73), channel_id=1, source_target_pairs={{0,24},{4,28},{8,0},{12,4},{16,8},{20,12},{24,16},{28,20},{1,25},{... | collective-permute-start | bytes 446984 | tf_op jit(solution)/shard_map/ppermute | solution.py:38
  290.5 13.3 %collective-permute-start.33 = (bf16[97,768]{1,0:T(8,128)(2,1)S(1)}, bf16[97,768]{1,0:T(8,128)(2,1)S(1)}, u32[]{:S(2)}, u32[]{:S(2)}) collective-permute-start(bf16[97,768]{1,0:T(8,128)(2,1)S(1)} %get-tuple-element.74), channel_id=1, source_target_pairs={{0,20},{4,24},{8,28},{12,0},{16,4},{20,8},{24,12},{28,16},{1,21},{... | collective-permute-start | bytes 446984 | tf_op jit(solution)/shard_map/ppermute | solution.py:38
  295.5 26.1 %collective-permute-start.32 = (bf16[97,768]{1,0:T(8,128)(2,1)S(1)}, bf16[97,768]{1,0:T(8,128)(2,1)S(1)}, u32[]{:S(2)}, u32[]{:S(2)}) collective-permute-start(bf16[97,768]{1,0:T(8,128)(2,1)S(1)} %get-tuple-element.75), channel_id=1, source_target_pairs={{0,16},{4,20},{8,24},{12,28},{16,0},{20,4},{24,8},{28,12},{1,17},{... | collective-permute-start | bytes 446984 | tf_op jit(solution)/shard_map/ppermute | solution.py:38
  295.5 27.3 %collective-permute-start.31 = (bf16[97,768]{1,0:T(8,128)(2,1)S(1)}, bf16[97,768]{1,0:T(8,128)(2,1)S(1)}, u32[]{:S(2)}, u32[]{:S(2)}) collective-permute-start(bf16[97,768]{1,0:T(8,128)(2,1)S(1)} %get-tuple-element.76), channel_id=1, source_target_pairs={{0,12},{4,16},{8,20},{12,24},{16,28},{20,0},{24,4},{28,8},{1,13},{... | collective-permute-start | bytes 446984 | tf_op jit(solution)/shard_map/ppermute | solution.py:38
  297.9 24.8 %collective-permute-start.30 = (bf16[97,768]{1,0:T(8,128)(2,1)S(1)}, bf16[97,768]{1,0:T(8,128)(2,1)S(1)}, u32[]{:S(2)}, u32[]{:S(2)}) collective-permute-start(bf16[97,768]{1,0:T(8,128)(2,1)S(1)} %get-tuple-element.77), channel_id=1, source_target_pairs={{0,8},{4,12},{8,16},{12,20},{16,24},{20,28},{24,0},{28,4},{1,9},{5... | collective-permute-start | bytes 446984 | tf_op jit(solution)/shard_map/ppermute | solution.py:38
  300.0 22.8 %collective-permute-start.29 = (bf16[97,768]{1,0:T(8,128)(2,1)S(1)}, bf16[97,768]{1,0:T(8,128)(2,1)S(1)}, u32[]{:S(2)}, u32[]{:S(2)}) collective-permute-start(bf16[97,768]{1,0:T(8,128)(2,1)S(1)} %get-tuple-element.71), channel_id=1, source_target_pairs={{0,4},{4,8},{8,12},{12,16},{16,20},{20,24},{24,28},{28,0},{1,5},{5... | collective-permute-start | bytes 446984 | tf_op jit(solution)/shard_map/ppermute | solution.py:38
  (73 other events, 510.4 us)

commit v2 on v1

v2 whole, which is shorter than its diff:
```python
import functools

import jax
import jax.numpy as jnp
import numpy as np
from jax import lax
from jax.experimental import pallas as pl
from jax.experimental.pallas import tpu as pltpu
from jax.sharding import PartitionSpec as P

HEAD_DIM = 64
DIRECT_SIZE = 8
STEPS = ((0, 0), (1, 0), (3, 1), (3, 0), (1, 1), (0, 1), (2, 0), (2, 1))
VEC_COLS = 128
LOW = jnp.bfloat16
F32 = jnp.float32
GELU_SCALE = float(np.sqrt(2.0 / np.pi))


def shape(rows, cols, dtype):
    return jax.ShapeDtypeStruct((rows, cols), dtype)


def on_core(body, outs, scalars, arrays, scratch=(), flops=0, limit=48):
    specs = [pl.BlockSpec(memory_space=pltpu.SMEM)] * len(scalars)
    specs += [pl.BlockSpec(memory_space=pltpu.VMEM)] * len(arrays)
    moved = sum(int(np.prod(a.shape)) * a.dtype.itemsize for a in arrays) + sum(
        int(np.prod(o.shape)) * o.dtype.itemsize for o in outs
    )
    return pl.pallas_call(
        body,
        out_shape=tuple(outs),
        in_specs=specs,
        out_specs=tuple(pl.BlockSpec(memory_space=pltpu.VMEM) for _ in outs),
        scratch_shapes=list(scratch),
        compiler_params=pltpu.CompilerParams(vmem_limit_bytes=limit * 2**20),
        cost_estimate=pl.CostEstimate(flops=flops, bytes_accessed=moved, transcendentals=0),
    )(*scalars, *arrays)


def dot(left, right, left_dim, right_dim):
    return lax.dot_general(
        left, right, (((left_dim,), (right_dim,)), ((), ())), preferred_element_type=F32
    )


def norm_parts(values):
    center = values - jnp.mean(values, axis=-1, keepdims=True)
    spread = jnp.mean(center * center, axis=-1, keepdims=True)
    inverse = lax.rsqrt(spread + 1e-05)
    return center * inverse, inverse


def norm_back(cot, scaled, inverse, gain):
    inner = cot * gain
    first = jnp.mean(inner, axis=-1, keepdims=True)
    second = jnp.mean(inner * scaled, axis=-1, keepdims=True)
    return (inner - first - scaled * second) * inverse


def turned(value):
    count = value.shape[1]
    row = lax.broadcasted_iota(jnp.int32, (count, count), 0)
    col = lax.broadcasted_iota(jnp.int32, (count, count), 1)
    return dot((row == col).astype(F32).astype(LOW), value, 1, 1).astype(LOW)


def turned_wide(value):
    rows = value.shape[0]
    lack = -rows % 128
    if lack:
        value = jnp.concatenate([value, jnp.zeros((lack, value.shape[1]), value.dtype)], axis=0)
    return value.T[:, :rows]


def swap(value, axis):
    return lax.ppermute(value, axis, [(0, 1), (1, 0)])


def send(value, turn, flip):
    pairs = [(i, (i // 2 + turn) % 4 * 2 + (i % 2 ^ flip)) for i in range(DIRECT_SIZE)]
    return lax.ppermute(value, "fsdp", pairs)


def after(value, *earlier):
    return lax.optimization_barrier((value, *earlier))[0]


def pieces_of(chunk):
    ahead = send(chunk, 3, 0)
    behind = send(chunk, 1, 1)
    rest = [send(chunk, 1, 0), send(chunk, 3, 1), send(chunk, 0, 1)]
    return [chunk, ahead, behind, *rest, send(ahead, 3, 0), send(behind, 1, 0)]


def sums_of(pieces):
    own, ahead, behind, near_behind, near_ahead, other, far, far_other = pieces
    passed = send(far, 1, 0), send(far_other, 3, 0)
    rest = [send(near_behind, 3, 0), send(near_ahead, 1, 1), send(other, 0, 1)]
    ahead, behind = [
        (mine.astype(F32) + got.astype(F32)).astype(LOW) for mine, got in zip((ahead, behind), passed)
    ]
    return [own, *rest, send(ahead, 1, 0), send(behind, 3, 1)]


def row_start(me, step, rows):
    turn, flip = STEPS[step]
    pair = lax.rem(lax.div(me, 2) + turn, 4)
    return pl.multiple_of((pair * 2 + (lax.rem(me, 2) ^ flip)) * rows, rows)


def pack_first_body(wqkv, wout, vecs, out):
    rows = wqkv.shape[1]
    cols = turned_wide(vecs[...].astype(F32))[:rows].astype(LOW)
    lack = jnp.zeros((rows, VEC_COLS - cols.shape[1]), LOW)
    out[...] = jnp.concatenate(
        [cols, lack, wqkv[0], wqkv[1], wqkv[2], turned(wout[...])], axis=1
    )


def pack_second_body(wfc, wproj, out):
    out[...] = jnp.concatenate([wfc[...], turned(wproj[...])], axis=1)


def open_first_body(size, scal, *refs):
    pieces, (sel, wqkv, wo, rows, bias, cols) = refs[:size], refs[size:]
    chunk = pieces[0].shape[0]
    split = VEC_COLS + wqkv.shape[1]
    for step, piece in enumerate(pieces):
        place = pl.ds(row_start(scal[0], step, chunk) if size > 1 else 0, chunk)
        value = piece[...]
        cols[place, :] = value[:, :VEC_COLS].astype(F32)
        wqkv[place, :] = value[:, VEC_COLS:split]
        wo[place, :] = value[:, split:]
    wide = cols[...].T
    rows[...] = wide[:8]
    bias[...] = dot(wide[:8].astype(LOW), sel[...], 1, 0)


def open_second_body(size, scal, *refs):
    pieces, (grad, wf, wp, da, cot) = refs[:size], refs[size:]
    chunk = pieces[0].shape[0]
    cols = wf.shape[1]
    own = cot.shape[0] // 4
    for step, piece in enumerate(pieces):
        place = pl.ds(row_start(scal[0], step, chunk) if size > 1 else 0, chunk)
        wf[place, :] = piece[:, :cols]
        wp[place, :] = piece[:, cols:]
    for block in range(4):
        start = pl.multiple_of((scal[1] ^ block) * own, own)
        cot[block * own : (block + 1) * own, :] = grad[pl.ds(start, own), :]
    da[...] = dot(cot[...], wp[...], 1, 0)


def fill_mask(mask, doc_col, doc_row, pos_col, pos_row):
    total = mask.shape[0]
    for low in range(0, total, 128):
        part = slice(low, low + 128)
        seen = (doc_col[part, :] == doc_row[...]) & (pos_row[...] <= pos_col[part, :])
        mask[part, :] = jnp.where(seen, 0.0, -1e30)


def attend_body(
    own, near, pair, wqkv, bias, rows, doc_col, doc_row, pos_col, pos_row,
    qkv, mixed, lse, normed, mask,
):
    total = qkv.shape[0]
    part = own.shape[0]
    gain, shift = rows[2:3, :], rows[3:4, :]
    sources = (own[...], near[...], pair[:part, :], pair[part:, :])
    for number, source in enumerate(sources):
        scaled, _ = norm_parts(source.astype(F32))
        normed[number * part : (number + 1) * part, :] = (scaled * gain + shift).astype(LOW)
    qkv[...] = (dot(normed[...], wqkv[...], 1, 0) + bias[7:8, :]).astype(LOW)
    fill_mask(mask, doc_col, doc_row, pos_col, pos_row)
    width = qkv.shape[1] // 3
    heads = width // HEAD_DIM
    step = total // 2
    for low in range(0, total, step):
        here = slice(low, low + step)
        found, norms = [], []
        for head in range(heads):
            at = head * HEAD_DIM
            query = qkv[here, at : at + HEAD_DIM]
            key = qkv[:, width + at : width + at + HEAD_DIM]
            value = qkv[:, 2 * width + at : 2 * width + at + HEAD_DIM]
            scores = dot(query, key, 1, 1) * 0.125 + mask[here, :]
            top = jnp.max(scores, axis=-1, keepdims=True)
            raised = jnp.exp(scores - top)
            total_raised = jnp.sum(raised, axis=-1, keepdims=True)
            probs = (raised * (1.0 / total_raised)).astype(LOW)
            found.append(dot(probs, value, 1, 0))
            norms.append(top + jnp.log(total_raised))
        mixed[here, :] = jnp.concatenate(found, axis=1).astype(LOW)
        for head in range(heads):
            lse[here, head : head + 1] = norms[head]


def feed_body(
    own, near, pair, mixed_own, mixed_near, mixed_pair, wo_own, wo_near, wo_pair, wf, rows, da,
    keep, send, middle, normed, active, grad_hidden,
):
    part = own.shape[0]
    half = 2 * part
    head_cols = mixed_own.shape[1]
    for number in range(2):
        here = slice(number * half, (number + 1) * half)
        if number == 0:
            source = jnp.concatenate([own[...], near[...]], axis=0)
            swapped = slice(half, 2 * half)
        else:
            source = pair[...]
            swapped = slice(0, half)
        low = number * half
        across = jnp.concatenate(
            [mixed_near[low + part : low + half, :], mixed_near[low : low + part, :]], axis=0
        )
        total = source.astype(F32) + rows[0:1, :]
        total += dot(mixed_own[here, :], wo_own[...], 1, 1)
        total += dot(across, wo_near[...], 1, 1)
        total += dot(mixed_pair[swapped, :], wo_pair[...], 1, 1)
        if number == 0:
            middle[...] = total
        scaled, _ = norm_parts(total)
        low_norm = (scaled * rows[4:5, :] + rows[5:6, :]).astype(LOW)
        normed[here, :] = low_norm
        hidden = dot(low_norm, wf[...], 1, 0) + rows[6:7, :]
        square = hidden * hidden
        bent = jnp.tanh(GELU_SCALE * hidden * (1.0 + 0.044715 * square))
        rise = 0.5 * (1.0 + bent)
        active[here, :] = (hidden * rise).astype(LOW)
        slope = rise + 0.5 * hidden * (1.0 - bent * bent) * (
            GELU_SCALE * (1.0 + 3 * 0.044715 * square)
        )
        grad_low = (da[here, :] * slope).astype(LOW)
        grad_hidden[here, :] = grad_low
        back = dot(grad_low, wf[...], 1, 1)
        if number == 0:
            keep[...] = back
        else:
            send[...] = back.astype(LOW)


def put_pieces(me, whole, outs):
    size = len(outs)
    if size == 1:
        outs[0][...] = whole[...]
        return
    chunk = outs[0].shape[0]
    for step, out in enumerate(outs):
        value = whole[pl.ds(row_start(me, step, chunk), chunk), :]
        out[...] = value.astype(out.dtype)


def feed_grad_body(size, scal, active, wp, normed, grad_hidden, cot, *refs):
    keep, send, fc_sum = refs[:3]
    pieces, whole = refs[3 : 3 + size], refs[3 + size]
    half = keep.shape[0]
    cols = wp.shape[1]
    whole[:, :cols] = dot(normed[...], grad_hidden[...], 0, 0)
    whole[:, cols:] = dot(cot[...], active[...], 0, 0)
    put_pieces(scal[0], whole, pieces)
    keep[...] = dot(active[:half, :], wp[...], 1, 1)
    send[...] = dot(active[half:, :], wp[...], 1, 1).astype(LOW)
    fc_sum[...] = jnp.sum(grad_hidden[...].astype(F32), axis=0, keepdims=True)


def middle_body(part_two, far, middle, cot, rows, grad_low, grad_own, early):
    own = grad_own.shape[0]
    flipped = jnp.concatenate([far[own:, :], far[:own, :]], axis=0).astype(F32)
    grad = part_two[...] + flipped
    scaled, inverse = norm_parts(middle[...])
    cotangent = cot[: 2 * own, :].astype(F32)
    total = cotangent + norm_back(grad, scaled, inverse, rows[4:5, :])
    grad_low[...] = total.astype(LOW)
    grad_own[...] = total[:own]
    add = functools.partial(jnp.sum, axis=0, keepdims=True)
    empty = jnp.zeros((2, total.shape[1]), F32)
    early[...] = jnp.concatenate(
        [add(total[:own]), add(cotangent[:own]), empty, add(grad[:own] * scaled[:own]), add(grad[:own]), empty],
        axis=0,
    )


def attend_back_body(
    grad_half, grad_other, wo, wqkv, qkv, lse, own, near, pair, early, doc_col, doc_row, pos_col, pos_row,
    keep, send, grad_qkv, late, qkv_sum, mask,
):
    total = qkv.shape[0]
    half = total // 2
    part = own.shape[0]
    width = qkv.shape[1] // 3
    heads = width // HEAD_DIM
    fill_mask(mask, doc_col, doc_row, pos_col, pos_row)
    grad_attn = [dot(g[...], wo[...], 1, 0).astype(LOW) for g in (grad_half, grad_other)]
    query_grads = [[], []]
    key_grads, value_grads = [], []
    for head in range(heads):
        at = head * HEAD_DIM
        key = qkv[:, width + at : width + at + HEAD_DIM]
        value = qkv[:, 2 * width + at : 2 * width + at + HEAD_DIM]
        key_grad = value_grad = None
        for number in range(2):
            here = slice(number * half, (number + 1) * half)
            query = qkv[here, at : at + HEAD_DIM]
            grad = grad_attn[number][:, at : at + HEAD_DIM]
            scores = dot(query, key, 1, 1) * 0.125 + mask[here, :]
            probs = jnp.exp(scores - lse[here, head : head + 1])
            grad_probs = dot(grad, value, 1, 1)
            inner = jnp.sum(probs * grad_probs, axis=-1, keepdims=True)
            grad_scores = (probs * (grad_probs - inner)).astype(LOW)
            query_grads[number].append(dot(grad_scores, key, 1, 0) * 0.125)
            more_key = dot(grad_scores, query, 0, 0)
            more_value = dot(probs.astype(LOW), grad, 0, 0)
            key_grad = more_key if key_grad is None else key_grad + more_key
            value_grad = more_value if value_grad is None else value_grad + more_value
        key_grads.append(key_grad * 0.125)
        value_grads.append(value_grad)
    for number in range(2):
        here = slice(number * half, (number + 1) * half)
        grad_qkv[here, :] = jnp.concatenate(
            query_grads[number] + [k[here] for k in key_grads] + [v[here] for v in value_grads], axis=1
        ).astype(LOW)
    gain_sum = shift_sum = 0.0
    for number in range(2):
        here = slice(number * half, (number + 1) * half)
        back = dot(grad_qkv[here, :], wqkv[...], 1, 1)
        source = jnp.concatenate([own[...], near[...]], axis=0) if number == 0 else pair[...]
        scaled, _ = norm_parts(source.astype(F32))
        gain_sum += jnp.sum(back * scaled, axis=0, keepdims=True)
        shift_sum += jnp.sum(back, axis=0, keepdims=True)
        if number == 0:
            keep[...] = back
        else:
            send[...] = back.astype(LOW)
    late[...] = jnp.concatenate([early[:2, :], gain_sum, shift_sum, early[4:, :]], axis=0)
    sums = jnp.sum(grad_qkv[...].astype(F32), axis=0, keepdims=True)
    qkv_sum[...] = jnp.concatenate([sums, jnp.zeros((7, sums.shape[1]), F32)], axis=0)


def last_grad_body(
    size, scal, grad_half, grad_other, mixed, own, near, pair, rows, grad_qkv, late, fc_sum, qkv_sum, sel, *refs
):
    pieces, (whole, normed) = refs[:size], refs[size:]
    part = own.shape[0]
    half = 2 * part
    sources = (own[...], near[...], pair[:part, :], pair[part:, :])
    for number, source in enumerate(sources):
        scaled, _ = norm_parts(source.astype(F32))
        normed[number * part : (number + 1) * part, :] = (scaled * rows[2:3, :] + rows[3:4, :]).astype(LOW)
    qkv_cols = grad_qkv.shape[1]
    split = VEC_COLS + qkv_cols
    placed = lax.dot_general(
        qkv_sum[...], sel[...].astype(F32), (((1,), (1,)), ((), ())),
        preferred_element_type=F32, precision=lax.Precision.HIGHEST,
    )
    line = jnp.concatenate([late[:6, :], fc_sum[...], placed[:1]], axis=0)
    lack = jnp.zeros((VEC_COLS - 8, line.shape[1]), F32)
    whole[:, :VEC_COLS] = jnp.concatenate([line, lack], axis=0).T
    whole[:, VEC_COLS:] = jnp.concatenate(
        [
            dot(normed[...], grad_qkv[...], 0, 0),
            dot(grad_half[...], mixed[:half, :], 0, 0) + dot(grad_other[...], mixed[half:, :], 0, 0),
        ],
        axis=1,
    )
    put_pieces(scal[0], whole, pieces)


def input_body(keep, far, middle_grad, own, rows, out):
    part = own.shape[0]
    grad = keep[:part, :] + far[...].astype(F32)
    scaled, inverse = norm_parts(own[...].astype(F32))
    out[...] = middle_grad[...] + norm_back(grad, scaled, inverse, rows[2:3, :])


def total_of(refs):
    total = refs[0][...]
    for ref in refs[1:]:
        total = total + ref[...].astype(F32)
    return total


def sum_feed_body(size, *refs):
    total = total_of(refs[:size])
    wfc, wproj = refs[size:]
    cols = wfc.shape[1]
    wfc[...] = total[:, :cols]
    wproj[...] = turned_wide(total[:, cols:])


def sum_last_body(size, *refs):
    total = total_of(refs[:size])
    wqkv, wout, vecs = refs[size:]
    width = wout.shape[0]
    for number in range(3):
        low = VEC_COLS + number * width
        wqkv[number] = total[:, low : low + width]
    wout[...] = turned_wide(total[:, VEC_COLS + 3 * width :])
    vecs[...] = turned_wide(total[:, :VEC_COLS])[:8]


def local(
    tokens,
    segments,
    grad_out,
    w_qkv,
    b_qv,
    w_out,
    b_out,
    w_fc,
    b_fc,
    w_proj,
    b_proj,
    ln1_gain,
    ln1_bias,
    ln2_gain,
    ln2_bias,
):
    size = lax.axis_size("fsdp")
    direct = size == DIRECT_SIZE
    me = lax.axis_index("fsdp")
    chunk, hidden_cols = w_fc.shape
    own_rows, width = tokens.shape
    seq_rows = segments.shape[0]
    half = 2 * own_rows
    head_cols = w_out.shape[0]
    qkv_cols = 3 * head_cols
    qv_count = b_qv.shape[1]
    place = lax.axis_index("seq") * 2 + lax.axis_index("tensor")
    scal = jnp.stack([me, place]).astype(jnp.int32)
    parts = size if direct else 1

    near = swap(tokens, "tensor")
    pair = swap(jnp.concatenate([tokens, near]), "seq")

    flat_qv = jnp.pad(b_qv.reshape(-1), (0, chunk - 2 * qv_count))
    vecs = jnp.stack([b_out, b_proj, ln1_gain, ln1_bias, ln2_gain, ln2_bias, b_fc, flat_qv])
    col = np.arange(qkv_cols)
    inner = col % head_cols
    source = (inner // qv_count) * chunk + inner % qv_count + qv_count * (col >= 2 * head_cols)
    used = (col < head_cols) | (col >= 2 * head_cols)
    row_number = lax.broadcasted_iota(jnp.int32, (width, qkv_cols), 0)
    sel = (row_number == jnp.asarray(np.where(used, source, -1), jnp.int32)[None, :]).astype(LOW)

    rows_shape = shape(8, width, F32)
    bias_shape = shape(8, qkv_cols, F32)
    wqkv_shape, wo_shape = shape(width, qkv_cols, LOW), shape(width, head_cols, LOW)
    if direct:
        (first,) = on_core(
            pack_first_body, [shape(chunk, VEC_COLS + qkv_cols + head_cols, LOW)], [], [w_qkv, w_out, vecs]
        )
        (second,) = on_core(pack_second_body, [shape(chunk, 2 * hidden_cols, LOW)], [], [w_fc, w_proj])
        firsts = pieces_of(first)
        second = after(second, *firsts[1:6])
        seconds = pieces_of(second)
    else:
        lack = jnp.zeros((chunk, VEC_COLS - 8), LOW)
        first = jnp.concatenate([vecs.T, lack, w_qkv[0], w_qkv[1], w_qkv[2], w_out.T], axis=1)
        second = jnp.concatenate([w_fc, w_proj.T], axis=1)
        firsts = [lax.all_gather(first, "fsdp", axis=0, tiled=True)]
        seconds = [lax.all_gather(second, "fsdp", axis=0, tiled=True)]
        scal = scal * jnp.asarray([0, 1], jnp.int32)
    wqkv, wo, rows, bias = on_core(
        functools.partial(open_first_body, parts),
        [wqkv_shape, wo_shape, rows_shape, bias_shape],
        [scal],
        [*firsts, sel],
        [pltpu.VMEM((width, VEC_COLS), F32)],
    )
    wo_near = swap(wo, "tensor")
    wo_pair = swap(jnp.concatenate([wo, wo_near], axis=1), "seq")

    blocks = [place ^ b for b in range(4)]
    docs = jnp.concatenate([lax.dynamic_slice_in_dim(segments, b * own_rows, own_rows, 0) for b in blocks])
    spots = jnp.concatenate([b * own_rows + jnp.arange(own_rows, dtype=jnp.int32) for b in blocks])
    marks = [docs[:, None], docs[None, :], spots[:, None], spots[None, :]]

    mask_scratch = pltpu.VMEM((seq_rows, seq_rows), F32)
    normed_scratch = pltpu.VMEM((seq_rows, width), LOW)
    qkv, mixed, lse = on_core(
        attend_body,
        [shape(seq_rows, qkv_cols, LOW), shape(seq_rows, head_cols, LOW), shape(seq_rows, 128, F32)],
        [],
        [tokens, near, pair, wqkv, bias, rows, *marks],
        [normed_scratch, mask_scratch],
        flops=2 * seq_rows * (width * qkv_cols + 2 * head_cols * seq_rows),
    )
    mixed_near = swap(mixed, "tensor")
    crossed = mixed_near.reshape(2, 2, own_rows, head_cols)[:, ::-1].reshape(seq_rows, head_cols)
    mixed_pair = swap(jnp.concatenate([mixed, crossed], axis=1), "seq")

    square = 2 * seq_rows * width * hidden_cols
    wf, wp, da, cot = on_core(
        functools.partial(open_second_body, parts),
        [
            shape(width, hidden_cols, LOW),
            shape(width, hidden_cols, LOW),
            shape(seq_rows, hidden_cols, F32),
            shape(seq_rows, width, LOW),
        ],
        [scal],
        [*seconds, grad_out],
        flops=square,
    )
    keep, send, middle, normed_two, active, grad_hidden = on_core(
        feed_body,
        [
            shape(half, width, F32),
            shape(half, width, LOW),
            shape(half, width, F32),
            shape(seq_rows, width, LOW),
            shape(seq_rows, hidden_cols, LOW),
            shape(seq_rows, hidden_cols, LOW),
        ],
        [],
        [tokens, near, pair, mixed, mixed_near, mixed_pair, wo, wo_near, wo_pair, wf, rows, da],
        flops=3 * square,
    )
    part_two = keep + swap(send, "seq").astype(F32)
    far = swap(part_two.astype(LOW), "tensor")

    piece_cols = 2 * hidden_cols
    ff_pieces = [shape(width // parts, piece_cols, F32 if step == 0 else LOW) for step in range(parts)]
    out_keep, out_send, fc_sum, *grad_ff = on_core(
        functools.partial(feed_grad_body, parts),
        [shape(half, width, F32), shape(half, width, LOW), shape(1, hidden_cols, F32), *ff_pieces],
        [scal],
        [active, wp, normed_two, grad_hidden, cot],
        [pltpu.VMEM((width, piece_cols), F32)],
        flops=3 * square,
    )
    far = after(far, fc_sum)
    grad_mid_half, grad_mid_own, early = on_core(
        middle_body,
        [shape(half, width, LOW), shape(own_rows, width, F32), rows_shape],
        [],
        [part_two, far, middle, cot, rows],
    )
    grad_mid_other = swap(grad_mid_half, "seq")

    keep_one, send_one, grad_qkv, late, qkv_sum = on_core(
        attend_back_body,
        [
            shape(half, width, F32),
            shape(half, width, LOW),
            shape(seq_rows, qkv_cols, LOW),
            rows_shape,
            bias_shape,
        ],
        [],
        [grad_mid_half, grad_mid_other, wo, wqkv, qkv, lse, tokens, near, pair, early, *marks],
        [mask_scratch],
        flops=2 * seq_rows * (width * (qkv_cols + head_cols) + 5 * head_cols * seq_rows),
    )
    part_one = keep_one + swap(send_one, "seq").astype(F32)
    late = late + swap(late, "tensor")
    late = late + swap(late, "seq")
    far_one = swap(part_one[own_rows:].astype(LOW), "tensor")
    (grad_inputs,) = on_core(
        input_body,
        [shape(own_rows, width, F32)],
        [],
        [part_one, far_one, grad_mid_own, tokens, rows],
    )

    out_half = out_keep + swap(after(out_send, grad_qkv), "seq").astype(F32)
    out_own = out_half[:own_rows] + swap(out_half[own_rows:].astype(LOW), "tensor").astype(F32)
    result = (middle[:own_rows] + out_own + rows[1:2]).astype(LOW)

    last_cols = VEC_COLS + qkv_cols + head_cols
    last_pieces = [shape(width // parts, last_cols, F32 if step == 0 else LOW) for step in range(parts)]
    grad_last = on_core(
        functools.partial(last_grad_body, parts),
        last_pieces,
        [scal],
        [
            grad_mid_half, grad_mid_other, mixed, tokens, near, pair, rows, grad_qkv, late, fc_sum, qkv_sum, sel,
        ],
        [pltpu.VMEM((width, last_cols), F32), normed_scratch],
        flops=2 * seq_rows * width * (qkv_cols + head_cols),
    )

    if direct:
        got_ff = sums_of(grad_ff)
        got_last = sums_of(grad_last)
        grad_wfc, grad_wproj = on_core(
            functools.partial(sum_feed_body, len(got_ff)),
            [shape(chunk, hidden_cols, F32), shape(hidden_cols, chunk, F32)],
            [],
            got_ff,
        )
        grad_wqkv, grad_wout, sums = on_core(
            functools.partial(sum_last_body, len(got_last)),
            [jax.ShapeDtypeStruct((3, chunk, head_cols), F32), shape(head_cols, chunk, F32), shape(8, chunk, F32)],
            [],
            got_last,
        )
    else:
        sum_ff = lax.psum_scatter(grad_ff[0], "fsdp", scatter_dimension=0, tiled=True)
        sum_last = lax.psum_scatter(grad_last[0], "fsdp", scatter_dimension=0, tiled=True)
        grad_wfc, grad_wproj = sum_ff[:, :hidden_cols], sum_ff[:, hidden_cols:].T
        split = VEC_COLS + qkv_cols
        grad_wqkv = sum_last[:, VEC_COLS:split].reshape(chunk, 3, head_cols).transpose(1, 0, 2)
        grad_wout = sum_last[:, split:].T
        sums = sum_last[:, :8].T

    return (
        result,
        grad_inputs,
        grad_wqkv,
        grad_wout,
        grad_wfc,
        grad_wproj,
        sums[7, : 2 * qv_count].reshape(2, qv_count),
        sums[0],
        sums[6],
        sums[1],
        sums[2],
        sums[3],
        sums[4],
        sums[5],
    )


def solution(mesh):
    in_specs = (
        P(("fsdp", "seq", "tensor"), None),
        P("fsdp"),
        P("fsdp", None),
        P(None, "fsdp", ("seq", "tensor")),
        P(None, ("seq", "tensor", "fsdp")),
        P(("seq", "tensor"), "fsdp"),
        P("fsdp"),
        P("fsdp", ("seq", "tensor")),
        P(("seq", "tensor", "fsdp")),
        P(("seq", "tensor"), "fsdp"),
        P("fsdp"),
        P("fsdp"),
        P("fsdp"),
        P("fsdp"),
        P("fsdp"),
    )
    out_specs = (
        P(("fsdp", "seq", "tensor"), None),
        P(("fsdp", "seq", "tensor"), None),
        P(None, "fsdp", ("seq", "tensor")),
        P(("seq", "tensor"), "fsdp"),
        P("fsdp", ("seq", "tensor")),
        P(("seq", "tensor"), "fsdp"),
        P(None, ("seq", "tensor", "fsdp")),
        P("fsdp"),
        P(("seq", "tensor", "fsdp")),
        P("fsdp"),
        P("fsdp"),
        P("fsdp"),
        P("fsdp"),
        P("fsdp"),
    )
    return jax.shard_map(local, mesh=mesh, in_specs=in_specs, out_specs=out_specs, check_vma=False)
```

time: 327 us -> 196 us (0.60)
  waiting for transfers between devices: 157 us -> 74.6 us
  local copies, waits for them, and re-layouts: 56 us -> 16.9 us
  Pallas kernels: 0 us -> 35.2 us
  matrix products: 22.6 us -> 0 us
  other arithmetic: 24.3 us -> 9.8 us
  starting transfers between devices: 63.8 us -> 58.1 us
    ppermute x28, waiting for transfers between devices: 141 us -> 63.6 us  [send(): return lax.ppermute(value, 'fsdp', pairs)]
    pallas_call x0 -> x13, Pallas kernels: none -> 35.2 us  [on_core(): pl.pallas_call(body, out_shape=tuple(outs), in_specs=specs, out_specs=tup...]
    dot_general x18 -> x0, matrix products: 22.6 us -> none  [the longest x12 17.8 us: dot(): lax.dot_general(left, right, (((left_dim,), (right_dim,)), ((), ())), pre...]
    slice x22 -> x3, local copies, waits for them, and re-layouts: 10.3 us -> 0.06 us  [the longest x1 0.02 us: local(): far_one = swap(part_one[own_rows:].astype(LOW), 'tensor')]
    concatenate x3 -> x0, local copies, waits for them, and re-layouts: 8.76 us -> none  [the longest x1 4.75 us: local(): jnp.concatenate([b_out, b_proj, ln1_gain, ln1_bias, ln2_gain, ln2_bias, b...]
    unnamed x137 -> x52, local copies, waits for them, and re-layouts: 19.1 us -> 12.1 us
    ppermute x28, starting transfers between devices: 55.7 us -> 49.3 us  [send(): return lax.ppermute(value, 'fsdp', pairs)]
    concatenate x12 -> x5, other arithmetic: 9.67 us -> 3.99 us  [the longest x1 2.03 us: local(): wo_pair = swap(jnp.concatenate([wo, wo_near], axis=1), 'seq')]
  transfers between devices with their start and end apart: 43 -> 43, of which waited for: 20 -> 20; matrix products, arithmetic and copies ran while one was open for 25% -> 7% of each run, Pallas kernels for 0% -> 14%
where the time goes in v2:
time: 196 us
  waiting for transfers between devices  74.6 us (38%)
  starting transfers between devices  58.1 us (30%)
  Pallas kernels  35.2 us (18%)
  local copies, waits for them, and re-layouts  16.9 us (9%)
  other arithmetic  9.8 us (5%)
    ppermute x28, waiting for transfers between devices, send(): return lax.ppermute(value, 'fsdp', pairs)  63.6 us
    ppermute x28, starting transfers between devices, send(): return lax.ppermute(value, 'fsdp', pairs)  49.3 us
    pallas_call x13, Pallas kernels, on_core(): pl.pallas_call(body, out_shape=tuple(outs), in_specs=specs, out_specs=tup...  35.2 us
    unnamed x52, local copies, waits for them, and re-layouts  12.1 us
    ppermute x15, waiting for transfers between devices, swap(): return lax.ppermute(value, axis, [(0, 1), (1, 0)])  11 us
    ppermute x15, starting transfers between devices, swap(): return lax.ppermute(value, axis, [(0, 1), (1, 0)])  8.82 us
  transfers between devices with their start and end apart: 43, of which 20 were waited for; matrix products, arithmetic and copies ran while one was open for 7% of the time, Pallas kernels for 14%

profile of v2, /device:TPU:0, one launch (start us, length us, event | category | flops | bytes accessed | tf_op | source)
XLA Modules:
  0.0 195.6 jit_solution(5166565096110799411)
XLA Ops:
  4.2 5.1 %collective-permute-start.2 = (bf16[96,896]{1,0:T(8,128)(2,1)S(1)}, bf16[96,896]{1,0:T(8,128)(2,1)S(1)}, u32[]{:S(2)}, u32[]{:S(2)}) collective-permute-start(bf16[96,896]{1,0:T(8,128)(2,1)S(1)} %shard_map.263.refs_0_), channel_id=1, source_target_pairs={{0,24},{4,28},{8,0},{12,4},{16,8},{20,12},{24,16},{28,20},{1,25},{... | collective-permute-start | bytes 516104 | tf_op jit(solution)/shard_map/ppermute | solution.py:82
  10.2 3.8 %collective-permute-start.5 = (bf16[96,896]{1,0:T(8,128)(2,1)S(1)}, bf16[96,896]{1,0:T(8,128)(2,1)S(1)}, u32[]{:S(2)}, u32[]{:S(2)}) collective-permute-start(bf16[96,896]{1,0:T(8,128)(2,1)S(1)} %shard_map.263.refs_0_), channel_id=1, source_target_pairs={{0,28},{4,24},{8,4},{12,0},{16,12},{20,8},{24,20},{28,16},{1,29},{... | collective-permute-start | bytes 516104 | tf_op jit(solution)/shard_map/ppermute | solution.py:82
  19.4 2.2 %collective-permute-start.7 = (bf16[96,896]{1,0:T(8,128)(2,1)S(1)}, bf16[96,896]{1,0:T(8,128)(2,1)S(1)}, u32[]{:S(2)}, u32[]{:S(2)}) collective-permute-start(bf16[96,896]{1,0:T(8,128)(2,1)S(1)} %collective-permute-done.2.refs_1_), channel_id=1, source_target_pairs={{0,24},{4,28},{8,0},{12,4},{16,8},{20,12},{24,16},{28,20},{1,25},{... | collective-permute-start | bytes 516104 | tf_op jit(solution)/shard_map/ppermute | solution.py:82
  23.1 2.2 %collective-permute-done.5.refs_4_ = bf16[96,896]{1,0:T(8,128)(2,1)S(1)} collective-permute-done((bf16[96,896]{1,0:T(8,128)(2,1)S(1)}, bf16[96,896]{1,0:T(8,128)(2,1)S(1)}, u32[]{:S(2)}, u32[]{:S(2)}) %collective-permute-start.5) | collective-permute-done | bytes 172064 | tf_op jit(solution)/shard_map/ppermute | solution.py:82
  25.4 3.5 %collective-permute-done.7.refs_6_ = bf16[96,896]{1,0:T(8,128)(2,1)S(1)} collective-permute-done((bf16[96,896]{1,0:T(8,128)(2,1)S(1)}, bf16[96,896]{1,0:T(8,128)(2,1)S(1)}, u32[]{:S(2)}, u32[]{:S(2)}) %collective-permute-start.7) | collective-permute-done | bytes 172064 | tf_op jit(solution)/shard_map/ppermute | solution.py:82
  28.9 3.8 %collective-permute-done.8.refs_7_ = bf16[96,896]{1,0:T(8,128)(2,1)S(1)} collective-permute-done((bf16[96,896]{1,0:T(8,128)(2,1)S(1)}, bf16[96,896]{1,0:T(8,128)(2,1)S(1)}, u32[]{:S(2)}, u32[]{:S(2)}) %collective-permute-start.8) | collective-permute-done | bytes 172064 | tf_op jit(solution)/shard_map/ppermute | solution.py:82
  37.8 3.9 %shard_map.265 = (bf16[512,576]{1,0:T(8,128)(2,1)S(1)}, bf16[512,192]{1,0:T(8,128)(2,1)S(1)}, f32[512,128]{1,0:T(8,128)S(1)}) custom-call(bf16[128,768]{1,0:T(8,128)(2,1)S(1)} %copy-done, bf16[128,768]{1,0:T(8,128)(2,1)S(1)} %collective-permute-done.near, bf16[256,768]{1,0:T(8,128)(2,1)S(1)} %collective-permute-done.1.pair, bf16[768,576]{1,0:T(8,128)(2,1)S(1)} %copy-done.4, ...), custom_call_target="tpu_custom_call" | custom-call | flops 654311424 | bytes 2770944 | tf_op jit(solution)/shard_map/pallas_call | solution.py:30
  45.1 2.3 %collective-permute-start.13 = (bf16[96,1536]{1,0:T(8,128)(2,1)S(1)}, bf16[96,1536]{1,0:T(8,128)(2,1)S(1)}, u32[]{:S(2)}, u32[]{:S(2)}) collective-permute-start(bf16[96,1536]{1,0:T(8,128)(2,1)S(1)} %shard_map.266.refs_0_), channel_id=1, source_target_pairs={{0,24},{4,28},{8,0},{12,4},{16,8},{20,12},{24,16},{28,20},{1,25},{... | collective-permute-start | bytes 884744 | tf_op jit(solution)/shard_map/ppermute | solution.py:82
  49.5 2.7 %collective-permute-start.16 = (bf16[96,1536]{1,0:T(8,128)(2,1)S(1)}, bf16[96,1536]{1,0:T(8,128)(2,1)}, u32[]{:S(2)}, u32[]{:S(2)}) collective-permute-start(bf16[96,1536]{1,0:T(8,128)(2,1)S(1)} %shard_map.266.refs_0_), channel_id=1, source_target_pairs={{0,28},{4,24},{8,4},{12,0},{16,12},{20,8},{24,20},{28,16},{1,29},{... | collective-permute-start | bytes 884744 | tf_op jit(solution)/shard_map/ppermute | solution.py:82
  52.2 2.0 %pad_maximum_fusion = bf16[768,384]{1,0:T(8,128)(2,1)} fusion(bf16[768,192]{1,0:T(8,128)(2,1)} %collective-permute-done.11.wo_near, bf16[768,192]{1,0:T(8,128)(2,1)S(1)} %get-tuple-element.70.wo_own.wo), kind=kLoop, calls=%fused_computation.5 | loop fusion | flops 1179648 | bytes 1179648 | tf_op jit(solution)/shard_map/concatenate | solution.py:472
  57.1 9.2 %collective-permute-done.13.refs_1_ = bf16[96,1536]{1,0:T(8,128)(2,1)S(1)} collective-permute-done((bf16[96,1536]{1,0:T(8,128)(2,1)S(1)}, bf16[96,1536]{1,0:T(8,128)(2,1)S(1)}, u32[]{:S(2)}, u32[]{:S(2)}) %collective-permute-start.13) | collective-permute-done | bytes 294944 | tf_op jit(solution)/shard_map/ppermute | solution.py:82
  66.3 2.7 %collective-permute-start.17 = (bf16[96,1536]{1,0:T(8,128)(2,1)S(1)}, bf16[96,1536]{1,0:T(8,128)(2,1)S(1)}, u32[]{:S(2)}, u32[]{:S(2)}) collective-permute-start(bf16[96,1536]{1,0:T(8,128)(2,1)S(1)} %shard_map.266.refs_0_), channel_id=1, source_target_pairs={{0,4},{4,0},{8,12},{12,8},{16,20},{20,16},{24,28},{28,24},{1,5},{5... | collective-permute-start | bytes 884744 | tf_op jit(solution)/shard_map/ppermute | solution.py:82
  69.0 4.6 %collective-permute-done.16.refs_4_ = bf16[96,1536]{1,0:T(8,128)(2,1)} collective-permute-done((bf16[96,1536]{1,0:T(8,128)(2,1)S(1)}, bf16[96,1536]{1,0:T(8,128)(2,1)}, u32[]{:S(2)}, u32[]{:S(2)}) %collective-permute-start.16) | collective-permute-done | bytes 294944 | tf_op jit(solution)/shard_map/ppermute | solution.py:82
  74.2 4.5 %collective-permute-done.17.refs_5_ = bf16[96,1536]{1,0:T(8,128)(2,1)S(1)} collective-permute-done((bf16[96,1536]{1,0:T(8,128)(2,1)S(1)}, bf16[96,1536]{1,0:T(8,128)(2,1)S(1)}, u32[]{:S(2)}, u32[]{:S(2)}) %collective-permute-start.17) | collective-permute-done | bytes 294944 | tf_op jit(solution)/shard_map/ppermute | solution.py:82
  79.9 5.6 %collective-permute-done.19.refs_7_ = bf16[96,1536]{1,0:T(8,128)(2,1)S(1)} collective-permute-done((bf16[96,1536]{1,0:T(8,128)(2,1)}, bf16[96,1536]{1,0:T(8,128)(2,1)S(1)}, u32[]{:S(2)}, u32[]{:S(2)}) %collective-permute-start.19) | collective-permute-done | bytes 294944 | tf_op jit(solution)/shard_map/ppermute | solution.py:82
  85.5 3.3 %shard_map.267 = (bf16[768,768]{1,0:T(8,128)(2,1)S(1)}, bf16[768,768]{1,0:T(8,128)(2,1)}, f32[512,768]{1,0:T(8,128)}, bf16[512,768]{1,0:T(8,128)(2,1)S(1)}) custom-call(s32[2]{0:T(128)S(1)} %pad_add_fusion.2.scal, bf16[96,1536]{1,0:T(8,128)(2,1)S(1)} %shard_map.266.refs_0_, bf16[96,1536]{1,0:T(8,128)(2,1)S(1)} %collective-permute-done.13.refs_1_, ...), custom_call_target="tpu_custom_call" | custom-call | flops 603979776 | bytes 7864320 | tf_op jit(solution)/shard_map/pallas_call | solution.py:30
  90.8 7.2 %shard_map.268 = (f32[256,768]{1,0:T(8,128)S(1)}, bf16[256,768]{1,0:T(8,128)(2,1)S(1)}, f32[256,768]{1,0:T(8,128)S(1)}, bf16[512,768]{1,0:T(8,128)(2,1)S(1)}, bf...) custom-call(bf16[128,768]{1,0:T(8,128)(2,1)S(1)} %copy-done, bf16[128,768]{1,0:T(8,128)(2,1)S(1)} %collective-permute-done.near, ...), custom_call_target="tpu_custom_call" | custom-call | flops 1811939328 | bytes 9854976 | tf_op jit(solution)/shard_map/pallas_call | solution.py:30
  98.0 1.7 collective-permute-done.20
  101.3 4.6 %shard_map.269 = (f32[256,768]{1,0:T(8,128)S(1)}, bf16[256,768]{1,0:T(8,128)(2,1)}, f32[1,768]{1,0:T(1,128)S(1)}, f32[96,1536]{1,0:T(8,128)S(1)}, bf16[96,1536]{...) custom-call(s32[2]{0:T(128)S(1)} %pad_add_fusion.2.scal, ...), custom_call_target="tpu_custom_call" | custom-call | flops 1811939328 | bytes 8162304 | tf_op jit(solution)/shard_map/pallas_call | solution.py:30
  106.9 4.2 %collective-permute-done.21.far = bf16[256,768]{1,0:T(8,128)(2,1)S(1)} collective-permute-done((bf16[256,768]{1,0:T(8,128)(2,1)S(1)}, bf16[256,768]{1,0:T(8,128)(2,1)S(1)}, u32[]{:S(2)}, u32[]{:S(2)}) %collective-permute-start.21) | collective-permute-done | bytes 393248 | tf_op jit(solution)/shard_map/ppermute | solution.py:77
  112.5 3.0 %collective-permute-start.41 = (bf16[96,1536]{1,0:T(8,128)(2,1)S(1)}, bf16[96,1536]{1,0:T(8,128)(2,1)S(1)}, u32[]{:S(2)}, u32[]{:S(2)}) collective-permute-start(bf16[96,1536]{1,0:T(8,128)(2,1)S(1)} %get-tuple-element.114), channel_id=1, source_target_pairs={{0,24},{4,28},{8,0},{12,4},{16,8},{20,12},{24,16},{28,20},{1,25},{... | collective-permute-start | bytes 884744 | tf_op jit(solution)/shard_map/ppermute | solution.py:82
  115.5 6.9 %shard_map.271 = (f32[256,768]{1,0:T(8,128)S(1)}, bf16[256,768]{1,0:T(8,128)(2,1)}, bf16[512,576]{1,0:T(8,128)(2,1)S(1)}, f32[8,768]{1,0:T(8,128)S(1)}, f32[8,576]{1,0:T(8,128)S(1)}) custom-call(bf16[256,768]{1,0:T(8,128)(2,1)S(1)} %get-tuple-element.86.grad_half, bf16[256,768]{1,0:T(8,128)(2,1)S(1)} %collective-permute-done.22.grad_other, ...), custom_call_target="tpu_custom_call" | custom-call | flops 1107296256 | bytes 5449728 | tf_op jit(solution)/shard_map/pallas_call | solution.py:30
  124.9 3.8 %collective-permute-start.36 = (bf16[96,1536]{1,0:T(8,128)(2,1)S(1)}, bf16[96,1536]{1,0:T(8,128)(2,1)S(1)}, u32[]{:S(2)}, u32[]{:S(2)}) collective-permute-start(bf16[96,1536]{1,0:T(8,128)(2,1)S(1)} %get-tuple-element.108), channel_id=1, source_target_pairs={{0,24},{4,28},{8,0},{12,4},{16,8},{20,12},{24,16},{28,20},{1,25},{... | collective-permute-start | bytes 884744 | tf_op jit(solution)/shard_map/ppermute | solution.py:82
  130.5 4.7 %collective-permute-start.42 = (bf16[96,1536]{1,0:T(8,128)(2,1)S(1)}, bf16[96,1536]{1,0:T(8,128)(2,1)S(1)}, u32[]{:S(2)}, u32[]{:S(2)}) collective-permute-start(bf16[96,1536]{1,0:T(8,128)(2,1)S(1)} %add_convert_fusion), channel_id=1, source_target_pairs={{0,28},{4,24},{8,4},{12,0},{16,12},{20,8},{24,20},{28,16},{1,29},{... | collective-permute-start | bytes 884744 | tf_op jit(solution)/shard_map/ppermute | solution.py:82
  135.3 4.2 %shard_map.273 = (f32[96,896]{1,0:T(8,128)S(1)}, bf16[96,896]{1,0:T(8,128)(2,1)S(1)}, bf16[96,896]{1,0:T(8,128)(2,1)S(1)}, bf16[96,896]{1,0:T(8,128)(2,1)S(1)}, ...) custom-call(s32[2]{0:T(128)S(1)} %pad_add_fusion.2.scal, ...), custom_call_target="tpu_custom_call" | custom-call | flops 603979776 | bytes 4862976 | tf_op jit(solution)/shard_map/pallas_call | solution.py:30
  139.4 3.2 %collective-permute-start.34 = (bf16[96,896]{1,0:T(8,128)(2,1)S(1)}, bf16[96,896]{1,0:T(8,128)(2,1)S(1)}, u32[]{:S(2)}, u32[]{:S(2)}) collective-permute-start(bf16[96,896]{1,0:T(8,128)(2,1)S(1)} %get-tuple-element.104), channel_id=1, source_target_pairs={{0,24},{4,28},{8,0},{12,4},{16,8},{20,12},{24,16},{28,20},{1,25},{... | collective-permute-start | bytes 516104 | tf_op jit(solution)/shard_map/ppermute | solution.py:82
  143.5 12.9 %collective-permute-done.34 = bf16[96,896]{1,0:T(8,128)(2,1)S(1)} collective-permute-done((bf16[96,896]{1,0:T(8,128)(2,1)S(1)}, bf16[96,896]{1,0:T(8,128)(2,1)S(1)}, u32[]{:S(2)}, u32[]{:S(2)}) %collective-permute-start.34) | collective-permute-done | bytes 172064 | tf_op jit(solution)/shard_map/ppermute | solution.py:82
  158.1 2.9 %collective-permute-start.29 = (bf16[96,896]{1,0:T(8,128)(2,1)S(1)}, bf16[96,896]{1,0:T(8,128)(2,1)S(1)}, u32[]{:S(2)}, u32[]{:S(2)}) collective-permute-start(bf16[96,896]{1,0:T(8,128)(2,1)S(1)} %get-tuple-element.98), channel_id=1, source_target_pairs={{0,24},{4,28},{8,0},{12,4},{16,8},{20,12},{24,16},{28,20},{1,25},{... | collective-permute-start | bytes 516104 | tf_op jit(solution)/shard_map/ppermute | solution.py:82
  161.0 8.3 %collective-permute-done.32 = bf16[96,896]{1,0:T(8,128)(2,1)S(1)} collective-permute-done((bf16[96,896]{1,0:T(8,128)(2,1)S(1)}, bf16[96,896]{1,0:T(8,128)(2,1)S(1)}, u32[]{:S(2)}, u32[]{:S(2)}) %collective-permute-start.32) | collective-permute-done | bytes 172064 | tf_op jit(solution)/shard_map/ppermute | solution.py:82
  170.6 4.7 %collective-permute-start.35 = (bf16[96,896]{1,0:T(8,128)(2,1)}, bf16[96,896]{1,0:T(8,128)(2,1)S(1)}, u32[]{:S(2)}, u32[]{:S(2)}) collective-permute-start(bf16[96,896]{1,0:T(8,128)(2,1)} %add_convert_fusion.2), channel_id=1, source_target_pairs={{0,28},{4,24},{8,4},{12,0},{16,12},{20,8},{24,20},{28,16},{1,29},{... | collective-permute-start | bytes 516104 | tf_op jit(solution)/shard_map/ppermute | solution.py:82
  175.3 3.3 %collective-permute-done.30.refs_2_ = bf16[96,896]{1,0:T(8,128)(2,1)S(1)} collective-permute-done((bf16[96,896]{1,0:T(8,128)(2,1)S(1)}, bf16[96,896]{1,0:T(8,128)(2,1)S(1)}, u32[]{:S(2)}, u32[]{:S(2)}) %collective-permute-start.30) | collective-permute-done | bytes 172064 | tf_op jit(solution)/shard_map/ppermute | solution.py:82
  189.8 3.0 %collective-permute-done.26.far = bf16[128,768]{1,0:T(8,128)(2,1)S(1)} collective-permute-done((bf16[128,768]{1,0:T(8,128)(2,1)S(1)}, bf16[128,768]{1,0:T(8,128)(2,1)S(1)}, u32[]{:S(2)}, u32[]{:S(2)}) %collective-permute-start.26) | collective-permute-done | bytes 196640 | tf_op jit(solution)/shard_map/ppermute | solution.py:77
  (151 shorter events, 54.4 us)
Async XLA Ops:
  4.2 12.5 %collective-permute-start.2 = (bf16[96,896]{1,0:T(8,128)(2,1)S(1)}, bf16[96,896]{1,0:T(8,128)(2,1)S(1)}, u32[]{:S(2)}, u32[]{:S(2)}) collective-permute-start(bf16[96,896]{1,0:T(8,128)(2,1)S(1)} %shard_map.263.refs_0_), channel_id=1, source_target_pairs={{0,24},{4,28},{8,0},{12,4},{16,8},{20,12},{24,16},{28,20},{1,25},{... | collective-permute-start | bytes 516104 | tf_op jit(solution)/shard_map/ppermute | solution.py:82
  9.3 10.1 %collective-permute-start.3 = (bf16[96,896]{1,0:T(8,128)(2,1)S(1)}, bf16[96,896]{1,0:T(8,128)(2,1)S(1)}, u32[]{:S(2)}, u32[]{:S(2)}) collective-permute-start(bf16[96,896]{1,0:T(8,128)(2,1)S(1)} %shard_map.263.refs_0_), channel_id=1, source_target_pairs={{0,12},{4,8},{8,20},{12,16},{16,28},{20,24},{24,4},{28,0},{1,13},{... | collective-permute-start | bytes 516104 | tf_op jit(solution)/shard_map/ppermute | solution.py:82
  9.3 13.8 %collective-permute-start.4 = (bf16[96,896]{1,0:T(8,128)(2,1)S(1)}, bf16[96,896]{1,0:T(8,128)(2,1)S(1)}, u32[]{:S(2)}, u32[]{:S(2)}) collective-permute-start(bf16[96,896]{1,0:T(8,128)(2,1)S(1)} %shard_map.263.refs_0_), channel_id=1, source_target_pairs={{0,8},{4,12},{8,16},{12,20},{16,24},{20,28},{24,0},{28,4},{1,9},{5... | collective-permute-start | bytes 516104 | tf_op jit(solution)/shard_map/ppermute | solution.py:82
  10.2 15.1 %collective-permute-start.5 = (bf16[96,896]{1,0:T(8,128)(2,1)S(1)}, bf16[96,896]{1,0:T(8,128)(2,1)S(1)}, u32[]{:S(2)}, u32[]{:S(2)}) collective-permute-start(bf16[96,896]{1,0:T(8,128)(2,1)S(1)} %shard_map.263.refs_0_), channel_id=1, source_target_pairs={{0,28},{4,24},{8,4},{12,0},{16,12},{20,8},{24,20},{28,16},{1,29},{... | collective-permute-start | bytes 516104 | tf_op jit(solution)/shard_map/ppermute | solution.py:82
  19.4 9.5 %collective-permute-start.7 = (bf16[96,896]{1,0:T(8,128)(2,1)S(1)}, bf16[96,896]{1,0:T(8,128)(2,1)S(1)}, u32[]{:S(2)}, u32[]{:S(2)}) collective-permute-start(bf16[96,896]{1,0:T(8,128)(2,1)S(1)} %collective-permute-done.2.refs_1_), channel_id=1, source_target_pairs={{0,24},{4,28},{8,0},{12,4},{16,8},{20,12},{24,16},{28,20},{1,25},{... | collective-permute-start | bytes 516104 | tf_op jit(solution)/shard_map/ppermute | solution.py:82
  21.6 11.0 %collective-permute-start.8 = (bf16[96,896]{1,0:T(8,128)(2,1)S(1)}, bf16[96,896]{1,0:T(8,128)(2,1)S(1)}, u32[]{:S(2)}, u32[]{:S(2)}) collective-permute-start(bf16[96,896]{1,0:T(8,128)(2,1)S(1)} %collective-permute-done.3.refs_2_), channel_id=1, source_target_pairs={{0,8},{4,12},{8,16},{12,20},{16,24},{20,28},{24,0},{28,4},{1,9},{5... | collective-permute-start | bytes 516104 | tf_op jit(solution)/shard_map/ppermute | solution.py:82
  23.1 13.4 %collective-permute-start.1 = (bf16[256,768]{1,0:T(8,128)(2,1)}, bf16[256,768]{1,0:T(8,128)(2,1)S(1)}, u32[]{:S(2)}, u32[]{:S(2)}) collective-permute-start(bf16[256,768]{1,0:T(8,128)(2,1)} %pad_maximum_fusion.1), channel_id=1, source_target_pairs={{0,2},{2,0},{1,3},{3,1},{4,6},{6,4},{5,7},{7,5},{8,10},{10,8},{9,1... | collective-permute-start | bytes 1179656 | tf_op jit(solution)/shard_map/ppermute | solution.py:77
  34.6 14.8 %collective-permute-start.11 = (bf16[768,192]{1,0:T(8,128)(2,1)S(1)}, bf16[768,192]{1,0:T(8,128)(2,1)}, u32[]{:S(2)}, u32[]{:S(2)}) collective-permute-start(bf16[768,192]{1,0:T(8,128)(2,1)S(1)} %get-tuple-element.70.wo_own.wo), channel_id=1, source_target_pairs={{0,1},{1,0},{2,3},{3,2},{4,5},{5,4},{6,7},{7,6},{8,9},{9,8},{10,11... | collective-permute-start | bytes 884744 | tf_op jit(solution)/shard_map/ppermute | solution.py:77
  43.3 10.9 %collective-permute-start.9 = (bf16[512,192]{1,0:T(8,128)(2,1)S(1)}, bf16[512,192]{1,0:T(8,128)(2,1)}, u32[]{:S(2)}, u32[]{:S(2)}) collective-permute-start(bf16[512,192]{1,0:T(8,128)(2,1)S(1)} %get-tuple-element.69.mixed_own.mixed), channel_id=1, source_target_pairs={{0,1},{1,0},{2,3},{3,2},{4,5},{5,4},{6,7},{7,6},{8,9},{9,8},{10,11... | collective-permute-start | bytes 589832 | tf_op jit(solution)/shard_map/ppermute | solution.py:77
  45.1 21.2 %collective-permute-start.13 = (bf16[96,1536]{1,0:T(8,128)(2,1)S(1)}, bf16[96,1536]{1,0:T(8,128)(2,1)S(1)}, u32[]{:S(2)}, u32[]{:S(2)}) collective-permute-start(bf16[96,1536]{1,0:T(8,128)(2,1)S(1)} %shard_map.266.refs_0_), channel_id=1, source_target_pairs={{0,24},{4,28},{8,0},{12,4},{16,8},{20,12},{24,16},{28,20},{1,25},{... | collective-permute-start | bytes 884744 | tf_op jit(solution)/shard_map/ppermute | solution.py:82
  47.5 18.8 %collective-permute-start.14 = (bf16[96,1536]{1,0:T(8,128)(2,1)S(1)}, bf16[96,1536]{1,0:T(8,128)(2,1)}, u32[]{:S(2)}, u32[]{:S(2)}) collective-permute-start(bf16[96,1536]{1,0:T(8,128)(2,1)S(1)} %shard_map.266.refs_0_), channel_id=1, source_target_pairs={{0,12},{4,8},{8,20},{12,16},{16,28},{20,24},{24,4},{28,0},{1,13},{... | collective-permute-start | bytes 884744 | tf_op jit(solution)/shard_map/ppermute | solution.py:82
  47.9 21.1 %collective-permute-start.15 = (bf16[96,1536]{1,0:T(8,128)(2,1)S(1)}, bf16[96,1536]{1,0:T(8,128)(2,1)}, u32[]{:S(2)}, u32[]{:S(2)}) collective-permute-start(bf16[96,1536]{1,0:T(8,128)(2,1)S(1)} %shard_map.266.refs_0_), channel_id=1, source_target_pairs={{0,8},{4,12},{8,16},{12,20},{16,24},{20,28},{24,0},{28,4},{1,9},{5... | collective-permute-start | bytes 884744 | tf_op jit(solution)/shard_map/ppermute | solution.py:82
  49.5 24.1 %collective-permute-start.16 = (bf16[96,1536]{1,0:T(8,128)(2,1)S(1)}, bf16[96,1536]{1,0:T(8,128)(2,1)}, u32[]{:S(2)}, u32[]{:S(2)}) collective-permute-start(bf16[96,1536]{1,0:T(8,128)(2,1)S(1)} %shard_map.266.refs_0_), channel_id=1, source_target_pairs={{0,28},{4,24},{8,4},{12,0},{16,12},{20,8},{24,20},{28,16},{1,29},{... | collective-permute-start | bytes 884744 | tf_op jit(solution)/shard_map/ppermute | solution.py:82
  54.2 36.5 %collective-permute-start.12 = (bf16[768,384]{1,0:T(8,128)(2,1)}, bf16[768,384]{1,0:T(8,128)(2,1)}, u32[]{:S(2)}, u32[]{:S(2)}) collective-permute-start(bf16[768,384]{1,0:T(8,128)(2,1)} %pad_maximum_fusion), channel_id=1, source_target_pairs={{0,2},{2,0},{1,3},{3,1},{4,6},{6,4},{5,7},{7,5},{8,10},{10,8},{9,1... | collective-permute-start | bytes 1769480 | tf_op jit(solution)/shard_map/ppermute | solution.py:77
  66.3 24.5 %collective-permute-start.10 = (bf16[512,384]{1,0:T(8,128)(2,1)S(1)}, bf16[512,384]{1,0:T(8,128)(2,1)S(1)}, u32[]{:S(2)}, u32[]{:S(2)}) collective-permute-start(bf16[512,384]{1,0:T(8,128)(2,1)S(1)} %pad_maximum_fusion.2), channel_id=1, source_target_pairs={{0,2},{2,0},{1,3},{3,1},{4,6},{6,4},{5,7},{7,5},{8,10},{10,8},{9,1... | collective-permute-start | bytes 1179656 | tf_op jit(solution)/shard_map/ppermute | solution.py:77
  66.3 12.4 %collective-permute-start.17 = (bf16[96,1536]{1,0:T(8,128)(2,1)S(1)}, bf16[96,1536]{1,0:T(8,128)(2,1)S(1)}, u32[]{:S(2)}, u32[]{:S(2)}) collective-permute-start(bf16[96,1536]{1,0:T(8,128)(2,1)S(1)} %shard_map.266.refs_0_), channel_id=1, source_target_pairs={{0,4},{4,0},{8,12},{12,8},{16,20},{20,16},{24,28},{28,24},{1,5},{5... | collective-permute-start | bytes 884744 | tf_op jit(solution)/shard_map/ppermute | solution.py:82
  69.0 10.9 %collective-permute-start.18 = (bf16[96,1536]{1,0:T(8,128)(2,1)S(1)}, bf16[96,1536]{1,0:T(8,128)(2,1)S(1)}, u32[]{:S(2)}, u32[]{:S(2)}) collective-permute-start(bf16[96,1536]{1,0:T(8,128)(2,1)S(1)} %collective-permute-done.13.refs_1_), channel_id=1, source_target_pairs={{0,24},{4,28},{8,0},{12,4},{16,8},{20,12},{24,16},{28,20},{1,25},{... | collective-permute-start | bytes 884744 | tf_op jit(solution)/shard_map/ppermute | solution.py:82
  73.6 12.0 %collective-permute-start.19 = (bf16[96,1536]{1,0:T(8,128)(2,1)}, bf16[96,1536]{1,0:T(8,128)(2,1)S(1)}, u32[]{:S(2)}, u32[]{:S(2)}) collective-permute-start(bf16[96,1536]{1,0:T(8,128)(2,1)} %collective-permute-done.14.refs_2_), channel_id=1, source_target_pairs={{0,8},{4,12},{8,16},{12,20},{16,24},{20,28},{24,0},{28,4},{1,9},{5... | collective-permute-start | bytes 884744 | tf_op jit(solution)/shard_map/ppermute | solution.py:82
  99.8 11.2 %collective-permute-start.21 = (bf16[256,768]{1,0:T(8,128)(2,1)S(1)}, bf16[256,768]{1,0:T(8,128)(2,1)S(1)}, u32[]{:S(2)}, u32[]{:S(2)}) collective-permute-start(bf16[256,768]{1,0:T(8,128)(2,1)S(1)} %get-tuple-element.146), channel_id=1, source_target_pairs={{0,1},{1,0},{2,3},{3,2},{4,5},{5,4},{6,7},{7,6},{8,9},{9,8},{10,11... | collective-permute-start | bytes 1179656 | tf_op jit(solution)/shard_map/ppermute | solution.py:77
  112.5 16.8 %collective-permute-start.41 = (bf16[96,1536]{1,0:T(8,128)(2,1)S(1)}, bf16[96,1536]{1,0:T(8,128)(2,1)S(1)}, u32[]{:S(2)}, u32[]{:S(2)}) collective-permute-start(bf16[96,1536]{1,0:T(8,128)(2,1)S(1)} %get-tuple-element.114), channel_id=1, source_target_pairs={{0,24},{4,28},{8,0},{12,4},{16,8},{20,12},{24,16},{28,20},{1,25},{... | collective-permute-start | bytes 884744 | tf_op jit(solution)/shard_map/ppermute | solution.py:82
  124.9 14.6 %collective-permute-start.39 = (bf16[96,1536]{1,0:T(8,128)(2,1)S(1)}, bf16[96,1536]{1,0:T(8,128)(2,1)S(1)}, u32[]{:S(2)}, u32[]{:S(2)}) collective-permute-start(bf16[96,1536]{1,0:T(8,128)(2,1)S(1)} %get-tuple-element.112), channel_id=1, source_target_pairs={{0,8},{4,12},{8,16},{12,20},{16,24},{20,28},{24,0},{28,4},{1,9},{5... | collective-permute-start | bytes 884744 | tf_op jit(solution)/shard_map/ppermute | solution.py:82
  124.9 17.9 %collective-permute-start.36 = (bf16[96,1536]{1,0:T(8,128)(2,1)S(1)}, bf16[96,1536]{1,0:T(8,128)(2,1)S(1)}, u32[]{:S(2)}, u32[]{:S(2)}) collective-permute-start(bf16[96,1536]{1,0:T(8,128)(2,1)S(1)} %get-tuple-element.108), channel_id=1, source_target_pairs={{0,24},{4,28},{8,0},{12,4},{16,8},{20,12},{24,16},{28,20},{1,25},{... | collective-permute-start | bytes 884744 | tf_op jit(solution)/shard_map/ppermute | solution.py:82
  128.7 29.4 %collective-permute-start.37 = (bf16[96,1536]{1,0:T(8,128)(2,1)S(1)}, bf16[96,1536]{1,0:T(8,128)(2,1)S(1)}, u32[]{:S(2)}, u32[]{:S(2)}) collective-permute-start(bf16[96,1536]{1,0:T(8,128)(2,1)S(1)} %get-tuple-element.109), channel_id=1, source_target_pairs={{0,12},{4,8},{8,20},{12,16},{16,28},{20,24},{24,4},{28,0},{1,13},{... | collective-permute-start | bytes 884744 | tf_op jit(solution)/shard_map/ppermute | solution.py:82
  128.7 29.4 %collective-permute-start.38 = (bf16[96,1536]{1,0:T(8,128)(2,1)S(1)}, bf16[96,1536]{1,0:T(8,128)(2,1)S(1)}, u32[]{:S(2)}, u32[]{:S(2)}) collective-permute-start(bf16[96,1536]{1,0:T(8,128)(2,1)S(1)} %get-tuple-element.110), channel_id=1, source_target_pairs={{0,4},{4,0},{8,12},{12,8},{16,20},{20,16},{24,28},{28,24},{1,5},{5... | collective-permute-start | bytes 884744 | tf_op jit(solution)/shard_map/ppermute | solution.py:82
  130.5 39.5 %collective-permute-start.42 = (bf16[96,1536]{1,0:T(8,128)(2,1)S(1)}, bf16[96,1536]{1,0:T(8,128)(2,1)S(1)}, u32[]{:S(2)}, u32[]{:S(2)}) collective-permute-start(bf16[96,1536]{1,0:T(8,128)(2,1)S(1)} %add_convert_fusion), channel_id=1, source_target_pairs={{0,28},{4,24},{8,4},{12,0},{16,12},{20,8},{24,20},{28,16},{1,29},{... | collective-permute-start | bytes 884744 | tf_op jit(solution)/shard_map/ppermute | solution.py:82
  139.4 16.9 %collective-permute-start.34 = (bf16[96,896]{1,0:T(8,128)(2,1)S(1)}, bf16[96,896]{1,0:T(8,128)(2,1)S(1)}, u32[]{:S(2)}, u32[]{:S(2)}) collective-permute-start(bf16[96,896]{1,0:T(8,128)(2,1)S(1)} %get-tuple-element.104), channel_id=1, source_target_pairs={{0,24},{4,28},{8,0},{12,4},{16,8},{20,12},{24,16},{28,20},{1,25},{... | collective-permute-start | bytes 516104 | tf_op jit(solution)/shard_map/ppermute | solution.py:82
  142.8 27.8 %collective-permute-start.40 = (bf16[96,1536]{1,0:T(8,128)(2,1)S(1)}, bf16[96,1536]{1,0:T(8,128)(2,1)S(1)}, u32[]{:S(2)}, u32[]{:S(2)}) collective-permute-start(bf16[96,1536]{1,0:T(8,128)(2,1)S(1)} %add_convert_fusion.1), channel_id=1, source_target_pairs={{0,8},{4,12},{8,16},{12,20},{16,24},{20,28},{24,0},{28,4},{1,9},{5... | collective-permute-start | bytes 884744 | tf_op jit(solution)/shard_map/ppermute | solution.py:82
  156.4 12.9 %collective-permute-start.32 = (bf16[96,896]{1,0:T(8,128)(2,1)S(1)}, bf16[96,896]{1,0:T(8,128)(2,1)S(1)}, u32[]{:S(2)}, u32[]{:S(2)}) collective-permute-start(bf16[96,896]{1,0:T(8,128)(2,1)S(1)} %get-tuple-element.102), channel_id=1, source_target_pairs={{0,8},{4,12},{8,16},{12,20},{16,24},{20,28},{24,0},{28,4},{1,9},{5... | collective-permute-start | bytes 516104 | tf_op jit(solution)/shard_map/ppermute | solution.py:82
  158.1 26.7 %collective-permute-start.25 = (bf16[256,768]{1,0:T(8,128)(2,1)}, bf16[256,768]{1,0:T(8,128)(2,1)}, u32[]{:S(2)}, u32[]{:S(2)}) collective-permute-start(bf16[256,768]{1,0:T(8,128)(2,1)} %get-tuple-element.93), channel_id=1, source_target_pairs={{0,2},{2,0},{1,3},{3,1},{4,6},{6,4},{5,7},{7,5},{8,10},{10,8},{9,1... | collective-permute-start | bytes 1179656 | tf_op jit(solution)/shard_map/ppermute | solution.py:77
  158.1 17.2 %collective-permute-start.29 = (bf16[96,896]{1,0:T(8,128)(2,1)S(1)}, bf16[96,896]{1,0:T(8,128)(2,1)S(1)}, u32[]{:S(2)}, u32[]{:S(2)}) collective-permute-start(bf16[96,896]{1,0:T(8,128)(2,1)S(1)} %get-tuple-element.98), channel_id=1, source_target_pairs={{0,24},{4,28},{8,0},{12,4},{16,8},{20,12},{24,16},{28,20},{1,25},{... | collective-permute-start | bytes 516104 | tf_op jit(solution)/shard_map/ppermute | solution.py:82
  170.0 12.0 %collective-permute-start.31 = (bf16[96,896]{1,0:T(8,128)(2,1)}, bf16[96,896]{1,0:T(8,128)(2,1)S(1)}, u32[]{:S(2)}, u32[]{:S(2)}) collective-permute-start(bf16[96,896]{1,0:T(8,128)(2,1)} %get-tuple-element.100), channel_id=1, source_target_pairs={{0,4},{4,0},{8,12},{12,8},{16,20},{20,16},{24,28},{28,24},{1,5},{5... | collective-permute-start | bytes 516104 | tf_op jit(solution)/shard_map/ppermute | solution.py:82
  170.6 11.5 %collective-permute-start.35 = (bf16[96,896]{1,0:T(8,128)(2,1)}, bf16[96,896]{1,0:T(8,128)(2,1)S(1)}, u32[]{:S(2)}, u32[]{:S(2)}) collective-permute-start(bf16[96,896]{1,0:T(8,128)(2,1)} %add_convert_fusion.2), channel_id=1, source_target_pairs={{0,28},{4,24},{8,4},{12,0},{16,12},{20,8},{24,20},{28,16},{1,29},{... | collective-permute-start | bytes 516104 | tf_op jit(solution)/shard_map/ppermute | solution.py:82
  (36 other events, 191.8 us)

commit v3 on v2

--- a/solution.py
+++ b/solution.py
@@ -21,9 +21,9 @@
     return jax.ShapeDtypeStruct((rows, cols), dtype)
 
 
-def on_core(body, outs, scalars, arrays, scratch=(), flops=0, limit=48):
+def on_core(body, outs, scalars, arrays, scratch=(), flops=0, limit=40):
     specs = [pl.BlockSpec(memory_space=pltpu.SMEM)] * len(scalars)
-    specs += [pl.BlockSpec(memory_space=pltpu.VMEM)] * len(arrays)
+    specs += [pl.BlockSpec()] * len(arrays)
     moved = sum(int(np.prod(a.shape)) * a.dtype.itemsize for a in arrays) + sum(
         int(np.prod(o.shape)) * o.dtype.itemsize for o in outs
     )
@@ -31,7 +31,7 @@
         body,
         out_shape=tuple(outs),
         in_specs=specs,
-        out_specs=tuple(pl.BlockSpec(memory_space=pltpu.VMEM) for _ in outs),
+        out_specs=tuple(pl.BlockSpec() for _ in outs),
         scratch_shapes=list(scratch),
         compiler_params=pltpu.CompilerParams(vmem_limit_bytes=limit * 2**20),
         cost_estimate=pl.CostEstimate(flops=flops, bytes_accessed=moved, transcendentals=0),
@@ -86,21 +86,37 @@
     return lax.optimization_barrier((value, *earlier))[0]
 
 
-def pieces_of(chunk):
-    ahead = send(chunk, 3, 0)
-    behind = send(chunk, 1, 1)
-    rest = [send(chunk, 1, 0), send(chunk, 3, 1), send(chunk, 0, 1)]
-    return [chunk, ahead, behind, *rest, send(ahead, 3, 0), send(behind, 1, 0)]
-
-
-def sums_of(pieces):
-    own, ahead, behind, near_behind, near_ahead, other, far, far_other = pieces
-    passed = send(far, 1, 0), send(far_other, 3, 0)
-    rest = [send(near_behind, 3, 0), send(near_ahead, 1, 1), send(other, 0, 1)]
-    ahead, behind = [
-        (mine.astype(F32) + got.astype(F32)).astype(LOW) for mine, got in zip((ahead, behind), passed)
-    ]
-    return [own, *rest, send(ahead, 1, 0), send(behind, 3, 1)]
+def pieces_ring_first(chunk):
+    ahead, behind = send(chunk, 3, 0), send(chunk, 1, 0)
+    other = send(chunk, 0, 1)
+    far = send(ahead, 3, 0)
+    across = [send(behind, 0, 1), send(ahead, 0, 1)]
+    return [chunk, ahead, across[0], behind, across[1], other, far, send(far, 0, 1)]
+
+
+def pieces_mixed(chunk, ring_free, pair_free):
+    ahead, behind = [send(after(chunk, ring_free), turn, 0) for turn in (3, 1)]
+    other = send(after(chunk, *pair_free), 0, 1)
+    far = send(ahead, 3, 0)
+    return [chunk, ahead, send(other, 1, 0), behind, send(ahead, 0, 1), other, far, send(far, 0, 1)]
+
+
+def added(*values):
+    total = values[0].astype(F32)
+    for value in values[1:]:
+        total = total + value.astype(F32)
+    return total.astype(LOW)
+
+
+def over_pair(pieces):
+    return [send(pieces[step], 0, 1) for step in (7, 4, 2, 5)]
+
+
+def round_ring(pieces, got):
+    far = send(added(pieces[6], got[0]), 1, 0)
+    behind = send(added(pieces[3], got[2]), 3, 0)
+    ahead = send(added(pieces[1], got[1], far), 1, 0)
+    return [pieces[0], got[3], ahead, behind]
 
 
 def row_start(me, step, rows):
@@ -109,37 +125,44 @@
     return pl.multiple_of((pair * 2 + (lax.rem(me, 2) ^ flip)) * rows, rows)
 
 
-def pack_first_body(wqkv, wout, vecs, out):
+def pack_body(wqkv, wout, wfc, wproj, bqv, *refs):
+    vecs, first, second = refs[:-2], refs[-2], refs[-1]
     rows = wqkv.shape[1]
-    cols = turned_wide(vecs[...].astype(F32))[:rows].astype(LOW)
-    lack = jnp.zeros((rows, VEC_COLS - cols.shape[1]), LOW)
-    out[...] = jnp.concatenate(
-        [cols, lack, wqkv[0], wqkv[1], wqkv[2], turned(wout[...])], axis=1
-    )
-
-
-def pack_second_body(wfc, wproj, out):
-    out[...] = jnp.concatenate([wfc[...], turned(wproj[...])], axis=1)
+    lines = [vec[...].astype(F32).reshape(1, rows) for vec in vecs]
+    lack = jnp.zeros((2, rows - bqv.shape[1]), F32)
+    lines.append(jnp.concatenate([bqv[...].astype(F32), lack], axis=1))
+    lines.append(jnp.zeros((VEC_COLS - len(vecs) - 2, rows), F32))
+    cols = jnp.concatenate(lines, axis=0)
+    lack = -rows % 128
+    if lack:
+        cols = jnp.concatenate([cols, jnp.zeros((VEC_COLS, lack), F32)], axis=1)
+    cols = cols.T[:rows].astype(LOW)
+    first[...] = jnp.concatenate([cols, wqkv[0], wqkv[1], wqkv[2], turned(wout[...])], axis=1)
+    second[...] = jnp.concatenate([wfc[...], wproj[...]], axis=1)
 
 
 def open_first_body(size, scal, *refs):
     pieces, (sel, wqkv, wo, rows, bias, cols) = refs[:size], refs[size:]
     chunk = pieces[0].shape[0]
     split = VEC_COLS + wqkv.shape[1]
+    end = split + wo.shape[1]
     for step, piece in enumerate(pieces):
         place = pl.ds(row_start(scal[0], step, chunk) if size > 1 else 0, chunk)
-        value = piece[...]
+        value = piece[:, :end]
         cols[place, :] = value[:, :VEC_COLS].astype(F32)
         wqkv[place, :] = value[:, VEC_COLS:split]
         wo[place, :] = value[:, split:]
     wide = cols[...].T
     rows[...] = wide[:8]
-    bias[...] = dot(wide[:8].astype(LOW), sel[...], 1, 0)
+    spread = dot(wide[:16].astype(LOW), sel[...], 1, 0)
+    col = lax.broadcasted_iota(jnp.int32, (8, bias.shape[1]), 1)
+    count = wo.shape[1]
+    bias[...] = jnp.where(col < count, spread[7:8], jnp.where(col >= 2 * count, spread[8:9], 0.0))
 
 
 def open_second_body(size, scal, *refs):
     pieces, (grad, wf, wp, da, cot) = refs[:size], refs[size:]
-    chunk = pieces[0].shape[0]
+    chunk = pieces[-1].shape[0]
     cols = wf.shape[1]
     own = cot.shape[0] // 4
     for step, piece in enumerate(pieces):
@@ -161,15 +184,14 @@
 
 
 def attend_body(
-    own, near, pair, wqkv, bias, rows, doc_col, doc_row, pos_col, pos_row,
+    tok0, tok1, tok2, tok3, wqkv, bias, rows, doc_col, doc_row, pos_col, pos_row,
     qkv, mixed, lse, normed, mask,
 ):
     total = qkv.shape[0]
-    part = own.shape[0]
+    part = tok0.shape[0]
     gain, shift = rows[2:3, :], rows[3:4, :]
-    sources = (own[...], near[...], pair[:part, :], pair[part:, :])
-    for number, source in enumerate(sources):
-        scaled, _ = norm_parts(source.astype(F32))
+    for number, source in enumerate((tok0, tok1, tok2, tok3)):
+        scaled, _ = norm_parts(source[...].astype(F32))
         normed[number * part : (number + 1) * part, :] = (scaled * gain + shift).astype(LOW)
     qkv[...] = (dot(normed[...], wqkv[...], 1, 0) + bias[7:8, :]).astype(LOW)
     fill_mask(mask, doc_col, doc_row, pos_col, pos_row)
@@ -197,28 +219,19 @@
 
 
 def feed_body(
-    own, near, pair, mixed_own, mixed_near, mixed_pair, wo_own, wo_near, wo_pair, wf, rows, da,
+    tok0, tok1, tok2, tok3, mixed0, mixed1, mixed2, mixed3, wo0, wo1, wo2, wo3, wf, rows, da,
     keep, send, middle, normed, active, grad_hidden,
 ):
-    part = own.shape[0]
+    part = tok0.shape[0]
     half = 2 * part
-    head_cols = mixed_own.shape[1]
+    toks = (tok0, tok1, tok2, tok3)
     for number in range(2):
         here = slice(number * half, (number + 1) * half)
-        if number == 0:
-            source = jnp.concatenate([own[...], near[...]], axis=0)
-            swapped = slice(half, 2 * half)
-        else:
-            source = pair[...]
-            swapped = slice(0, half)
-        low = number * half
-        across = jnp.concatenate(
-            [mixed_near[low + part : low + half, :], mixed_near[low : low + part, :]], axis=0
-        )
+        source = jnp.concatenate([toks[2 * number][...], toks[2 * number + 1][...]], axis=0)
         total = source.astype(F32) + rows[0:1, :]
-        total += dot(mixed_own[here, :], wo_own[...], 1, 1)
-        total += dot(across, wo_near[...], 1, 1)
-        total += dot(mixed_pair[swapped, :], wo_pair[...], 1, 1)
+        for peer, (found, weight) in enumerate(((mixed0, wo0), (mixed1, wo1), (mixed2, wo2), (mixed3, wo3))):
+            blocks = [found[(b ^ peer) * part : (b ^ peer) * part + part, :] for b in (2 * number, 2 * number + 1)]
+            total += dot(jnp.concatenate(blocks, axis=0), weight[...], 1, 1)
         if number == 0:
             middle[...] = total
         scaled, _ = norm_parts(total)
@@ -241,25 +254,29 @@
             send[...] = back.astype(LOW)
 
 
-def put_pieces(me, whole, outs):
-    size = len(outs)
-    if size == 1:
-        outs[0][...] = whole[...]
-        return
+def put_pieces(me, outs, parts):
     chunk = outs[0].shape[0]
     for step, out in enumerate(outs):
-        value = whole[pl.ds(row_start(me, step, chunk), chunk), :]
-        out[...] = value.astype(out.dtype)
-
-
-def feed_grad_body(size, scal, active, wp, normed, grad_hidden, cot, *refs):
+        place = pl.ds(row_start(me, step, chunk), chunk) if len(outs) > 1 else slice(None)
+        low = 0
+        for part in parts:
+            high = low + part.shape[1]
+            out[:, low:high] = part[place, :].astype(out.dtype)
+            low = high
+
+
+def piece_shapes(parts, width, cols):
+    return [shape(width // parts, cols, LOW if step else F32) for step in range(parts)]
+
+
+def feed_grad_body(scal, active, wp, normed, grad_hidden, cot, *refs):
     keep, send, fc_sum = refs[:3]
-    pieces, whole = refs[3 : 3 + size], refs[3 + size]
+    pieces, whole = refs[3:-1], refs[-1]
     half = keep.shape[0]
     cols = wp.shape[1]
     whole[:, :cols] = dot(normed[...], grad_hidden[...], 0, 0)
     whole[:, cols:] = dot(cot[...], active[...], 0, 0)
-    put_pieces(scal[0], whole, pieces)
+    put_pieces(scal[0], pieces, [whole])
     keep[...] = dot(active[:half, :], wp[...], 1, 1)
     send[...] = dot(active[half:, :], wp[...], 1, 1).astype(LOW)
     fc_sum[...] = jnp.sum(grad_hidden[...].astype(F32), axis=0, keepdims=True)
@@ -283,12 +300,12 @@
 
 
 def attend_back_body(
-    grad_half, grad_other, wo, wqkv, qkv, lse, own, near, pair, early, doc_col, doc_row, pos_col, pos_row,
+    grad_half, grad_other, wo, wqkv, qkv, lse, tok0, tok1, tok2, tok3, early, doc_col, doc_row, pos_col, pos_row,
     keep, send, grad_qkv, late, qkv_sum, mask,
 ):
     total = qkv.shape[0]
     half = total // 2
-    part = own.shape[0]
+    toks = (tok0, tok1, tok2, tok3)
     width = qkv.shape[1] // 3
     heads = width // HEAD_DIM
     fill_mask(mask, doc_col, doc_row, pos_col, pos_row)
@@ -325,7 +342,7 @@
     for number in range(2):
         here = slice(number * half, (number + 1) * half)
         back = dot(grad_qkv[here, :], wqkv[...], 1, 1)
-        source = jnp.concatenate([own[...], near[...]], axis=0) if number == 0 else pair[...]
+        source = jnp.concatenate([toks[2 * number][...], toks[2 * number + 1][...]], axis=0)
         scaled, _ = norm_parts(source.astype(F32))
         gain_sum += jnp.sum(back * scaled, axis=0, keepdims=True)
         shift_sum += jnp.sum(back, axis=0, keepdims=True)
@@ -339,32 +356,34 @@
 
 
 def last_grad_body(
-    size, scal, grad_half, grad_other, mixed, own, near, pair, rows, grad_qkv, late, fc_sum, qkv_sum, sel, *refs
+    grad_half, grad_other, mixed, tok0, tok1, tok2, tok3, rows, grad_qkv, fc_sum, qkv_sum, sel, whole, lines, normed
 ):
-    pieces, (whole, normed) = refs[:size], refs[size:]
-    part = own.shape[0]
+    part = tok0.shape[0]
     half = 2 * part
-    sources = (own[...], near[...], pair[:part, :], pair[part:, :])
-    for number, source in enumerate(sources):
-        scaled, _ = norm_parts(source.astype(F32))
+    for number, source in enumerate((tok0, tok1, tok2, tok3)):
+        scaled, _ = norm_parts(source[...].astype(F32))
         normed[number * part : (number + 1) * part, :] = (scaled * rows[2:3, :] + rows[3:4, :]).astype(LOW)
-    qkv_cols = grad_qkv.shape[1]
-    split = VEC_COLS + qkv_cols
+    split = grad_qkv.shape[1]
+    whole[:, :split] = dot(normed[...], grad_qkv[...], 0, 0)
+    whole[:, split:] = dot(grad_half[...], mixed[:half, :], 0, 0) + dot(grad_other[...], mixed[half:, :], 0, 0)
+    count = qkv_sum.shape[1] // 3
+    col = lax.broadcasted_iota(jnp.int32, qkv_sum.shape, 1)
+    line = lax.broadcasted_iota(jnp.int32, qkv_sum.shape, 0)
+    sums = qkv_sum[0:1, :]
+    sums = jnp.where((line == 0) & (col < count) | (line == 1) & (col >= 2 * count), sums, 0.0)
     placed = lax.dot_general(
-        qkv_sum[...], sel[...].astype(F32), (((1,), (1,)), ((), ())),
+        sums, sel[...].astype(F32), (((1,), (1,)), ((), ())),
         preferred_element_type=F32, precision=lax.Precision.HIGHEST,
     )
-    line = jnp.concatenate([late[:6, :], fc_sum[...], placed[:1]], axis=0)
-    lack = jnp.zeros((VEC_COLS - 8, line.shape[1]), F32)
-    whole[:, :VEC_COLS] = jnp.concatenate([line, lack], axis=0).T
-    whole[:, VEC_COLS:] = jnp.concatenate(
-        [
-            dot(normed[...], grad_qkv[...], 0, 0),
-            dot(grad_half[...], mixed[:half, :], 0, 0) + dot(grad_other[...], mixed[half:, :], 0, 0),
-        ],
-        axis=1,
-    )
-    put_pieces(scal[0], whole, pieces)
+    lines[...] = jnp.concatenate([fc_sum[...], placed[:7]], axis=0)
+
+
+def last_cut_body(scal, whole, late, lines, *refs):
+    pieces, cols = refs[:-1], refs[-1]
+    line = jnp.concatenate([late[:6, :], lines[:3, :]], axis=0)
+    lack = jnp.zeros((VEC_COLS - line.shape[0], line.shape[1]), F32)
+    cols[...] = jnp.concatenate([line, lack], axis=0).T
+    put_pieces(scal[0], pieces, [cols, whole])
 
 
 def input_body(keep, far, middle_grad, own, rows, out):
@@ -374,30 +393,30 @@
     out[...] = middle_grad[...] + norm_back(grad, scaled, inverse, rows[2:3, :])
 
 
-def total_of(refs):
+def total_of(*refs):
     total = refs[0][...]
     for ref in refs[1:]:
         total = total + ref[...].astype(F32)
     return total
 
 
-def sum_feed_body(size, *refs):
-    total = total_of(refs[:size])
-    wfc, wproj = refs[size:]
+def sum_feed_body(*refs):
+    total = total_of(*refs[:4])
+    wfc, wproj = refs[4:]
     cols = wfc.shape[1]
     wfc[...] = total[:, :cols]
-    wproj[...] = turned_wide(total[:, cols:])
-
-
-def sum_last_body(size, *refs):
-    total = total_of(refs[:size])
-    wqkv, wout, vecs = refs[size:]
+    wproj[...] = total[:, cols:]
+
+
+def sum_last_body(*refs):
+    total = total_of(*refs[:4])
+    wqkv, wout, vecs = refs[4:]
     width = wout.shape[0]
     for number in range(3):
         low = VEC_COLS + number * width
         wqkv[number] = total[:, low : low + width]
     wout[...] = turned_wide(total[:, VEC_COLS + 3 * width :])
-    vecs[...] = turned_wide(total[:, :VEC_COLS])[:8]
+    vecs[...] = turned_wide(total[:, :VEC_COLS])[:16]
 
 
 def local(
@@ -432,31 +451,32 @@
     parts = size if direct else 1
 
     near = swap(tokens, "tensor")
-    pair = swap(jnp.concatenate([tokens, near]), "seq")
-
-    flat_qv = jnp.pad(b_qv.reshape(-1), (0, chunk - 2 * qv_count))
-    vecs = jnp.stack([b_out, b_proj, ln1_gain, ln1_bias, ln2_gain, ln2_bias, b_fc, flat_qv])
+    toks = [tokens, near, swap(tokens, "seq"), swap(near, "seq")]
+
+    vecs = [b_out, b_proj, ln1_gain, ln1_bias, ln2_gain, ln2_bias, b_fc]
     col = np.arange(qkv_cols)
     inner = col % head_cols
-    source = (inner // qv_count) * chunk + inner % qv_count + qv_count * (col >= 2 * head_cols)
-    used = (col < head_cols) | (col >= 2 * head_cols)
+    source = (inner // qv_count) * chunk + inner % qv_count
     row_number = lax.broadcasted_iota(jnp.int32, (width, qkv_cols), 0)
-    sel = (row_number == jnp.asarray(np.where(used, source, -1), jnp.int32)[None, :]).astype(LOW)
+    sel = (row_number == jnp.asarray(source, jnp.int32)[None, :]).astype(LOW)
 
     rows_shape = shape(8, width, F32)
     bias_shape = shape(8, qkv_cols, F32)
     wqkv_shape, wo_shape = shape(width, qkv_cols, LOW), shape(width, head_cols, LOW)
     if direct:
-        (first,) = on_core(
-            pack_first_body, [shape(chunk, VEC_COLS + qkv_cols + head_cols, LOW)], [], [w_qkv, w_out, vecs]
+        first, second = on_core(
+            pack_body,
+            [shape(chunk, VEC_COLS + qkv_cols + head_cols, LOW), shape(chunk, 2 * hidden_cols, LOW)],
+            [],
+            [w_qkv, w_out, w_fc, w_proj.T, b_qv, *vecs],
+            limit=62,
         )
-        (second,) = on_core(pack_second_body, [shape(chunk, 2 * hidden_cols, LOW)], [], [w_fc, w_proj])
-        firsts = pieces_of(first)
-        second = after(second, *firsts[1:6])
-        seconds = pieces_of(second)
+        firsts = pieces_ring_first(first)
+        seconds = pieces_mixed(second, firsts[6], [firsts[2], firsts[4]])
     else:
-        lack = jnp.zeros((chunk, VEC_COLS - 8), LOW)
-        first = jnp.concatenate([vecs.T, lack, w_qkv[0], w_qkv[1], w_qkv[2], w_out.T], axis=1)
+        lines = jnp.stack([*vecs, *jnp.pad(b_qv, ((0, 0), (0, chunk - qv_count)))])
+        lack = jnp.zeros((chunk, VEC_COLS - lines.shape[0]), LOW)
+        first = jnp.concatenate([lines.T, lack, w_qkv[0], w_qkv[1], w_qkv[2], w_out.T], axis=1)
         second = jnp.concatenate([w_fc, w_proj.T], axis=1)
         firsts = [lax.all_gather(first, "fsdp", axis=0, tiled=True)]
         seconds = [lax.all_gather(second, "fsdp", axis=0, tiled=True)]
@@ -469,7 +489,7 @@
         [pltpu.VMEM((width, VEC_COLS), F32)],
     )
     wo_near = swap(wo, "tensor")
-    wo_pair = swap(jnp.concatenate([wo, wo_near], axis=1), "seq")
+    wos = [wo, wo_near, swap(wo, "seq"), swap(wo_near, "seq")]
 
     blocks = [place ^ b for b in range(4)]
     docs = jnp.concatenate([lax.dynamic_slice_in_dim(segments, b * own_rows, own_rows, 0) for b in blocks])
@@ -482,13 +502,12 @@
         attend_body,
         [shape(seq_rows, qkv_cols, LOW), shape(seq_rows, head_cols, LOW), shape(seq_rows, 128, F32)],
         [],
-        [tokens, near, pair, wqkv, bias, rows, *marks],
+        [*toks, wqkv, bias, rows, *marks],
         [normed_scratch, mask_scratch],
         flops=2 * seq_rows * (width * qkv_cols + 2 * head_cols * seq_rows),
     )
     mixed_near = swap(mixed, "tensor")
-    crossed = mixed_near.reshape(2, 2, own_rows, head_cols)[:, ::-1].reshape(seq_rows, head_cols)
-    mixed_pair = swap(jnp.concatenate([mixed, crossed], axis=1), "seq")
+    mixeds = [mixed, mixed_near, swap(mixed, "seq"), swap(mixed_near, "seq")]
 
     square = 2 * seq_rows * width * hidden_cols
     wf, wp, da, cot = on_core(
@@ -514,23 +533,28 @@
             shape(seq_rows, hidden_cols, LOW),
         ],
         [],
-        [tokens, near, pair, mixed, mixed_near, mixed_pair, wo, wo_near, wo_pair, wf, rows, da],
+        [*toks, *mixeds, *wos, wf, rows, da],
         flops=3 * square,
     )
     part_two = keep + swap(send, "seq").astype(F32)
     far = swap(part_two.astype(LOW), "tensor")
 
     piece_cols = 2 * hidden_cols
-    ff_pieces = [shape(width // parts, piece_cols, F32 if step == 0 else LOW) for step in range(parts)]
     out_keep, out_send, fc_sum, *grad_ff = on_core(
-        functools.partial(feed_grad_body, parts),
-        [shape(half, width, F32), shape(half, width, LOW), shape(1, hidden_cols, F32), *ff_pieces],
+        feed_grad_body,
+        [shape(half, width, F32), shape(half, width, LOW), shape(1, hidden_cols, F32), *piece_shapes(parts, width, piece_cols)],
         [scal],
-        [active, wp, normed_two, grad_hidden, cot],
+        [active, wp, normed_two, grad_hidden, after(cot, part_two)],
         [pltpu.VMEM((width, piece_cols), F32)],
         flops=3 * square,
     )
-    far = after(far, fc_sum)
+    out_half = out_keep + swap(out_send, "seq").astype(F32)
+    out_far = swap(out_half[own_rows:].astype(LOW), "tensor")
+    result = (middle[:own_rows] + out_half[:own_rows] + out_far.astype(F32) + rows[1:2]).astype(LOW)
+    far = after(far, fc_sum, out_half)
+    if direct:
+        crossed = over_pair(grad_ff)
+        far = after(far, crossed[0])
     grad_mid_half, grad_mid_own, early = on_core(
         middle_body,
         [shape(half, width, LOW), shape(own_rows, width, F32), rows_shape],
@@ -539,6 +563,9 @@
     )
     grad_mid_other = swap(grad_mid_half, "seq")
 
+    if direct:
+        grad_mid_other = after(grad_mid_other, crossed[1])
+        got_ff = round_ring(grad_ff, crossed)
     keep_one, send_one, grad_qkv, late, qkv_sum = on_core(
         attend_back_body,
         [
@@ -549,7 +576,7 @@
             bias_shape,
         ],
         [],
-        [grad_mid_half, grad_mid_other, wo, wqkv, qkv, lse, tokens, near, pair, early, *marks],
+        [grad_mid_half, grad_mid_other, wo, wqkv, qkv, lse, *toks, early, *marks],
         [mask_scratch],
         flops=2 * seq_rows * (width * (qkv_cols + head_cols) + 5 * head_cols * seq_rows),
     )
@@ -564,35 +591,40 @@
         [part_one, far_one, grad_mid_own, tokens, rows],
     )
 
-    out_half = out_keep + swap(after(out_send, grad_qkv), "seq").astype(F32)
-    out_own = out_half[:own_rows] + swap(out_half[own_rows:].astype(LOW), "tensor").astype(F32)
-    result = (middle[:own_rows] + out_own + rows[1:2]).astype(LOW)
-
     last_cols = VEC_COLS + qkv_cols + head_cols
-    last_pieces = [shape(width // parts, last_cols, F32 if step == 0 else LOW) for step in range(parts)]
+    whole, lines = on_core(
+        last_grad_body,
+        [shape(width, qkv_cols + head_cols, F32), rows_shape],
+        [],
+        [grad_mid_half, grad_mid_other, mixed, *toks, rows, grad_qkv, fc_sum, qkv_sum, sel],
+        [normed_scratch],
+        flops=2 * seq_rows * width * (qkv_cols + head_cols),
+    )
+    late = after(late, part_one)
+    if direct:
+        late = after(late, *crossed)
     grad_last = on_core(
-        functools.partial(last_grad_body, parts),
-        last_pieces,
+        last_cut_body,
+        piece_shapes(parts, width, last_cols),
         [scal],
-        [
-            grad_mid_half, grad_mid_other, mixed, tokens, near, pair, rows, grad_qkv, late, fc_sum, qkv_sum, sel,
-        ],
-        [pltpu.VMEM((width, last_cols), F32), normed_scratch],
-        flops=2 * seq_rows * width * (qkv_cols + head_cols),
+        [whole, late, lines],
+        [pltpu.VMEM((width, VEC_COLS), F32)],
     )
 
     if direct:
-        got_ff = sums_of(grad_ff)
-        got_last = sums_of(grad_last)
+        crossed = over_pair(grad_last)
+        crossed[2] = after(crossed[2], far_one, out_far)
+        got_last = round_ring(grad_last, crossed)
         grad_wfc, grad_wproj = on_core(
-            functools.partial(sum_feed_body, len(got_ff)),
-            [shape(chunk, hidden_cols, F32), shape(hidden_cols, chunk, F32)],
+            sum_feed_body,
+            [shape(chunk, hidden_cols, F32)] * 2,
             [],
             got_ff,
         )
+        grad_wproj = grad_wproj.T
         grad_wqkv, grad_wout, sums = on_core(
-            functools.partial(sum_last_body, len(got_last)),
-            [jax.ShapeDtypeStruct((3, chunk, head_cols), F32), shape(head_cols, chunk, F32), shape(8, chunk, F32)],
+            sum_last_body,
+            [jax.ShapeDtypeStruct((3, chunk, head_cols), F32), shape(head_cols, chunk, F32), shape(16, chunk, F32)],
             [],
             got_last,
         )
@@ -603,7 +635,7 @@
         split = VEC_COLS + qkv_cols
         grad_wqkv = sum_last[:, VEC_COLS:split].reshape(chunk, 3, head_cols).transpose(1, 0, 2)
         grad_wout = sum_last[:, split:].T
-        sums = sum_last[:, :8].T
+        sums = sum_last[:, :16].T
 
     return (
         result,
@@ -612,7 +644,7 @@
         grad_wout,
         grad_wfc,
         grad_wproj,
-        sums[7, : 2 * qv_count].reshape(2, qv_count),
+        sums[7:9, :qv_count],
         sums[0],
         sums[6],
         sums[1],

time: 196 us -> 144 us (0.73)
  waiting for transfers between devices: 74.6 us -> 49 us
  local copies, waits for them, and re-layouts: 16.9 us -> 8.05 us
  other arithmetic: 9.8 us -> 2.53 us
  starting transfers between devices: 58.1 us -> 52.1 us
  Pallas kernels: 35.2 us -> 31.4 us
    ppermute x28, waiting for transfers between devices: 63.6 us -> 34.3 us  [send(): return lax.ppermute(value, 'fsdp', pairs)]
    unnamed x52 -> x20, local copies, waits for them, and re-layouts: 12.1 us -> 5.69 us
    ppermute x28, starting transfers between devices: 49.3 us -> 43.4 us  [send(): return lax.ppermute(value, 'fsdp', pairs)]
    concatenate x3 -> x0, other arithmetic: 3.97 us -> none  [the longest x1 2.03 us: local(): wo_pair = swap(jnp.concatenate([wo, wo_near], axis=1), 'seq')]
    pallas_call x13, Pallas kernels: 35.2 us -> 31.4 us  [on_core(): pl.pallas_call(body, out_shape=tuple(outs), in_specs=specs, out_specs=tup...]
    ppermute x15 -> x18, waiting for transfers between devices: 11 us -> 14.8 us  [swap(): return lax.ppermute(value, axis, [(0, 1), (1, 0)])]
    ppermute x15 -> x18, starting transfers between devices: 8.82 us -> 8.69 us  [swap(): return lax.ppermute(value, axis, [(0, 1), (1, 0)])]
  transfers between devices with their start and end apart: 43 -> 46, of which waited for: 20 -> 19; matrix products, arithmetic and copies ran while one was open for 7% -> 3% of each run, Pallas kernels for 14% -> 14%
where the time goes in v3:
time: 144 us
  starting transfers between devices  52.1 us (36%)
  waiting for transfers between devices  49 us (34%)
  Pallas kernels  31.4 us (22%)
  local copies, waits for them, and re-layouts  8.05 us (6%)
  other arithmetic  2.53 us (2%)
    ppermute x28, starting transfers between devices, send(): return lax.ppermute(value, 'fsdp', pairs)  43.4 us
    ppermute x28, waiting for transfers between devices, send(): return lax.ppermute(value, 'fsdp', pairs)  34.3 us
    pallas_call x13, Pallas kernels, on_core(): pl.pallas_call(body, out_shape=tuple(outs), in_specs=specs, out_specs=tup...  31.4 us
    ppermute x18, waiting for transfers between devices, swap(): return lax.ppermute(value, axis, [(0, 1), (1, 0)])  14.8 us
    ppermute x18, starting transfers between devices, swap(): return lax.ppermute(value, axis, [(0, 1), (1, 0)])  8.69 us
    unnamed x20, local copies, waits for them, and re-layouts  5.69 us
  transfers between devices with their start and end apart: 46, of which 19 were waited for; matrix products, arithmetic and copies ran while one was open for 3% of the time, Pallas kernels for 14%

profile of v3, /device:TPU:0, one launch (start us, length us, event | category | flops | bytes accessed | tf_op | source)
XLA Modules:
  0.0 144.1 jit_solution(8186741561482087349)
XLA Ops:
  0.6 2.1 %shard_map.263 = (bf16[96,896]{1,0:T(8,128)(2,1)}, bf16[96,1536]{1,0:T(8,128)(2,1)}) custom-call(bf16[3,96,192]{2,1,0:T(8,128)(2,1)} %wqkv.1, bf16[192,96]{1,0:T(8,128)(2,1)} %wout.1, bf16[96,768]{1,0:T(8,128)(2,1)} %wfc.1, bf16[96,768]{1,0:T(8,128)(2,1)} %bitcast.28, bf16[2,24]{1,0:T(2,128)(2,1)} %bqv.1, bf16[96]{0:T(256)(128)(2,1)} %refs_0_.1, ...), custom_call_target="tpu_custom_call" | custom-call | bytes 910752 | tf_op jit(solution)/shard_map/pallas_call | solution.py:30
  2.8 5.0 %collective-permute-start.3 = (bf16[96,896]{1,0:T(8,128)(2,1)}, bf16[96,896]{1,0:T(8,128)(2,1)S(1)}, u32[]{:S(2)}, u32[]{:S(2)}) collective-permute-start(bf16[96,896]{1,0:T(8,128)(2,1)} %get-tuple-element.76.refs_0_), channel_id=1, source_target_pairs={{0,24},{4,28},{8,0},{12,4},{16,8},{20,12},{24,16},{28,20},{1,25},{... | collective-permute-start | bytes 516104 | tf_op jit(solution)/shard_map/ppermute | solution.py:82
  12.9 4.2 %collective-permute-start.8 = (bf16[96,896]{1,0:T(8,128)(2,1)S(1)}, bf16[96,896]{1,0:T(8,128)(2,1)S(1)}, u32[]{:S(2)}, u32[]{:S(2)}) collective-permute-start(bf16[96,896]{1,0:T(8,128)(2,1)S(1)} %collective-permute-done.3.refs_1_), channel_id=1, source_target_pairs={{0,24},{4,28},{8,0},{12,4},{16,8},{20,12},{24,16},{28,20},{1,25},{... | collective-permute-start | bytes 516104 | tf_op jit(solution)/shard_map/ppermute | solution.py:82
  20.1 4.2 %collective-permute-start.16 = (bf16[96,1536]{1,0:T(8,128)(2,1)}, bf16[96,1536]{1,0:T(8,128)(2,1)}, u32[]{:S(2)}, u32[]{:S(2)}) collective-permute-start(bf16[96,1536]{1,0:T(8,128)(2,1)} %get-tuple-element.84.refs_0_), channel_id=1, source_target_pairs={{0,24},{4,28},{8,0},{12,4},{16,8},{20,12},{24,16},{28,20},{1,25},{... | collective-permute-start | bytes 884744 | tf_op jit(solution)/shard_map/ppermute | solution.py:82
  27.8 2.6 %collective-permute-done.9.refs_7_ = bf16[96,896]{1,0:T(8,128)(2,1)S(1)} collective-permute-done((bf16[96,896]{1,0:T(8,128)(2,1)S(1)}, bf16[96,896]{1,0:T(8,128)(2,1)S(1)}, u32[]{:S(2)}, u32[]{:S(2)}) %collective-permute-start.9) | collective-permute-done | bytes 172064 | tf_op jit(solution)/shard_map/ppermute | solution.py:82
  34.8 1.8 %shard_map.264 = (bf16[768,576]{1,0:T(8,128)(2,1)S(1)}, bf16[768,192]{1,0:T(8,128)(2,1)}, f32[8,768]{1,0:T(8,128)S(1)}, f32[8,576]{1,0:T(8,128)S(1)}) custom-call(s32[2]{0:T(128)S(1)} %pad_add_fusion.2.scal, bf16[96,896]{1,0:T(8,128)(2,1)S(1)} %copy-done.3, bf16[96,896]{1,0:T(8,128)(2,1)S(1)} %collective-permute-done.3.refs_1_, ...), custom_call_target="tpu_custom_call" | custom-call | bytes 3483648 | tf_op jit(solution)/shard_map/pallas_call | solution.py:30
  39.6 3.9 %shard_map.265 = (bf16[512,576]{1,0:T(8,128)(2,1)S(1)}, bf16[512,192]{1,0:T(8,128)(2,1)S(1)}, f32[512,128]{1,0:T(8,128)S(1)}) custom-call(bf16[128,768]{1,0:T(8,128)(2,1)S(1)} %copy-done, bf16[128,768]{1,0:T(8,128)(2,1)S(1)} %collective-permute-done.tok1, bf16[128,768]{1,0:T(8,128)(2,1)S(1)} %collective-permute-done.1.tok2, ...), custom_call_target="tpu_custom_call" | custom-call | flops 654311424 | bytes 2770944 | tf_op jit(solution)/shard_map/pallas_call | solution.py:30
  45.0 2.3 %collective-permute-start.20 = (bf16[96,1536]{1,0:T(8,128)(2,1)}, bf16[96,1536]{1,0:T(8,128)(2,1)S(1)}, u32[]{:S(2)}, u32[]{:S(2)}) collective-permute-start(bf16[96,1536]{1,0:T(8,128)(2,1)} %collective-permute-done.16.refs_1_), channel_id=1, source_target_pairs={{0,4},{4,0},{8,12},{12,8},{16,20},{20,16},{24,28},{28,24},{1,5},{5... | collective-permute-start | bytes 884744 | tf_op jit(solution)/shard_map/ppermute | solution.py:82
  47.5 2.3 %collective-permute-start.22 = (bf16[96,1536]{1,0:T(8,128)(2,1)}, bf16[96,1536]{1,0:T(8,128)(2,1)S(1)}, u32[]{:S(2)}, u32[]{:S(2)}) collective-permute-start(bf16[96,1536]{1,0:T(8,128)(2,1)} %collective-permute-done.21.refs_6_), channel_id=1, source_target_pairs={{0,4},{4,0},{8,12},{12,8},{16,20},{20,16},{24,28},{28,24},{1,5},{5... | collective-permute-start | bytes 884744 | tf_op jit(solution)/shard_map/ppermute | solution.py:82
  49.8 4.1 %collective-permute-done.10.mixed1 = bf16[512,192]{1,0:T(8,128)(2,1)S(1)} collective-permute-done((bf16[512,192]{1,0:T(8,128)(2,1)S(1)}, bf16[512,192]{1,0:T(8,128)(2,1)S(1)}, u32[]{:S(2)}, u32[]{:S(2)}) %collective-permute-start.10) | collective-permute-done | bytes 196640 | tf_op jit(solution)/shard_map/ppermute | solution.py:77
  55.4 5.0 %collective-permute-done.22.refs_7_ = bf16[96,1536]{1,0:T(8,128)(2,1)S(1)} collective-permute-done((bf16[96,1536]{1,0:T(8,128)(2,1)}, bf16[96,1536]{1,0:T(8,128)(2,1)S(1)}, u32[]{:S(2)}, u32[]{:S(2)}) %collective-permute-start.22) | collective-permute-done | bytes 294944 | tf_op jit(solution)/shard_map/ppermute | solution.py:82
  60.4 2.2 %shard_map.266 = (bf16[768,768]{1,0:T(8,128)(2,1)S(1)}, bf16[768,768]{1,0:T(8,128)(2,1)S(1)}, f32[512,768]{1,0:T(8,128)S(1)}, bf16[512,768]{1,0:T(8,128)(2,1)S(1)}) custom-call(s32[2]{0:T(128)S(1)} %pad_add_fusion.2.scal, bf16[96,1536]{1,0:T(8,128)(2,1)S(1)} %copy-done.2, bf16[96,1536]{1,0:T(8,128)(2,1)} %collective-permute-done.16.refs_1_, ...), custom_call_target="tpu_custom_call" | custom-call | flops 603979776 | bytes 7864320 | tf_op jit(solution)/shard_map/pallas_call | solution.py:30
  62.6 5.4 %shard_map.267 = (f32[256,768]{1,0:T(8,128)S(1)}, bf16[256,768]{1,0:T(8,128)(2,1)S(1)}, f32[256,768]{1,0:T(8,128)S(1)}, bf16[512,768]{1,0:T(8,128)(2,1)S(1)}, bf...) custom-call(bf16[128,768]{1,0:T(8,128)(2,1)S(1)} %copy-done, bf16[128,768]{1,0:T(8,128)(2,1)S(1)} %collective-permute-done.tok1, ...), custom_call_target="tpu_custom_call" | custom-call | flops 1811939328 | bytes 9854976 | tf_op jit(solution)/shard_map/pallas_call | solution.py:30
  70.0 2.8 %shard_map.268 = (f32[256,768]{1,0:T(8,128)S(1)}, bf16[256,768]{1,0:T(8,128)(2,1)S(1)}, f32[1,768]{1,0:T(1,128)S(1)}, f32[96,1536]{1,0:T(8,128)S(1)}, bf16[96,15...) custom-call(s32[2]{0:T(128)S(1)} %pad_add_fusion.2.scal, ...), custom_call_target="tpu_custom_call" | custom-call | flops 1811939328 | bytes 8162304 | tf_op jit(solution)/shard_map/pallas_call | solution.py:30
  74.5 1.7 %collective-permute-start.34 = (bf16[96,1536]{1,0:T(8,128)(2,1)S(1)}, bf16[96,1536]{1,0:T(8,128)(2,1)S(1)}, u32[]{:S(2)}, u32[]{:S(2)}) collective-permute-start(bf16[96,1536]{1,0:T(8,128)(2,1)S(1)} %get-tuple-element.116), channel_id=1, source_target_pairs={{0,4},{4,0},{8,12},{12,8},{16,20},{20,16},{24,28},{28,24},{1,5},{5... | collective-permute-start | bytes 884744 | tf_op jit(solution)/shard_map/ppermute | solution.py:82
  76.6 1.8 %collective-permute-start.29 = (bf16[96,1536]{1,0:T(8,128)(2,1)S(1)}, bf16[96,1536]{1,0:T(8,128)(2,1)S(1)}, u32[]{:S(2)}, u32[]{:S(2)}) collective-permute-start(bf16[96,1536]{1,0:T(8,128)(2,1)S(1)} %get-tuple-element.103), channel_id=1, source_target_pairs={{0,4},{4,0},{8,12},{12,8},{16,20},{20,16},{24,28},{28,24},{1,5},{5... | collective-permute-start | bytes 884744 | tf_op jit(solution)/shard_map/ppermute | solution.py:82
  78.7 5.7 %collective-permute-done.26.far = bf16[256,768]{1,0:T(8,128)(2,1)S(1)} collective-permute-done((bf16[256,768]{1,0:T(8,128)(2,1)S(1)}, bf16[256,768]{1,0:T(8,128)(2,1)S(1)}, u32[]{:S(2)}, u32[]{:S(2)}) %collective-permute-start.26) | collective-permute-done | bytes 393248 | tf_op jit(solution)/shard_map/ppermute | solution.py:77
  84.4 6.3 %collective-permute-done.27 = bf16[96,1536]{1,0:T(8,128)(2,1)S(1)} collective-permute-done((bf16[96,1536]{1,0:T(8,128)(2,1)S(1)}, bf16[96,1536]{1,0:T(8,128)(2,1)S(1)}, u32[]{:S(2)}, u32[]{:S(2)}) %collective-permute-start.27) | collective-permute-done | bytes 294944 | tf_op jit(solution)/shard_map/ppermute | solution.py:82
  91.5 2.7 %collective-permute-start.45 = (bf16[96,1536]{1,0:T(8,128)(2,1)S(1)}, bf16[96,1536]{1,0:T(8,128)(2,1)S(1)}, u32[]{:S(2)}, u32[]{:S(2)}) collective-permute-start(bf16[96,1536]{1,0:T(8,128)(2,1)S(1)} %add_convert_fusion), channel_id=1, source_target_pairs={{0,24},{4,28},{8,0},{12,4},{16,8},{20,12},{24,16},{28,20},{1,25},{... | collective-permute-start | bytes 884744 | tf_op jit(solution)/shard_map/ppermute | solution.py:82
  94.2 2.8 %collective-permute-done.29 = bf16[96,1536]{1,0:T(8,128)(2,1)S(1)} collective-permute-done((bf16[96,1536]{1,0:T(8,128)(2,1)S(1)}, bf16[96,1536]{1,0:T(8,128)(2,1)S(1)}, u32[]{:S(2)}, u32[]{:S(2)}) %collective-permute-start.29) | collective-permute-done | bytes 294944 | tf_op jit(solution)/shard_map/ppermute | solution.py:82
  97.0 5.9 %shard_map.270 = (f32[256,768]{1,0:T(8,128)S(1)}, bf16[256,768]{1,0:T(8,128)(2,1)S(1)}, bf16[512,576]{1,0:T(8,128)(2,1)S(1)}, f32[8,768]{1,0:T(8,128)S(1)}, f32[8,576]{1,0:T(8,128)S(1)}) custom-call(bf16[256,768]{1,0:T(8,128)(2,1)S(1)} %get-tuple-element.102.grad_half, bf16[256,768]{1,0:T(8,128)(2,1)S(1)} %collective-permute-done.28.grad_other, ...), custom_call_target="tpu_custom_call" | custom-call | flops 1107296256 | bytes 5449728 | tf_op jit(solution)/shard_map/pallas_call | solution.py:30
  104.1 2.8 %collective-permute-done.32 = f32[8,768]{1,0:T(8,128)S(1)} collective-permute-done((f32[8,768]{1,0:T(8,128)S(1)}, f32[8,768]{1,0:T(8,128)S(1)}, u32[]{:S(2)}, u32[]{:S(2)}) %collective-permute-start.32) | collective-permute-done | bytes 24608 | tf_op jit(solution)/shard_map/ppermute | solution.py:77
  106.9 2.9 %shard_map.272 = (f32[768,768]{1,0:T(8,128)S(1)}, f32[8,768]{1,0:T(8,128)S(1)}) custom-call(bf16[256,768]{1,0:T(8,128)(2,1)S(1)} %get-tuple-element.102.grad_half, bf16[256,768]{1,0:T(8,128)(2,1)S(1)} %collective-permute-done.28.grad_other, bf16[512,192]{1,0:T(8,128)(2,1)S(1)} %get-tuple-element.80.mixed0.mixed, bf16[128,768]{1,0:T(8,128)(2,1)S(1)} %copy-done, ...), custom_call_target="tpu_custom_call" | custom-call | flops 603979776 | bytes 5673984 | tf_op jit(solution)/shard_map/pallas_call | solution.py:30
  111.3 1.8 %collective-permute-start.38 = (bf16[96,896]{1,0:T(8,128)(2,1)S(1)}, bf16[96,896]{1,0:T(8,128)(2,1)S(1)}, u32[]{:S(2)}, u32[]{:S(2)}) collective-permute-start(bf16[96,896]{1,0:T(8,128)(2,1)S(1)} %get-tuple-element.125), channel_id=1, source_target_pairs={{0,4},{4,0},{8,12},{12,8},{16,20},{20,16},{24,28},{28,24},{1,5},{5... | collective-permute-start | bytes 516104 | tf_op jit(solution)/shard_map/ppermute | solution.py:82
  113.1 1.9 %collective-permute-done.43 = bf16[96,1536]{1,0:T(8,128)(2,1)S(1)} collective-permute-done((bf16[96,1536]{1,0:T(8,128)(2,1)S(1)}, bf16[96,1536]{1,0:T(8,128)(2,1)S(1)}, u32[]{:S(2)}, u32[]{:S(2)}) %collective-permute-start.43) | collective-permute-done | bytes 294944 | tf_op jit(solution)/shard_map/ppermute | solution.py:82
  115.2 1.8 %collective-permute-start.41 = (bf16[96,896]{1,0:T(8,128)(2,1)S(1)}, bf16[96,896]{1,0:T(8,128)(2,1)S(1)}, u32[]{:S(2)}, u32[]{:S(2)}) collective-permute-start(bf16[96,896]{1,0:T(8,128)(2,1)S(1)} %get-tuple-element.127), channel_id=1, source_target_pairs={{0,4},{4,0},{8,12},{12,8},{16,20},{20,16},{24,28},{28,24},{1,5},{5... | collective-permute-start | bytes 516104 | tf_op jit(solution)/shard_map/ppermute | solution.py:82
  119.6 1.8 %collective-permute-start.37 = (bf16[96,896]{1,0:T(8,128)(2,1)S(1)}, bf16[96,896]{1,0:T(8,128)(2,1)S(1)}, u32[]{:S(2)}, u32[]{:S(2)}) collective-permute-start(bf16[96,896]{1,0:T(8,128)(2,1)S(1)} %get-tuple-element.123), channel_id=1, source_target_pairs={{0,4},{4,0},{8,12},{12,8},{16,20},{20,16},{24,28},{28,24},{1,5},{5... | collective-permute-start | bytes 516104 | tf_op jit(solution)/shard_map/ppermute | solution.py:82
  121.8 1.7 %collective-permute-start.36 = (bf16[96,896]{1,0:T(8,128)(2,1)S(1)}, bf16[96,896]{1,0:T(8,128)(2,1)S(1)}, u32[]{:S(2)}, u32[]{:S(2)}) collective-permute-start(bf16[96,896]{1,0:T(8,128)(2,1)S(1)} %get-tuple-element.121), channel_id=1, source_target_pairs={{0,4},{4,0},{8,12},{12,8},{16,20},{20,16},{24,28},{28,24},{1,5},{5... | collective-permute-start | bytes 516104 | tf_op jit(solution)/shard_map/ppermute | solution.py:82
  124.6 2.4 %collective-permute-done.37 = bf16[96,896]{1,0:T(8,128)(2,1)S(1)} collective-permute-done((bf16[96,896]{1,0:T(8,128)(2,1)S(1)}, bf16[96,896]{1,0:T(8,128)(2,1)S(1)}, u32[]{:S(2)}, u32[]{:S(2)}) %collective-permute-start.37) | collective-permute-done | bytes 172064 | tf_op jit(solution)/shard_map/ppermute | solution.py:82
  127.0 2.7 %collective-permute-start.42 = (bf16[96,896]{1,0:T(8,128)(2,1)S(1)}, bf16[96,896]{1,0:T(8,128)(2,1)S(1)}, u32[]{:S(2)}, u32[]{:S(2)}) collective-permute-start(bf16[96,896]{1,0:T(8,128)(2,1)S(1)} %add_convert_fusion.3), channel_id=1, source_target_pairs={{0,24},{4,28},{8,0},{12,4},{16,8},{20,12},{24,16},{28,20},{1,25},{... | collective-permute-start | bytes 516104 | tf_op jit(solution)/shard_map/ppermute | solution.py:82
  129.7 2.7 %collective-permute-done.39 = bf16[96,896]{1,0:T(8,128)(2,1)S(1)} collective-permute-done((bf16[96,896]{1,0:T(8,128)(2,1)S(1)}, bf16[96,896]{1,0:T(8,128)(2,1)S(1)}, u32[]{:S(2)}, u32[]{:S(2)}) %collective-permute-start.39) | collective-permute-done | bytes 172064 | tf_op jit(solution)/shard_map/ppermute | solution.py:82
  135.3 6.8 %collective-permute-done.40.refs_2_ = bf16[96,896]{1,0:T(8,128)(2,1)S(1)} collective-permute-done((bf16[96,896]{1,0:T(8,128)(2,1)S(1)}, bf16[96,896]{1,0:T(8,128)(2,1)S(1)}, u32[]{:S(2)}, u32[]{:S(2)}) %collective-permute-start.40) | collective-permute-done | bytes 172064 | tf_op jit(solution)/shard_map/ppermute | solution.py:82
  (119 shorter events, 38.9 us)
Async XLA Ops:
  2.8 10.1 %collective-permute-start.3 = (bf16[96,896]{1,0:T(8,128)(2,1)}, bf16[96,896]{1,0:T(8,128)(2,1)S(1)}, u32[]{:S(2)}, u32[]{:S(2)}) collective-permute-start(bf16[96,896]{1,0:T(8,128)(2,1)} %get-tuple-element.76.refs_0_), channel_id=1, source_target_pairs={{0,24},{4,28},{8,0},{12,4},{16,8},{20,12},{24,16},{28,20},{1,25},{... | collective-permute-start | bytes 516104 | tf_op jit(solution)/shard_map/ppermute | solution.py:82
  7.8 11.7 %collective-permute-start.4 = (bf16[96,896]{1,0:T(8,128)(2,1)}, bf16[96,896]{1,0:T(8,128)(2,1)S(1)}, u32[]{:S(2)}, u32[]{:S(2)}) collective-permute-start(bf16[96,896]{1,0:T(8,128)(2,1)} %get-tuple-element.76.refs_0_), channel_id=1, source_target_pairs={{0,8},{4,12},{8,16},{12,20},{16,24},{20,28},{24,0},{28,4},{1,9},{5... | collective-permute-start | bytes 516104 | tf_op jit(solution)/shard_map/ppermute | solution.py:82
  7.8 19.3 %collective-permute-start.7 = (bf16[96,896]{1,0:T(8,128)(2,1)}, bf16[96,896]{1,0:T(8,128)(2,1)S(1)}, u32[]{:S(2)}, u32[]{:S(2)}) collective-permute-start(bf16[96,896]{1,0:T(8,128)(2,1)} %get-tuple-element.76.refs_0_), channel_id=1, source_target_pairs={{0,4},{4,0},{8,12},{12,8},{16,20},{20,16},{24,28},{28,24},{1,5},{5... | collective-permute-start | bytes 516104 | tf_op jit(solution)/shard_map/ppermute | solution.py:82
  9.3 17.8 %collective-permute-start = (bf16[128,768]{1,0:T(8,128)(2,1)}, bf16[128,768]{1,0:T(8,128)(2,1)S(1)}, u32[]{:S(2)}, u32[]{:S(2)}) collective-permute-start(bf16[128,768]{1,0:T(8,128)(2,1)} %tok0.7), channel_id=1, source_target_pairs={{0,1},{1,0},{2,3},{3,2},{4,5},{5,4},{6,7},{7,6},{8,9},{9,8},{10,11... | collective-permute-start | bytes 589832 | tf_op jit(solution)/shard_map/ppermute | solution.py:77
  20.1 18.0 %collective-permute-start.16 = (bf16[96,1536]{1,0:T(8,128)(2,1)}, bf16[96,1536]{1,0:T(8,128)(2,1)}, u32[]{:S(2)}, u32[]{:S(2)}) collective-permute-start(bf16[96,1536]{1,0:T(8,128)(2,1)} %get-tuple-element.84.refs_0_), channel_id=1, source_target_pairs={{0,24},{4,28},{8,0},{12,4},{16,8},{20,12},{24,16},{28,20},{1,25},{... | collective-permute-start | bytes 884744 | tf_op jit(solution)/shard_map/ppermute | solution.py:82
  27.1 9.4 %collective-permute-start.1 = (bf16[128,768]{1,0:T(8,128)(2,1)}, bf16[128,768]{1,0:T(8,128)(2,1)S(1)}, u32[]{:S(2)}, u32[]{:S(2)}) collective-permute-start(bf16[128,768]{1,0:T(8,128)(2,1)} %tok0.7), channel_id=1, source_target_pairs={{0,2},{2,0},{1,3},{3,1},{4,6},{6,4},{5,7},{7,5},{8,10},{10,8},{9,1... | collective-permute-start | bytes 589832 | tf_op jit(solution)/shard_map/ppermute | solution.py:77
  27.1 17.8 %collective-permute-start.19 = (bf16[96,1536]{1,0:T(8,128)(2,1)}, bf16[96,1536]{1,0:T(8,128)(2,1)}, u32[]{:S(2)}, u32[]{:S(2)}) collective-permute-start(bf16[96,1536]{1,0:T(8,128)(2,1)} %get-tuple-element.84.refs_0_), channel_id=1, source_target_pairs={{0,8},{4,12},{8,16},{12,20},{16,24},{20,28},{24,0},{28,4},{1,9},{5... | collective-permute-start | bytes 884744 | tf_op jit(solution)/shard_map/ppermute | solution.py:82
  27.2 16.9 %collective-permute-start.17 = (bf16[96,1536]{1,0:T(8,128)(2,1)}, bf16[96,1536]{1,0:T(8,128)(2,1)}, u32[]{:S(2)}, u32[]{:S(2)}) collective-permute-start(bf16[96,1536]{1,0:T(8,128)(2,1)} %get-tuple-element.84.refs_0_), channel_id=1, source_target_pairs={{0,4},{4,0},{8,12},{12,8},{16,20},{20,16},{24,28},{28,24},{1,5},{5... | collective-permute-start | bytes 884744 | tf_op jit(solution)/shard_map/ppermute | solution.py:82
  31.0 8.5 %collective-permute-start.2 = (bf16[128,768]{1,0:T(8,128)(2,1)S(1)}, bf16[128,768]{1,0:T(8,128)(2,1)S(1)}, u32[]{:S(2)}, u32[]{:S(2)}) collective-permute-start(bf16[128,768]{1,0:T(8,128)(2,1)S(1)} %collective-permute-done.tok1), channel_id=1, source_target_pairs={{0,2},{2,0},{1,3},{3,1},{4,6},{6,4},{5,7},{7,5},{8,10},{10,8},{9,1... | collective-permute-start | bytes 589832 | tf_op jit(solution)/shard_map/ppermute | solution.py:77
  36.6 17.4 %collective-permute-start.13 = (bf16[768,192]{1,0:T(8,128)(2,1)}, bf16[768,192]{1,0:T(8,128)(2,1)}, u32[]{:S(2)}, u32[]{:S(2)}) collective-permute-start(bf16[768,192]{1,0:T(8,128)(2,1)} %get-tuple-element.81.wo0.wo), channel_id=1, source_target_pairs={{0,1},{1,0},{2,3},{3,2},{4,5},{5,4},{6,7},{7,6},{8,9},{9,8},{10,11... | collective-permute-start | bytes 884744 | tf_op jit(solution)/shard_map/ppermute | solution.py:77
  38.1 9.5 %collective-permute-start.21 = (bf16[96,1536]{1,0:T(8,128)(2,1)}, bf16[96,1536]{1,0:T(8,128)(2,1)}, u32[]{:S(2)}, u32[]{:S(2)}) collective-permute-start(bf16[96,1536]{1,0:T(8,128)(2,1)} %collective-permute-done.16.refs_1_), channel_id=1, source_target_pairs={{0,24},{4,28},{8,0},{12,4},{16,8},{20,12},{24,16},{28,20},{1,25},{... | collective-permute-start | bytes 884744 | tf_op jit(solution)/shard_map/ppermute | solution.py:82
  43.5 10.4 %collective-permute-start.10 = (bf16[512,192]{1,0:T(8,128)(2,1)S(1)}, bf16[512,192]{1,0:T(8,128)(2,1)S(1)}, u32[]{:S(2)}, u32[]{:S(2)}) collective-permute-start(bf16[512,192]{1,0:T(8,128)(2,1)S(1)} %get-tuple-element.80.mixed0.mixed), channel_id=1, source_target_pairs={{0,1},{1,0},{2,3},{3,2},{4,5},{5,4},{6,7},{7,6},{8,9},{9,8},{10,11... | collective-permute-start | bytes 589832 | tf_op jit(solution)/shard_map/ppermute | solution.py:77
  44.1 10.6 %collective-permute-start.18 = (bf16[96,1536]{1,0:T(8,128)(2,1)}, bf16[96,1536]{1,0:T(8,128)(2,1)S(1)}, u32[]{:S(2)}, u32[]{:S(2)}) collective-permute-start(bf16[96,1536]{1,0:T(8,128)(2,1)} %collective-permute-done.17.refs_5_), channel_id=1, source_target_pairs={{0,8},{4,12},{8,16},{12,20},{16,24},{20,28},{24,0},{28,4},{1,9},{5... | collective-permute-start | bytes 884744 | tf_op jit(solution)/shard_map/ppermute | solution.py:82
  45.0 10.4 %collective-permute-start.20 = (bf16[96,1536]{1,0:T(8,128)(2,1)}, bf16[96,1536]{1,0:T(8,128)(2,1)S(1)}, u32[]{:S(2)}, u32[]{:S(2)}) collective-permute-start(bf16[96,1536]{1,0:T(8,128)(2,1)} %collective-permute-done.16.refs_1_), channel_id=1, source_target_pairs={{0,4},{4,0},{8,12},{12,8},{16,20},{20,16},{24,28},{28,24},{1,5},{5... | collective-permute-start | bytes 884744 | tf_op jit(solution)/shard_map/ppermute | solution.py:82
  47.5 12.8 %collective-permute-start.22 = (bf16[96,1536]{1,0:T(8,128)(2,1)}, bf16[96,1536]{1,0:T(8,128)(2,1)S(1)}, u32[]{:S(2)}, u32[]{:S(2)}) collective-permute-start(bf16[96,1536]{1,0:T(8,128)(2,1)} %collective-permute-done.21.refs_6_), channel_id=1, source_target_pairs={{0,4},{4,0},{8,12},{12,8},{16,20},{20,16},{24,28},{28,24},{1,5},{5... | collective-permute-start | bytes 884744 | tf_op jit(solution)/shard_map/ppermute | solution.py:82
  53.9 8.7 %collective-permute-start.14 = (bf16[768,192]{1,0:T(8,128)(2,1)}, bf16[768,192]{1,0:T(8,128)(2,1)S(1)}, u32[]{:S(2)}, u32[]{:S(2)}) collective-permute-start(bf16[768,192]{1,0:T(8,128)(2,1)} %get-tuple-element.81.wo0.wo), channel_id=1, source_target_pairs={{0,2},{2,0},{1,3},{3,1},{4,6},{6,4},{5,7},{7,5},{8,10},{10,8},{9,1... | collective-permute-start | bytes 884744 | tf_op jit(solution)/shard_map/ppermute | solution.py:77
  53.9 8.7 %collective-permute-start.15 = (bf16[768,192]{1,0:T(8,128)(2,1)}, bf16[768,192]{1,0:T(8,128)(2,1)S(1)}, u32[]{:S(2)}, u32[]{:S(2)}) collective-permute-start(bf16[768,192]{1,0:T(8,128)(2,1)} %collective-permute-done.13.wo1), channel_id=1, source_target_pairs={{0,2},{2,0},{1,3},{3,1},{4,6},{6,4},{5,7},{7,5},{8,10},{10,8},{9,1... | collective-permute-start | bytes 884744 | tf_op jit(solution)/shard_map/ppermute | solution.py:77
  54.7 7.9 %collective-permute-start.11 = (bf16[512,192]{1,0:T(8,128)(2,1)S(1)}, bf16[512,192]{1,0:T(8,128)(2,1)S(1)}, u32[]{:S(2)}, u32[]{:S(2)}) collective-permute-start(bf16[512,192]{1,0:T(8,128)(2,1)S(1)} %get-tuple-element.80.mixed0.mixed), channel_id=1, source_target_pairs={{0,2},{2,0},{1,3},{3,1},{4,6},{6,4},{5,7},{7,5},{8,10},{10,8},{9,1... | collective-permute-start | bytes 589832 | tf_op jit(solution)/shard_map/ppermute | solution.py:77
  73.0 11.4 %collective-permute-start.26 = (bf16[256,768]{1,0:T(8,128)(2,1)S(1)}, bf16[256,768]{1,0:T(8,128)(2,1)S(1)}, u32[]{:S(2)}, u32[]{:S(2)}) collective-permute-start(bf16[256,768]{1,0:T(8,128)(2,1)S(1)} %get-tuple-element.138), channel_id=1, source_target_pairs={{0,1},{1,0},{2,3},{3,2},{4,5},{5,4},{6,7},{7,6},{8,9},{9,8},{10,11... | collective-permute-start | bytes 1179656 | tf_op jit(solution)/shard_map/ppermute | solution.py:77
  74.5 16.9 %collective-permute-start.34 = (bf16[96,1536]{1,0:T(8,128)(2,1)S(1)}, bf16[96,1536]{1,0:T(8,128)(2,1)S(1)}, u32[]{:S(2)}, u32[]{:S(2)}) collective-permute-start(bf16[96,1536]{1,0:T(8,128)(2,1)S(1)} %get-tuple-element.116), channel_id=1, source_target_pairs={{0,4},{4,0},{8,12},{12,8},{16,20},{20,16},{24,28},{28,24},{1,5},{5... | collective-permute-start | bytes 884744 | tf_op jit(solution)/shard_map/ppermute | solution.py:82
  76.3 14.4 %collective-permute-start.27 = (bf16[96,1536]{1,0:T(8,128)(2,1)S(1)}, bf16[96,1536]{1,0:T(8,128)(2,1)S(1)}, u32[]{:S(2)}, u32[]{:S(2)}) collective-permute-start(bf16[96,1536]{1,0:T(8,128)(2,1)S(1)} %get-tuple-element.100), channel_id=1, source_target_pairs={{0,4},{4,0},{8,12},{12,8},{16,20},{20,16},{24,28},{28,24},{1,5},{5... | collective-permute-start | bytes 884744 | tf_op jit(solution)/shard_map/ppermute | solution.py:82
  76.6 20.5 %collective-permute-start.29 = (bf16[96,1536]{1,0:T(8,128)(2,1)S(1)}, bf16[96,1536]{1,0:T(8,128)(2,1)S(1)}, u32[]{:S(2)}, u32[]{:S(2)}) collective-permute-start(bf16[96,1536]{1,0:T(8,128)(2,1)S(1)} %get-tuple-element.103), channel_id=1, source_target_pairs={{0,4},{4,0},{8,12},{12,8},{16,20},{20,16},{24,28},{28,24},{1,5},{5... | collective-permute-start | bytes 884744 | tf_op jit(solution)/shard_map/ppermute | solution.py:82
  78.4 32.1 %collective-permute-start.35 = (bf16[96,1536]{1,0:T(8,128)(2,1)S(1)}, bf16[96,1536]{1,0:T(8,128)(2,1)S(1)}, u32[]{:S(2)}, u32[]{:S(2)}) collective-permute-start(bf16[96,1536]{1,0:T(8,128)(2,1)S(1)} %get-tuple-element.117), channel_id=1, source_target_pairs={{0,4},{4,0},{8,12},{12,8},{16,20},{20,16},{24,28},{28,24},{1,5},{5... | collective-permute-start | bytes 884744 | tf_op jit(solution)/shard_map/ppermute | solution.py:82
  91.5 41.8 %collective-permute-start.45 = (bf16[96,1536]{1,0:T(8,128)(2,1)S(1)}, bf16[96,1536]{1,0:T(8,128)(2,1)S(1)}, u32[]{:S(2)}, u32[]{:S(2)}) collective-permute-start(bf16[96,1536]{1,0:T(8,128)(2,1)S(1)} %add_convert_fusion), channel_id=1, source_target_pairs={{0,24},{4,28},{8,0},{12,4},{16,8},{20,12},{24,16},{28,20},{1,25},{... | collective-permute-start | bytes 884744 | tf_op jit(solution)/shard_map/ppermute | solution.py:82
  103.7 11.3 %collective-permute-start.43 = (bf16[96,1536]{1,0:T(8,128)(2,1)S(1)}, bf16[96,1536]{1,0:T(8,128)(2,1)S(1)}, u32[]{:S(2)}, u32[]{:S(2)}) collective-permute-start(bf16[96,1536]{1,0:T(8,128)(2,1)S(1)} %add_convert_fusion.2), channel_id=1, source_target_pairs={{0,8},{4,12},{8,16},{12,20},{16,24},{20,28},{24,0},{28,4},{1,9},{5... | collective-permute-start | bytes 884744 | tf_op jit(solution)/shard_map/ppermute | solution.py:82
  109.8 9.8 %collective-permute-start.25 = (bf16[128,768]{1,0:T(8,128)(2,1)S(1)}, bf16[128,768]{1,0:T(8,128)(2,1)S(1)}, u32[]{:S(2)}, u32[]{:S(2)}) collective-permute-start(bf16[128,768]{1,0:T(8,128)(2,1)S(1)} %slice.76), channel_id=1, source_target_pairs={{0,1},{1,0},{2,3},{3,2},{4,5},{5,4},{6,7},{7,6},{8,9},{9,8},{10,11... | collective-permute-start | bytes 589832 | tf_op jit(solution)/shard_map/ppermute | solution.py:77
  115.1 18.3 %collective-permute-start.44 = (bf16[96,1536]{1,0:T(8,128)(2,1)S(1)}, bf16[96,1536]{1,0:T(8,128)(2,1)S(1)}, u32[]{:S(2)}, u32[]{:S(2)}) collective-permute-start(bf16[96,1536]{1,0:T(8,128)(2,1)S(1)} %add_convert_fusion.1), channel_id=1, source_target_pairs={{0,8},{4,12},{8,16},{12,20},{16,24},{20,28},{24,0},{28,4},{1,9},{5... | collective-permute-start | bytes 884744 | tf_op jit(solution)/shard_map/ppermute | solution.py:82
  119.6 7.4 %collective-permute-start.37 = (bf16[96,896]{1,0:T(8,128)(2,1)S(1)}, bf16[96,896]{1,0:T(8,128)(2,1)S(1)}, u32[]{:S(2)}, u32[]{:S(2)}) collective-permute-start(bf16[96,896]{1,0:T(8,128)(2,1)S(1)} %get-tuple-element.123), channel_id=1, source_target_pairs={{0,4},{4,0},{8,12},{12,8},{16,20},{20,16},{24,28},{28,24},{1,5},{5... | collective-permute-start | bytes 516104 | tf_op jit(solution)/shard_map/ppermute | solution.py:82
  121.8 13.5 %collective-permute-start.36 = (bf16[96,896]{1,0:T(8,128)(2,1)S(1)}, bf16[96,896]{1,0:T(8,128)(2,1)S(1)}, u32[]{:S(2)}, u32[]{:S(2)}) collective-permute-start(bf16[96,896]{1,0:T(8,128)(2,1)S(1)} %get-tuple-element.121), channel_id=1, source_target_pairs={{0,4},{4,0},{8,12},{12,8},{16,20},{20,16},{24,28},{28,24},{1,5},{5... | collective-permute-start | bytes 516104 | tf_op jit(solution)/shard_map/ppermute | solution.py:82
  124.0 8.4 %collective-permute-start.39 = (bf16[96,896]{1,0:T(8,128)(2,1)S(1)}, bf16[96,896]{1,0:T(8,128)(2,1)S(1)}, u32[]{:S(2)}, u32[]{:S(2)}) collective-permute-start(bf16[96,896]{1,0:T(8,128)(2,1)S(1)} %add_convert_fusion.5), channel_id=1, source_target_pairs={{0,8},{4,12},{8,16},{12,20},{16,24},{20,28},{24,0},{28,4},{1,9},{5... | collective-permute-start | bytes 516104 | tf_op jit(solution)/shard_map/ppermute | solution.py:82
  127.0 8.3 %collective-permute-start.42 = (bf16[96,896]{1,0:T(8,128)(2,1)S(1)}, bf16[96,896]{1,0:T(8,128)(2,1)S(1)}, u32[]{:S(2)}, u32[]{:S(2)}) collective-permute-start(bf16[96,896]{1,0:T(8,128)(2,1)S(1)} %add_convert_fusion.3), channel_id=1, source_target_pairs={{0,24},{4,28},{8,0},{12,4},{16,8},{20,12},{24,16},{28,20},{1,25},{... | collective-permute-start | bytes 516104 | tf_op jit(solution)/shard_map/ppermute | solution.py:82
  132.5 9.6 %collective-permute-start.40 = (bf16[96,896]{1,0:T(8,128)(2,1)S(1)}, bf16[96,896]{1,0:T(8,128)(2,1)S(1)}, u32[]{:S(2)}, u32[]{:S(2)}) collective-permute-start(bf16[96,896]{1,0:T(8,128)(2,1)S(1)} %add_convert_fusion.4), channel_id=1, source_target_pairs={{0,8},{4,12},{8,16},{12,20},{16,24},{20,28},{24,0},{28,4},{1,9},{5... | collective-permute-start | bytes 516104 | tf_op jit(solution)/shard_map/ppermute | solution.py:82
  (24 other events, 164.2 us)

commit v4 on v3

--- a/solution.py
+++ b/solution.py
@@ -12,6 +12,7 @@
 DIRECT_SIZE = 8
 STEPS = ((0, 0), (1, 0), (3, 1), (3, 0), (1, 1), (0, 1), (2, 0), (2, 1))
 VEC_COLS = 128
+FIRST_LIMIT = 40
 LOW = jnp.bfloat16
 F32 = jnp.float32
 GELU_SCALE = float(np.sqrt(2.0 / np.pi))
@@ -94,9 +95,9 @@
     return [chunk, ahead, across[0], behind, across[1], other, far, send(far, 0, 1)]
 
 
-def pieces_mixed(chunk, ring_free, pair_free):
-    ahead, behind = [send(after(chunk, ring_free), turn, 0) for turn in (3, 1)]
-    other = send(after(chunk, *pair_free), 0, 1)
+def pieces_mixed(chunk, ring_free):
+    ahead, behind = [send(after(chunk, *ring_free), turn, 0) for turn in (3, 1)]
+    other = send(chunk, 0, 1)
     far = send(ahead, 3, 0)
     return [chunk, ahead, send(other, 1, 0), behind, send(ahead, 0, 1), other, far, send(far, 0, 1)]
 
@@ -108,15 +109,15 @@
     return total.astype(LOW)
 
 
-def over_pair(pieces):
-    return [send(pieces[step], 0, 1) for step in (7, 4, 2, 5)]
-
-
-def round_ring(pieces, got):
-    far = send(added(pieces[6], got[0]), 1, 0)
-    behind = send(added(pieces[3], got[2]), 3, 0)
+def sums_begin(pieces):
+    return [send(pieces[7], 0, 1), send(pieces[4], 0, 1), send(pieces[2], 3, 0), send(pieces[3], 3, 0)]
+
+
+def sums_end(pieces, got):
+    far = send(added(after(pieces[6], got[2]), got[0]), 1, 0)
+    other = send(added(after(pieces[5], far), got[2]), 0, 1)
     ahead = send(added(pieces[1], got[1], far), 1, 0)
-    return [pieces[0], got[3], ahead, behind]
+    return [pieces[0], got[3], other, ahead]
 
 
 def row_start(me, step, rows):
@@ -141,25 +142,6 @@
     second[...] = jnp.concatenate([wfc[...], wproj[...]], axis=1)
 
 
-def open_first_body(size, scal, *refs):
-    pieces, (sel, wqkv, wo, rows, bias, cols) = refs[:size], refs[size:]
-    chunk = pieces[0].shape[0]
-    split = VEC_COLS + wqkv.shape[1]
-    end = split + wo.shape[1]
-    for step, piece in enumerate(pieces):
-        place = pl.ds(row_start(scal[0], step, chunk) if size > 1 else 0, chunk)
-        value = piece[:, :end]
-        cols[place, :] = value[:, :VEC_COLS].astype(F32)
-        wqkv[place, :] = value[:, VEC_COLS:split]
-        wo[place, :] = value[:, split:]
-    wide = cols[...].T
-    rows[...] = wide[:8]
-    spread = dot(wide[:16].astype(LOW), sel[...], 1, 0)
-    col = lax.broadcasted_iota(jnp.int32, (8, bias.shape[1]), 1)
-    count = wo.shape[1]
-    bias[...] = jnp.where(col < count, spread[7:8], jnp.where(col >= 2 * count, spread[8:9], 0.0))
-
-
 def open_second_body(size, scal, *refs):
     pieces, (grad, wf, wp, da, cot) = refs[:size], refs[size:]
     chunk = pieces[-1].shape[0]
@@ -183,17 +165,32 @@
         mask[part, :] = jnp.where(seen, 0.0, -1e30)
 
 
-def attend_body(
-    tok0, tok1, tok2, tok3, wqkv, bias, rows, doc_col, doc_row, pos_col, pos_row,
-    qkv, mixed, lse, normed, mask,
-):
+def attend_body(size, scal, *refs):
+    pieces, refs = refs[:size], refs[size:]
+    sel, tok0, tok1, tok2, tok3, doc_col, doc_row, pos_col, pos_row = refs[:9]
+    qkv, mixed, lse, wqkv, wo, rows, cols, normed, mask = refs[9:]
+    chunk = pieces[0].shape[0]
+    split = VEC_COLS + wqkv.shape[1]
+    end = split + wo.shape[1]
+    for step, piece in enumerate(pieces):
+        place = pl.ds(row_start(scal[0], step, chunk) if size > 1 else 0, chunk)
+        value = piece[:, :end]
+        cols[place, :] = value[:, :VEC_COLS].astype(F32)
+        wqkv[place, :] = value[:, VEC_COLS:split]
+        wo[place, :] = value[:, split:]
+    wide = cols[...].T
+    rows[...] = wide[:8]
+    spread = dot(wide[:16].astype(LOW), sel[...], 1, 0)
+    col = lax.broadcasted_iota(jnp.int32, (1, qkv.shape[1]), 1)
+    count = wo.shape[1]
+    bias = jnp.where(col < count, spread[7:8], jnp.where(col >= 2 * count, spread[8:9], 0.0))
     total = qkv.shape[0]
     part = tok0.shape[0]
-    gain, shift = rows[2:3, :], rows[3:4, :]
+    gain, shift = wide[2:3], wide[3:4]
     for number, source in enumerate((tok0, tok1, tok2, tok3)):
         scaled, _ = norm_parts(source[...].astype(F32))
         normed[number * part : (number + 1) * part, :] = (scaled * gain + shift).astype(LOW)
-    qkv[...] = (dot(normed[...], wqkv[...], 1, 0) + bias[7:8, :]).astype(LOW)
+    qkv[...] = (dot(normed[...], wqkv[...], 1, 0) + bias).astype(LOW)
     fill_mask(mask, doc_col, doc_row, pos_col, pos_row)
     width = qkv.shape[1] // 3
     heads = width // HEAD_DIM
@@ -410,13 +407,16 @@
 
 def sum_last_body(*refs):
     total = total_of(*refs[:4])
-    wqkv, wout, vecs = refs[4:]
+    wqkv, wout, qv, *vecs = refs[4:]
     width = wout.shape[0]
     for number in range(3):
         low = VEC_COLS + number * width
         wqkv[number] = total[:, low : low + width]
     wout[...] = turned_wide(total[:, VEC_COLS + 3 * width :])
-    vecs[...] = turned_wide(total[:, :VEC_COLS])[:16]
+    turned_vecs = turned_wide(total[:, :VEC_COLS])
+    for number, vec in enumerate(vecs):
+        vec[...] = turned_vecs[number : number + 1]
+    qv[...] = turned_vecs[7:9, : qv.shape[1]]
 
 
 def local(
@@ -462,7 +462,6 @@
 
     rows_shape = shape(8, width, F32)
     bias_shape = shape(8, qkv_cols, F32)
-    wqkv_shape, wo_shape = shape(width, qkv_cols, LOW), shape(width, head_cols, LOW)
     if direct:
         first, second = on_core(
             pack_body,
@@ -472,7 +471,7 @@
             limit=62,
         )
         firsts = pieces_ring_first(first)
-        seconds = pieces_mixed(second, firsts[6], [firsts[2], firsts[4]])
+        seconds = pieces_mixed(second, [firsts[1], firsts[3]])
     else:
         lines = jnp.stack([*vecs, *jnp.pad(b_qv, ((0, 0), (0, chunk - qv_count)))])
         lack = jnp.zeros((chunk, VEC_COLS - lines.shape[0]), LOW)
@@ -481,16 +480,6 @@
         firsts = [lax.all_gather(first, "fsdp", axis=0, tiled=True)]
         seconds = [lax.all_gather(second, "fsdp", axis=0, tiled=True)]
         scal = scal * jnp.asarray([0, 1], jnp.int32)
-    wqkv, wo, rows, bias = on_core(
-        functools.partial(open_first_body, parts),
-        [wqkv_shape, wo_shape, rows_shape, bias_shape],
-        [scal],
-        [*firsts, sel],
-        [pltpu.VMEM((width, VEC_COLS), F32)],
-    )
-    wo_near = swap(wo, "tensor")
-    wos = [wo, wo_near, swap(wo, "seq"), swap(wo_near, "seq")]
-
     blocks = [place ^ b for b in range(4)]
     docs = jnp.concatenate([lax.dynamic_slice_in_dim(segments, b * own_rows, own_rows, 0) for b in blocks])
     spots = jnp.concatenate([b * own_rows + jnp.arange(own_rows, dtype=jnp.int32) for b in blocks])
@@ -498,14 +487,23 @@
 
     mask_scratch = pltpu.VMEM((seq_rows, seq_rows), F32)
     normed_scratch = pltpu.VMEM((seq_rows, width), LOW)
-    qkv, mixed, lse = on_core(
-        attend_body,
-        [shape(seq_rows, qkv_cols, LOW), shape(seq_rows, head_cols, LOW), shape(seq_rows, 128, F32)],
-        [],
-        [*toks, wqkv, bias, rows, *marks],
-        [normed_scratch, mask_scratch],
+    qkv, mixed, lse, wqkv, wo, rows = on_core(
+        functools.partial(attend_body, parts),
+        [
+            shape(seq_rows, qkv_cols, LOW),
+            shape(seq_rows, head_cols, LOW),
+            shape(seq_rows, 128, F32),
+            shape(width, qkv_cols, LOW),
+            shape(width, head_cols, LOW),
+            rows_shape,
+        ],
+        [scal],
+        [*firsts, sel, *toks, *marks],
+        [pltpu.VMEM((width, VEC_COLS), F32), normed_scratch, mask_scratch],
         flops=2 * seq_rows * (width * qkv_cols + 2 * head_cols * seq_rows),
     )
+    wo_near = swap(after(wo, mixed), "tensor")
+    wos = [wo, wo_near, swap(wo, "seq"), swap(wo_near, "seq")]
     mixed_near = swap(mixed, "tensor")
     mixeds = [mixed, mixed_near, swap(mixed, "seq"), swap(mixed_near, "seq")]
 
@@ -551,10 +549,10 @@
     out_half = out_keep + swap(out_send, "seq").astype(F32)
     out_far = swap(out_half[own_rows:].astype(LOW), "tensor")
     result = (middle[:own_rows] + out_half[:own_rows] + out_far.astype(F32) + rows[1:2]).astype(LOW)
-    far = after(far, fc_sum, out_half)
+    far = after(far, fc_sum)
     if direct:
-        crossed = over_pair(grad_ff)
-        far = after(far, crossed[0])
+        begun = sums_begin(grad_ff)
+        far = after(far, begun[0], begun[2])
     grad_mid_half, grad_mid_own, early = on_core(
         middle_body,
         [shape(half, width, LOW), shape(own_rows, width, F32), rows_shape],
@@ -564,8 +562,7 @@
     grad_mid_other = swap(grad_mid_half, "seq")
 
     if direct:
-        grad_mid_other = after(grad_mid_other, crossed[1])
-        got_ff = round_ring(grad_ff, crossed)
+        got_ff = sums_end(grad_ff, begun)
     keep_one, send_one, grad_qkv, late, qkv_sum = on_core(
         attend_back_body,
         [
@@ -581,8 +578,6 @@
         flops=2 * seq_rows * (width * (qkv_cols + head_cols) + 5 * head_cols * seq_rows),
     )
     part_one = keep_one + swap(send_one, "seq").astype(F32)
-    late = late + swap(late, "tensor")
-    late = late + swap(late, "seq")
     far_one = swap(part_one[own_rows:].astype(LOW), "tensor")
     (grad_inputs,) = on_core(
         input_body,
@@ -600,9 +595,11 @@
         [normed_scratch],
         flops=2 * seq_rows * width * (qkv_cols + head_cols),
     )
-    late = after(late, part_one)
+    late = late + swap(late, "tensor")
+    late = after(late, part_one, lines)
+    late = late + swap(late, "seq")
     if direct:
-        late = after(late, *crossed)
+        late = after(late, *begun)
     grad_last = on_core(
         last_cut_body,
         piece_shapes(parts, width, last_cols),
@@ -612,9 +609,9 @@
     )
 
     if direct:
-        crossed = over_pair(grad_last)
-        crossed[2] = after(crossed[2], far_one, out_far)
-        got_last = round_ring(grad_last, crossed)
+        begun = sums_begin(grad_last)
+        begun[1] = after(begun[1], far_one, out_far)
+        got_last = sums_end(grad_last, begun)
         grad_wfc, grad_wproj = on_core(
             sum_feed_body,
             [shape(chunk, hidden_cols, F32)] * 2,
@@ -622,9 +619,10 @@
             got_ff,
         )
         grad_wproj = grad_wproj.T
-        grad_wqkv, grad_wout, sums = on_core(
+        grad_wqkv, grad_wout, grad_qv, *sums = on_core(
             sum_last_body,
-            [jax.ShapeDtypeStruct((3, chunk, head_cols), F32), shape(head_cols, chunk, F32), shape(16, chunk, F32)],
+            [jax.ShapeDtypeStruct((3, chunk, head_cols), F32), shape(head_cols, chunk, F32), shape(2, qv_count, F32)]
+            + [shape(1, chunk, F32)] * 7,
             [],
             got_last,
         )
@@ -635,7 +633,8 @@
         split = VEC_COLS + qkv_cols
         grad_wqkv = sum_last[:, VEC_COLS:split].reshape(chunk, 3, head_cols).transpose(1, 0, 2)
         grad_wout = sum_last[:, split:].T
-        sums = sum_last[:, :16].T
+        sums = sum_last[:, :7].T
+        grad_qv = sum_last[:qv_count, 7:9].T
 
     return (
         result,
@@ -644,14 +643,8 @@
         grad_wout,
         grad_wfc,
         grad_wproj,
-        sums[7:9, :qv_count],
-        sums[0],
-        sums[6],
-        sums[1],
-        sums[2],
-        sums[3],
-        sums[4],
-        sums[5],
+        grad_qv,
+        *[sums[number].reshape(chunk) for number in (0, 6, 1, 2, 3, 4, 5)],
     )
 
 

time: 144 us -> 130 us (0.903)
  waiting for transfers between devices: 49 us -> 42.3 us
  starting transfers between devices: 52.1 us -> 48.8 us
  Pallas kernels: 31.4 us -> 28.7 us
  local copies, waits for them, and re-layouts: 8.05 us -> 6.03 us
    ppermute x18, waiting for transfers between devices: 14.8 us -> 10.6 us  [swap(): return lax.ppermute(value, axis, [(0, 1), (1, 0)])]
    ppermute x28, starting transfers between devices: 43.4 us -> 39.4 us  [send(): return lax.ppermute(value, 'fsdp', pairs)]
    pallas_call x13 -> x12, Pallas kernels: 31.4 us -> 28.7 us  [on_core(): pl.pallas_call(body, out_shape=tuple(outs), in_specs=specs, out_specs=tup...]
    ppermute x28, waiting for transfers between devices: 34.3 us -> 31.7 us  [send(): return lax.ppermute(value, 'fsdp', pairs)]
  transfers between devices with their start and end apart: 46 -> 46, of which waited for: 19 -> 19; matrix products, arithmetic and copies ran while one was open for 3% -> 3% of each run, Pallas kernels for 14% -> 16%
where the time goes in v4:
time: 130 us
  starting transfers between devices  48.8 us (38%)
  waiting for transfers between devices  42.3 us (33%)
  Pallas kernels  28.7 us (22%)
  local copies, waits for them, and re-layouts  6.03 us (5%)
  other arithmetic  3.01 us (2%)
    ppermute x28, starting transfers between devices, send(): return lax.ppermute(value, 'fsdp', pairs)  39.4 us
    ppermute x28, waiting for transfers between devices, send(): return lax.ppermute(value, 'fsdp', pairs)  31.7 us
    pallas_call x12, Pallas kernels, on_core(): pl.pallas_call(body, out_shape=tuple(outs), in_specs=specs, out_specs=tup...  28.7 us
    ppermute x18, waiting for transfers between devices, swap(): return lax.ppermute(value, axis, [(0, 1), (1, 0)])  10.6 us
    ppermute x18, starting transfers between devices, swap(): return lax.ppermute(value, axis, [(0, 1), (1, 0)])  9.38 us
    unnamed x20, local copies, waits for them, and re-layouts  4.76 us
  transfers between devices with their start and end apart: 46, of which 19 were waited for; matrix products, arithmetic and copies ran while one was open for 3% of the time, Pallas kernels for 16%

profile of v4, /device:TPU:0, one launch (start us, length us, event | category | flops | bytes accessed | tf_op | source)
XLA Modules:
  0.0 129.9 jit_solution(3760555318964526779)
XLA Ops:
  0.7 2.1 %shard_map.263 = (bf16[96,896]{1,0:T(8,128)(2,1)}, bf16[96,1536]{1,0:T(8,128)(2,1)}) custom-call(bf16[3,96,192]{2,1,0:T(8,128)(2,1)} %wqkv.1, bf16[192,96]{1,0:T(8,128)(2,1)} %wout.1, bf16[96,768]{1,0:T(8,128)(2,1)} %wfc.1, bf16[96,768]{1,0:T(8,128)(2,1)} %bitcast.21, bf16[2,24]{1,0:T(2,128)(2,1)} %bqv.1, bf16[96]{0:T(256)(128)(2,1)} %refs_0_.1, ...), custom_call_target="tpu_custom_call" | custom-call | bytes 910752 | tf_op jit(solution)/shard_map/pallas_call | solution.py:31
  2.8 5.0 %collective-permute-start.3 = (bf16[96,896]{1,0:T(8,128)(2,1)}, bf16[96,896]{1,0:T(8,128)(2,1)S(1)}, u32[]{:S(2)}, u32[]{:S(2)}) collective-permute-start(bf16[96,896]{1,0:T(8,128)(2,1)} %get-tuple-element.85.refs_0_), channel_id=1, source_target_pairs={{0,24},{4,28},{8,0},{12,4},{16,8},{20,12},{24,16},{28,20},{1,25},{... | collective-permute-start | bytes 516104 | tf_op jit(solution)/shard_map/ppermute | solution.py:83
  13.5 2.9 %collective-permute-done.4.refs_3_ = bf16[96,896]{1,0:T(8,128)(2,1)} collective-permute-done((bf16[96,896]{1,0:T(8,128)(2,1)}, bf16[96,896]{1,0:T(8,128)(2,1)}, u32[]{:S(2)}, u32[]{:S(2)}) %collective-permute-start.4) | collective-permute-done | bytes 172064 | tf_op jit(solution)/shard_map/ppermute | solution.py:83
  16.4 1.7 %collective-permute-start.8 = (bf16[96,896]{1,0:T(8,128)(2,1)S(1)}, bf16[96,896]{1,0:T(8,128)(2,1)}, u32[]{:S(2)}, u32[]{:S(2)}) collective-permute-start(bf16[96,896]{1,0:T(8,128)(2,1)S(1)} %collective-permute-done.3.refs_1_), channel_id=1, source_target_pairs={{0,24},{4,28},{8,0},{12,4},{16,8},{20,12},{24,16},{28,20},{1,25},{... | collective-permute-start | bytes 516104 | tf_op jit(solution)/shard_map/ppermute | solution.py:83
  19.4 2.0 %collective-permute-start.6 = (bf16[96,896]{1,0:T(8,128)(2,1)S(1)}, bf16[96,896]{1,0:T(8,128)(2,1)S(1)}, u32[]{:S(2)}, u32[]{:S(2)}) collective-permute-start(bf16[96,896]{1,0:T(8,128)(2,1)S(1)} %collective-permute-done.3.refs_1_), channel_id=1, source_target_pairs={{0,4},{4,0},{8,12},{12,8},{16,20},{20,16},{24,28},{28,24},{1,5},{5... | collective-permute-start | bytes 516104 | tf_op jit(solution)/shard_map/ppermute | solution.py:83
  24.5 2.2 %collective-permute-done.6.refs_4_ = bf16[96,896]{1,0:T(8,128)(2,1)S(1)} collective-permute-done((bf16[96,896]{1,0:T(8,128)(2,1)S(1)}, bf16[96,896]{1,0:T(8,128)(2,1)S(1)}, u32[]{:S(2)}, u32[]{:S(2)}) %collective-permute-start.6) | collective-permute-done | bytes 172064 | tf_op jit(solution)/shard_map/ppermute | solution.py:83
  30.1 1.7 %collective-permute-start.18 = (bf16[96,1536]{1,0:T(8,128)(2,1)}, bf16[96,1536]{1,0:T(8,128)(2,1)S(1)}, u32[]{:S(2)}, u32[]{:S(2)}) collective-permute-start(bf16[96,1536]{1,0:T(8,128)(2,1)} %collective-permute-done.17.refs_5_), channel_id=1, source_target_pairs={{0,8},{4,12},{8,16},{12,20},{16,24},{20,28},{24,0},{28,4},{1,9},{5... | collective-permute-start | bytes 884744 | tf_op jit(solution)/shard_map/ppermute | solution.py:83
  31.8 2.1 %collective-permute-start.21 = (bf16[96,1536]{1,0:T(8,128)(2,1)}, bf16[96,1536]{1,0:T(8,128)(2,1)S(1)}, u32[]{:S(2)}, u32[]{:S(2)}) collective-permute-start(bf16[96,1536]{1,0:T(8,128)(2,1)} %collective-permute-done.16.refs_1_), channel_id=1, source_target_pairs={{0,24},{4,28},{8,0},{12,4},{16,8},{20,12},{24,16},{28,20},{1,25},{... | collective-permute-start | bytes 884744 | tf_op jit(solution)/shard_map/ppermute | solution.py:83
  37.4 5.2 %shard_map.264 = (bf16[512,576]{1,0:T(8,128)(2,1)S(1)}, bf16[512,192]{1,0:T(8,128)(2,1)S(1)}, f32[512,128]{1,0:T(8,128)S(1)}, bf16[768,576]{1,0:T(8,128)(2,1)S(1...) custom-call(s32[2]{0:T(128)S(1)} %copy-done.8, bf16[96,896]{1,0:T(8,128)(2,1)S(1)} %copy-done.3, ...), custom_call_target="tpu_custom_call" | custom-call | flops 654311424 | bytes 5308416 | tf_op jit(solution)/shard_map/pallas_call | solution.py:31
  46.2 1.8 %collective-permute-done.21.refs_6_ = bf16[96,1536]{1,0:T(8,128)(2,1)S(1)} collective-permute-done((bf16[96,1536]{1,0:T(8,128)(2,1)}, bf16[96,1536]{1,0:T(8,128)(2,1)S(1)}, u32[]{:S(2)}, u32[]{:S(2)}) %collective-permute-start.21) | collective-permute-done | bytes 294944 | tf_op jit(solution)/shard_map/ppermute | solution.py:83
  49.2 4.2 %collective-permute-done.13.wo1 = bf16[768,192]{1,0:T(8,128)(2,1)S(1)} collective-permute-done((bf16[768,192]{1,0:T(8,128)(2,1)S(1)}, bf16[768,192]{1,0:T(8,128)(2,1)S(1)}, u32[]{:S(2)}, u32[]{:S(2)}) %collective-permute-start.13) | collective-permute-done | bytes 294944 | tf_op jit(solution)/shard_map/ppermute | solution.py:78
  53.3 2.8 %collective-permute-done.10.mixed1 = bf16[512,192]{1,0:T(8,128)(2,1)S(1)} collective-permute-done((bf16[512,192]{1,0:T(8,128)(2,1)S(1)}, bf16[512,192]{1,0:T(8,128)(2,1)S(1)}, u32[]{:S(2)}, u32[]{:S(2)}) %collective-permute-start.10) | collective-permute-done | bytes 196640 | tf_op jit(solution)/shard_map/ppermute | solution.py:78
  57.3 2.1 %shard_map.265 = (bf16[768,768]{1,0:T(8,128)(2,1)S(1)}, bf16[768,768]{1,0:T(8,128)(2,1)S(1)}, f32[512,768]{1,0:T(8,128)S(1)}, bf16[512,768]{1,0:T(8,128)(2,1)S(1)}) custom-call(s32[2]{0:T(128)S(1)} %copy-done.8, bf16[96,1536]{1,0:T(8,128)(2,1)S(1)} %copy-done.2, bf16[96,1536]{1,0:T(8,128)(2,1)} %collective-permute-done.16.refs_1_, ...), custom_call_target="tpu_custom_call" | custom-call | flops 603979776 | bytes 7864320 | tf_op jit(solution)/shard_map/pallas_call | solution.py:31
  59.5 4.3 %shard_map.266 = (f32[256,768]{1,0:T(8,128)S(1)}, bf16[256,768]{1,0:T(8,128)(2,1)S(1)}, f32[256,768]{1,0:T(8,128)S(1)}, bf16[512,768]{1,0:T(8,128)(2,1)S(1)}, bf...) custom-call(bf16[128,768]{1,0:T(8,128)(2,1)S(1)} %copy-done, ...), custom_call_target="tpu_custom_call" | custom-call | flops 1811939328 | bytes 9854976 | tf_op jit(solution)/shard_map/pallas_call | solution.py:31
  63.9 1.7 %collective-permute-done.23 = bf16[256,768]{1,0:T(8,128)(2,1)S(1)} collective-permute-done((bf16[256,768]{1,0:T(8,128)(2,1)S(1)}, bf16[256,768]{1,0:T(8,128)(2,1)S(1)}, u32[]{:S(2)}, u32[]{:S(2)}) %collective-permute-start.23) | collective-permute-done | bytes 393248 | tf_op jit(solution)/shard_map/ppermute | solution.py:78
  66.9 2.9 %shard_map.267 = (f32[256,768]{1,0:T(8,128)S(1)}, bf16[256,768]{1,0:T(8,128)(2,1)S(1)}, f32[1,768]{1,0:T(1,128)S(1)}, f32[96,1536]{1,0:T(8,128)S(1)}, bf16[96,15...) custom-call(s32[2]{0:T(128)S(1)} %copy-done.9, ...), custom_call_target="tpu_custom_call" | custom-call | flops 1811939328 | bytes 8162304 | tf_op jit(solution)/shard_map/pallas_call | solution.py:31
  69.7 3.5 %collective-permute-start.28 = (bf16[96,1536]{1,0:T(8,128)(2,1)S(1)}, bf16[96,1536]{1,0:T(8,128)(2,1)S(1)}, u32[]{:S(2)}, u32[]{:S(2)}) collective-permute-start(bf16[96,1536]{1,0:T(8,128)(2,1)S(1)} %get-tuple-element.108), channel_id=1, source_target_pairs={{0,24},{4,28},{8,0},{12,4},{16,8},{20,12},{24,16},{28,20},{1,25},{... | collective-permute-start | bytes 884744 | tf_op jit(solution)/shard_map/ppermute | solution.py:83
  73.2 2.0 %collective-permute-start.27 = (bf16[96,1536]{1,0:T(8,128)(2,1)S(1)}, bf16[96,1536]{1,0:T(8,128)(2,1)S(1)}, u32[]{:S(2)}, u32[]{:S(2)}) collective-permute-start(bf16[96,1536]{1,0:T(8,128)(2,1)S(1)} %get-tuple-element.107), channel_id=1, source_target_pairs={{0,4},{4,0},{8,12},{12,8},{16,20},{20,16},{24,28},{28,24},{1,5},{5... | collective-permute-start | bytes 884744 | tf_op jit(solution)/shard_map/ppermute | solution.py:83
  75.2 1.7 %collective-permute-done.26.far = bf16[256,768]{1,0:T(8,128)(2,1)S(1)} collective-permute-done((bf16[256,768]{1,0:T(8,128)(2,1)S(1)}, bf16[256,768]{1,0:T(8,128)(2,1)S(1)}, u32[]{:S(2)}, u32[]{:S(2)}) %collective-permute-start.26) | collective-permute-done | bytes 393248 | tf_op jit(solution)/shard_map/ppermute | solution.py:78
  76.9 3.4 %collective-permute-done.28 = bf16[96,1536]{1,0:T(8,128)(2,1)S(1)} collective-permute-done((bf16[96,1536]{1,0:T(8,128)(2,1)S(1)}, bf16[96,1536]{1,0:T(8,128)(2,1)S(1)}, u32[]{:S(2)}, u32[]{:S(2)}) %collective-permute-start.28) | collective-permute-done | bytes 294944 | tf_op jit(solution)/shard_map/ppermute | solution.py:83
  80.3 1.6 %collective-permute-done.27 = bf16[96,1536]{1,0:T(8,128)(2,1)S(1)} collective-permute-done((bf16[96,1536]{1,0:T(8,128)(2,1)S(1)}, bf16[96,1536]{1,0:T(8,128)(2,1)S(1)}, u32[]{:S(2)}, u32[]{:S(2)}) %collective-permute-start.27) | collective-permute-done | bytes 294944 | tf_op jit(solution)/shard_map/ppermute | solution.py:83
  82.7 1.8 %collective-permute-start.34 = (bf16[96,1536]{1,0:T(8,128)(2,1)S(1)}, bf16[96,1536]{1,0:T(8,128)(2,1)S(1)}, u32[]{:S(2)}, u32[]{:S(2)}) collective-permute-start(bf16[96,1536]{1,0:T(8,128)(2,1)S(1)} %get-tuple-element.124), channel_id=1, source_target_pairs={{0,4},{4,0},{8,12},{12,8},{16,20},{20,16},{24,28},{28,24},{1,5},{5... | collective-permute-start | bytes 884744 | tf_op jit(solution)/shard_map/ppermute | solution.py:83
  84.5 2.1 %collective-permute-start.35 = (bf16[96,1536]{1,0:T(8,128)(2,1)S(1)}, bf16[96,1536]{1,0:T(8,128)(2,1)S(1)}, u32[]{:S(2)}, u32[]{:S(2)}) collective-permute-start(bf16[96,1536]{1,0:T(8,128)(2,1)S(1)} %get-tuple-element.125), channel_id=1, source_target_pairs={{0,24},{4,28},{8,0},{12,4},{16,8},{20,12},{24,16},{28,20},{1,25},{... | collective-permute-start | bytes 884744 | tf_op jit(solution)/shard_map/ppermute | solution.py:83
  86.6 4.9 %shard_map.269 = (f32[256,768]{1,0:T(8,128)S(1)}, bf16[256,768]{1,0:T(8,128)(2,1)S(1)}, bf16[512,576]{1,0:T(8,128)(2,1)S(1)}, f32[8,768]{1,0:T(8,128)S(1)}, f32[8,576]{1,0:T(8,128)S(1)}) custom-call(bf16[256,768]{1,0:T(8,128)(2,1)S(1)} %get-tuple-element.110.grad_half, bf16[256,768]{1,0:T(8,128)(2,1)S(1)} %collective-permute-done.29.grad_other, ...), custom_call_target="tpu_custom_call" | custom-call | flops 1107296256 | bytes 5449728 | tf_op jit(solution)/shard_map/pallas_call | solution.py:31
  93.0 2.9 %shard_map.271 = (f32[768,768]{1,0:T(8,128)S(1)}, f32[8,768]{1,0:T(8,128)S(1)}) custom-call(bf16[256,768]{1,0:T(8,128)(2,1)S(1)} %get-tuple-element.110.grad_half, bf16[256,768]{1,0:T(8,128)(2,1)S(1)} %collective-permute-done.29.grad_other, bf16[512,192]{1,0:T(8,128)(2,1)S(1)} %get-tuple-element.86.mixed0.mixed, bf16[128,768]{1,0:T(8,128)(2,1)S(1)} %copy-done, ...), custom_call_target="tpu_custom_call" | custom-call | flops 603979776 | bytes 5673984 | tf_op jit(solution)/shard_map/pallas_call | solution.py:31
  98.4 3.9 %collective-permute-start.37 = (bf16[96,896]{1,0:T(8,128)(2,1)S(1)}, bf16[96,896]{1,0:T(8,128)(2,1)S(1)}, u32[]{:S(2)}, u32[]{:S(2)}) collective-permute-start(bf16[96,896]{1,0:T(8,128)(2,1)S(1)} %get-tuple-element.131), channel_id=1, source_target_pairs={{0,24},{4,28},{8,0},{12,4},{16,8},{20,12},{24,16},{28,20},{1,25},{... | collective-permute-start | bytes 516104 | tf_op jit(solution)/shard_map/ppermute | solution.py:83
  102.5 5.3 %collective-permute-done.43 = bf16[96,1536]{1,0:T(8,128)(2,1)S(1)} collective-permute-done((bf16[96,1536]{1,0:T(8,128)(2,1)S(1)}, bf16[96,1536]{1,0:T(8,128)(2,1)S(1)}, u32[]{:S(2)}, u32[]{:S(2)}) %collective-permute-start.43) | collective-permute-done | bytes 294944 | tf_op jit(solution)/shard_map/ppermute | solution.py:83
  111.5 1.7 %collective-permute-start.44 = (bf16[96,1536]{1,0:T(8,128)(2,1)S(1)}, bf16[96,1536]{1,0:T(8,128)(2,1)S(1)}, u32[]{:S(2)}, u32[]{:S(2)}) collective-permute-start(bf16[96,1536]{1,0:T(8,128)(2,1)S(1)} %add_convert_fusion.1), channel_id=1, source_target_pairs={{0,4},{4,0},{8,12},{12,8},{16,20},{20,16},{24,28},{28,24},{1,5},{5... | collective-permute-start | bytes 884744 | tf_op jit(solution)/shard_map/ppermute | solution.py:83
  113.2 4.5 %collective-permute-done.41 = bf16[96,896]{1,0:T(8,128)(2,1)S(1)} collective-permute-done((bf16[96,896]{1,0:T(8,128)(2,1)S(1)}, bf16[96,896]{1,0:T(8,128)(2,1)S(1)}, u32[]{:S(2)}, u32[]{:S(2)}) %collective-permute-start.41) | collective-permute-done | bytes 172064 | tf_op jit(solution)/shard_map/ppermute | solution.py:83
  117.7 2.2 %collective-permute-start.36 = (bf16[96,896]{1,0:T(8,128)(2,1)S(1)}, bf16[96,896]{1,0:T(8,128)(2,1)S(1)}, u32[]{:S(2)}, u32[]{:S(2)}) collective-permute-start(bf16[96,896]{1,0:T(8,128)(2,1)S(1)} %get-tuple-element.128), channel_id=1, source_target_pairs={{0,24},{4,28},{8,0},{12,4},{16,8},{20,12},{24,16},{28,20},{1,25},{... | collective-permute-start | bytes 516104 | tf_op jit(solution)/shard_map/ppermute | solution.py:83
  120.0 1.7 %collective-permute-done.39 = bf16[96,896]{1,0:T(8,128)(2,1)S(1)} collective-permute-done((bf16[96,896]{1,0:T(8,128)(2,1)S(1)}, bf16[96,896]{1,0:T(8,128)(2,1)S(1)}, u32[]{:S(2)}, u32[]{:S(2)}) %collective-permute-start.39) | collective-permute-done | bytes 172064 | tf_op jit(solution)/shard_map/ppermute | solution.py:83
  126.0 3.0 %collective-permute-done.42.refs_3_ = bf16[96,896]{1,0:T(8,128)(2,1)S(1)} collective-permute-done((bf16[96,896]{1,0:T(8,128)(2,1)S(1)}, bf16[96,896]{1,0:T(8,128)(2,1)S(1)}, u32[]{:S(2)}, u32[]{:S(2)}) %collective-permute-start.42) | collective-permute-done | bytes 172064 | tf_op jit(solution)/shard_map/ppermute | solution.py:83
  (116 shorter events, 37.8 us)
Async XLA Ops:
  2.8 10.6 %collective-permute-start.3 = (bf16[96,896]{1,0:T(8,128)(2,1)}, bf16[96,896]{1,0:T(8,128)(2,1)S(1)}, u32[]{:S(2)}, u32[]{:S(2)}) collective-permute-start(bf16[96,896]{1,0:T(8,128)(2,1)} %get-tuple-element.85.refs_0_), channel_id=1, source_target_pairs={{0,24},{4,28},{8,0},{12,4},{16,8},{20,12},{24,16},{28,20},{1,25},{... | collective-permute-start | bytes 516104 | tf_op jit(solution)/shard_map/ppermute | solution.py:83
  7.9 8.5 %collective-permute-start.4 = (bf16[96,896]{1,0:T(8,128)(2,1)}, bf16[96,896]{1,0:T(8,128)(2,1)}, u32[]{:S(2)}, u32[]{:S(2)}) collective-permute-start(bf16[96,896]{1,0:T(8,128)(2,1)} %get-tuple-element.85.refs_0_), channel_id=1, source_target_pairs={{0,8},{4,12},{8,16},{12,20},{16,24},{20,28},{24,0},{28,4},{1,9},{5... | collective-permute-start | bytes 516104 | tf_op jit(solution)/shard_map/ppermute | solution.py:83
  7.9 10.3 %collective-permute-start.7 = (bf16[96,896]{1,0:T(8,128)(2,1)}, bf16[96,896]{1,0:T(8,128)(2,1)S(1)}, u32[]{:S(2)}, u32[]{:S(2)}) collective-permute-start(bf16[96,896]{1,0:T(8,128)(2,1)} %get-tuple-element.85.refs_0_), channel_id=1, source_target_pairs={{0,4},{4,0},{8,12},{12,8},{16,20},{20,16},{24,28},{28,24},{1,5},{5... | collective-permute-start | bytes 516104 | tf_op jit(solution)/shard_map/ppermute | solution.py:83
  9.3 10.0 %collective-permute-start = (bf16[128,768]{1,0:T(8,128)(2,1)}, bf16[128,768]{1,0:T(8,128)(2,1)S(1)}, u32[]{:S(2)}, u32[]{:S(2)}) collective-permute-start(bf16[128,768]{1,0:T(8,128)(2,1)} %tok0.5), channel_id=1, source_target_pairs={{0,1},{1,0},{2,3},{3,2},{4,5},{5,4},{6,7},{7,6},{8,9},{9,8},{10,11... | collective-permute-start | bytes 589832 | tf_op jit(solution)/shard_map/ppermute | solution.py:78
  10.9 10.6 %collective-permute-start.17 = (bf16[96,1536]{1,0:T(8,128)(2,1)}, bf16[96,1536]{1,0:T(8,128)(2,1)}, u32[]{:S(2)}, u32[]{:S(2)}) collective-permute-start(bf16[96,1536]{1,0:T(8,128)(2,1)} %get-tuple-element.90.refs_0_), channel_id=1, source_target_pairs={{0,4},{4,0},{8,12},{12,8},{16,20},{20,16},{24,28},{28,24},{1,5},{5... | collective-permute-start | bytes 884744 | tf_op jit(solution)/shard_map/ppermute | solution.py:83
  18.8 13.0 %collective-permute-start.16 = (bf16[96,1536]{1,0:T(8,128)(2,1)}, bf16[96,1536]{1,0:T(8,128)(2,1)}, u32[]{:S(2)}, u32[]{:S(2)}) collective-permute-start(bf16[96,1536]{1,0:T(8,128)(2,1)} %get-tuple-element.90.refs_0_), channel_id=1, source_target_pairs={{0,24},{4,28},{8,0},{12,4},{16,8},{20,12},{24,16},{28,20},{1,25},{... | collective-permute-start | bytes 884744 | tf_op jit(solution)/shard_map/ppermute | solution.py:83
  21.4 8.7 %collective-permute-start.5 = (bf16[96,896]{1,0:T(8,128)(2,1)}, bf16[96,896]{1,0:T(8,128)(2,1)}, u32[]{:S(2)}, u32[]{:S(2)}) collective-permute-start(bf16[96,896]{1,0:T(8,128)(2,1)} %collective-permute-done.4.refs_3_), channel_id=1, source_target_pairs={{0,4},{4,0},{8,12},{12,8},{16,20},{20,16},{24,28},{28,24},{1,5},{5... | collective-permute-start | bytes 516104 | tf_op jit(solution)/shard_map/ppermute | solution.py:83
  21.5 12.5 %collective-permute-start.2 = (bf16[128,768]{1,0:T(8,128)(2,1)S(1)}, bf16[128,768]{1,0:T(8,128)(2,1)S(1)}, u32[]{:S(2)}, u32[]{:S(2)}) collective-permute-start(bf16[128,768]{1,0:T(8,128)(2,1)S(1)} %collective-permute-done.refs_10_.tok1), channel_id=1, source_target_pairs={{0,2},{2,0},{1,3},{3,1},{4,6},{6,4},{5,7},{7,5},{8,10},{10,8},{9,1... | collective-permute-start | bytes 589832 | tf_op jit(solution)/shard_map/ppermute | solution.py:78
  23.0 11.0 %collective-permute-start.9 = (bf16[96,896]{1,0:T(8,128)(2,1)}, bf16[96,896]{1,0:T(8,128)(2,1)}, u32[]{:S(2)}, u32[]{:S(2)}) collective-permute-start(bf16[96,896]{1,0:T(8,128)(2,1)} %collective-permute-done.8.refs_6_), channel_id=1, source_target_pairs={{0,4},{4,0},{8,12},{12,8},{16,20},{20,16},{24,28},{28,24},{1,5},{5... | collective-permute-start | bytes 516104 | tf_op jit(solution)/shard_map/ppermute | solution.py:83
  27.4 18.2 %collective-permute-start.19 = (bf16[96,1536]{1,0:T(8,128)(2,1)}, bf16[96,1536]{1,0:T(8,128)(2,1)}, u32[]{:S(2)}, u32[]{:S(2)}) collective-permute-start(bf16[96,1536]{1,0:T(8,128)(2,1)} %get-tuple-element.90.refs_0_), channel_id=1, source_target_pairs={{0,8},{4,12},{8,16},{12,20},{16,24},{20,28},{24,0},{28,4},{1,9},{5... | collective-permute-start | bytes 884744 | tf_op jit(solution)/shard_map/ppermute | solution.py:83
  30.1 19.1 %collective-permute-start.18 = (bf16[96,1536]{1,0:T(8,128)(2,1)}, bf16[96,1536]{1,0:T(8,128)(2,1)S(1)}, u32[]{:S(2)}, u32[]{:S(2)}) collective-permute-start(bf16[96,1536]{1,0:T(8,128)(2,1)} %collective-permute-done.17.refs_5_), channel_id=1, source_target_pairs={{0,8},{4,12},{8,16},{12,20},{16,24},{20,28},{24,0},{28,4},{1,9},{5... | collective-permute-start | bytes 884744 | tf_op jit(solution)/shard_map/ppermute | solution.py:83
  31.8 16.1 %collective-permute-start.21 = (bf16[96,1536]{1,0:T(8,128)(2,1)}, bf16[96,1536]{1,0:T(8,128)(2,1)S(1)}, u32[]{:S(2)}, u32[]{:S(2)}) collective-permute-start(bf16[96,1536]{1,0:T(8,128)(2,1)} %collective-permute-done.16.refs_1_), channel_id=1, source_target_pairs={{0,24},{4,28},{8,0},{12,4},{16,8},{20,12},{24,16},{28,20},{1,25},{... | collective-permute-start | bytes 884744 | tf_op jit(solution)/shard_map/ppermute | solution.py:83
  42.6 10.7 %collective-permute-start.13 = (bf16[768,192]{1,0:T(8,128)(2,1)S(1)}, bf16[768,192]{1,0:T(8,128)(2,1)S(1)}, u32[]{:S(2)}, u32[]{:S(2)}) collective-permute-start(bf16[768,192]{1,0:T(8,128)(2,1)S(1)} %get-tuple-element.88.wo0.wo), channel_id=1, source_target_pairs={{0,1},{1,0},{2,3},{3,2},{4,5},{5,4},{6,7},{7,6},{8,9},{9,8},{10,11... | collective-permute-start | bytes 884744 | tf_op jit(solution)/shard_map/ppermute | solution.py:78
  44.1 12.1 %collective-permute-start.20 = (bf16[96,1536]{1,0:T(8,128)(2,1)}, bf16[96,1536]{1,0:T(8,128)(2,1)S(1)}, u32[]{:S(2)}, u32[]{:S(2)}) collective-permute-start(bf16[96,1536]{1,0:T(8,128)(2,1)} %collective-permute-done.16.refs_1_), channel_id=1, source_target_pairs={{0,4},{4,0},{8,12},{12,8},{16,20},{20,16},{24,28},{28,24},{1,5},{5... | collective-permute-start | bytes 884744 | tf_op jit(solution)/shard_map/ppermute | solution.py:83
  45.6 10.6 %collective-permute-start.10 = (bf16[512,192]{1,0:T(8,128)(2,1)S(1)}, bf16[512,192]{1,0:T(8,128)(2,1)S(1)}, u32[]{:S(2)}, u32[]{:S(2)}) collective-permute-start(bf16[512,192]{1,0:T(8,128)(2,1)S(1)} %get-tuple-element.86.mixed0.mixed), channel_id=1, source_target_pairs={{0,1},{1,0},{2,3},{3,2},{4,5},{5,4},{6,7},{7,6},{8,9},{9,8},{10,11... | collective-permute-start | bytes 589832 | tf_op jit(solution)/shard_map/ppermute | solution.py:78
  48.0 9.3 %collective-permute-start.22 = (bf16[96,1536]{1,0:T(8,128)(2,1)S(1)}, bf16[96,1536]{1,0:T(8,128)(2,1)S(1)}, u32[]{:S(2)}, u32[]{:S(2)}) collective-permute-start(bf16[96,1536]{1,0:T(8,128)(2,1)S(1)} %collective-permute-done.21.refs_6_), channel_id=1, source_target_pairs={{0,4},{4,0},{8,12},{12,8},{16,20},{20,16},{24,28},{28,24},{1,5},{5... | collective-permute-start | bytes 884744 | tf_op jit(solution)/shard_map/ppermute | solution.py:83
  49.2 10.3 %collective-permute-start.14 = (bf16[768,192]{1,0:T(8,128)(2,1)S(1)}, bf16[768,192]{1,0:T(8,128)(2,1)S(1)}, u32[]{:S(2)}, u32[]{:S(2)}) collective-permute-start(bf16[768,192]{1,0:T(8,128)(2,1)S(1)} %get-tuple-element.88.wo0.wo), channel_id=1, source_target_pairs={{0,2},{2,0},{1,3},{3,1},{4,6},{6,4},{5,7},{7,5},{8,10},{10,8},{9,1... | collective-permute-start | bytes 884744 | tf_op jit(solution)/shard_map/ppermute | solution.py:78
  65.7 11.2 %collective-permute-start.26 = (bf16[256,768]{1,0:T(8,128)(2,1)S(1)}, bf16[256,768]{1,0:T(8,128)(2,1)S(1)}, u32[]{:S(2)}, u32[]{:S(2)}) collective-permute-start(bf16[256,768]{1,0:T(8,128)(2,1)S(1)} %get-tuple-element.156), channel_id=1, source_target_pairs={{0,1},{1,0},{2,3},{3,2},{4,5},{5,4},{6,7},{7,6},{8,9},{9,8},{10,11... | collective-permute-start | bytes 1179656 | tf_op jit(solution)/shard_map/ppermute | solution.py:78
  69.7 10.6 %collective-permute-start.28 = (bf16[96,1536]{1,0:T(8,128)(2,1)S(1)}, bf16[96,1536]{1,0:T(8,128)(2,1)S(1)}, u32[]{:S(2)}, u32[]{:S(2)}) collective-permute-start(bf16[96,1536]{1,0:T(8,128)(2,1)S(1)} %get-tuple-element.108), channel_id=1, source_target_pairs={{0,24},{4,28},{8,0},{12,4},{16,8},{20,12},{24,16},{28,20},{1,25},{... | collective-permute-start | bytes 884744 | tf_op jit(solution)/shard_map/ppermute | solution.py:83
  73.2 8.7 %collective-permute-start.27 = (bf16[96,1536]{1,0:T(8,128)(2,1)S(1)}, bf16[96,1536]{1,0:T(8,128)(2,1)S(1)}, u32[]{:S(2)}, u32[]{:S(2)}) collective-permute-start(bf16[96,1536]{1,0:T(8,128)(2,1)S(1)} %get-tuple-element.107), channel_id=1, source_target_pairs={{0,4},{4,0},{8,12},{12,8},{16,20},{20,16},{24,28},{28,24},{1,5},{5... | collective-permute-start | bytes 884744 | tf_op jit(solution)/shard_map/ppermute | solution.py:83
  82.7 14.9 %collective-permute-start.34 = (bf16[96,1536]{1,0:T(8,128)(2,1)S(1)}, bf16[96,1536]{1,0:T(8,128)(2,1)S(1)}, u32[]{:S(2)}, u32[]{:S(2)}) collective-permute-start(bf16[96,1536]{1,0:T(8,128)(2,1)S(1)} %get-tuple-element.124), channel_id=1, source_target_pairs={{0,4},{4,0},{8,12},{12,8},{16,20},{20,16},{24,28},{28,24},{1,5},{5... | collective-permute-start | bytes 884744 | tf_op jit(solution)/shard_map/ppermute | solution.py:83
  84.5 13.1 %collective-permute-start.35 = (bf16[96,1536]{1,0:T(8,128)(2,1)S(1)}, bf16[96,1536]{1,0:T(8,128)(2,1)S(1)}, u32[]{:S(2)}, u32[]{:S(2)}) collective-permute-start(bf16[96,1536]{1,0:T(8,128)(2,1)S(1)} %get-tuple-element.125), channel_id=1, source_target_pairs={{0,24},{4,28},{8,0},{12,4},{16,8},{20,12},{24,16},{28,20},{1,25},{... | collective-permute-start | bytes 884744 | tf_op jit(solution)/shard_map/ppermute | solution.py:83
  86.6 9.6 %collective-permute-start.24 = (bf16[256,768]{1,0:T(8,128)(2,1)S(1)}, bf16[256,768]{1,0:T(8,128)(2,1)S(1)}, u32[]{:S(2)}, u32[]{:S(2)}) collective-permute-start(bf16[256,768]{1,0:T(8,128)(2,1)S(1)} %get-tuple-element.104), channel_id=1, source_target_pairs={{0,2},{2,0},{1,3},{3,1},{4,6},{6,4},{5,7},{7,5},{8,10},{10,8},{9,1... | collective-permute-start | bytes 1179656 | tf_op jit(solution)/shard_map/ppermute | solution.py:78
  96.0 11.8 %collective-permute-start.43 = (bf16[96,1536]{1,0:T(8,128)(2,1)S(1)}, bf16[96,1536]{1,0:T(8,128)(2,1)S(1)}, u32[]{:S(2)}, u32[]{:S(2)}) collective-permute-start(bf16[96,1536]{1,0:T(8,128)(2,1)S(1)} %add_convert_fusion.2), channel_id=1, source_target_pairs={{0,8},{4,12},{8,16},{12,20},{16,24},{20,28},{24,0},{28,4},{1,9},{5... | collective-permute-start | bytes 884744 | tf_op jit(solution)/shard_map/ppermute | solution.py:83
  96.3 15.2 %collective-permute-start.25 = (bf16[128,768]{1,0:T(8,128)(2,1)S(1)}, bf16[128,768]{1,0:T(8,128)(2,1)S(1)}, u32[]{:S(2)}, u32[]{:S(2)}) collective-permute-start(bf16[128,768]{1,0:T(8,128)(2,1)S(1)} %slice.37), channel_id=1, source_target_pairs={{0,1},{1,0},{2,3},{3,2},{4,5},{5,4},{6,7},{7,6},{8,9},{9,8},{10,11... | collective-permute-start | bytes 589832 | tf_op jit(solution)/shard_map/ppermute | solution.py:78
  98.4 12.1 %collective-permute-start.37 = (bf16[96,896]{1,0:T(8,128)(2,1)S(1)}, bf16[96,896]{1,0:T(8,128)(2,1)S(1)}, u32[]{:S(2)}, u32[]{:S(2)}) collective-permute-start(bf16[96,896]{1,0:T(8,128)(2,1)S(1)} %get-tuple-element.131), channel_id=1, source_target_pairs={{0,24},{4,28},{8,0},{12,4},{16,8},{20,12},{24,16},{28,20},{1,25},{... | collective-permute-start | bytes 516104 | tf_op jit(solution)/shard_map/ppermute | solution.py:83
  102.2 8.6 %collective-permute-start.38 = (bf16[96,896]{1,0:T(8,128)(2,1)S(1)}, bf16[96,896]{1,0:T(8,128)(2,1)S(1)}, u32[]{:S(2)}, u32[]{:S(2)}) collective-permute-start(bf16[96,896]{1,0:T(8,128)(2,1)S(1)} %get-tuple-element.133), channel_id=1, source_target_pairs={{0,4},{4,0},{8,12},{12,8},{16,20},{20,16},{24,28},{28,24},{1,5},{5... | collective-permute-start | bytes 516104 | tf_op jit(solution)/shard_map/ppermute | solution.py:83
  107.9 14.8 %collective-permute-start.45 = (bf16[96,1536]{1,0:T(8,128)(2,1)S(1)}, bf16[96,1536]{1,0:T(8,128)(2,1)S(1)}, u32[]{:S(2)}, u32[]{:S(2)}) collective-permute-start(bf16[96,1536]{1,0:T(8,128)(2,1)S(1)} %add_convert_fusion), channel_id=1, source_target_pairs={{0,8},{4,12},{8,16},{12,20},{16,24},{20,28},{24,0},{28,4},{1,9},{5... | collective-permute-start | bytes 884744 | tf_op jit(solution)/shard_map/ppermute | solution.py:83
  108.0 11.9 %collective-permute-start.31 = (bf16[128,768]{1,0:T(8,128)(2,1)S(1)}, bf16[128,768]{1,0:T(8,128)(2,1)S(1)}, u32[]{:S(2)}, u32[]{:S(2)}) collective-permute-start(bf16[128,768]{1,0:T(8,128)(2,1)S(1)} %slice.36), channel_id=1, source_target_pairs={{0,1},{1,0},{2,3},{3,2},{4,5},{5,4},{6,7},{7,6},{8,9},{9,8},{10,11... | collective-permute-start | bytes 589832 | tf_op jit(solution)/shard_map/ppermute | solution.py:78
  110.9 10.8 %collective-permute-start.39 = (bf16[96,896]{1,0:T(8,128)(2,1)S(1)}, bf16[96,896]{1,0:T(8,128)(2,1)S(1)}, u32[]{:S(2)}, u32[]{:S(2)}) collective-permute-start(bf16[96,896]{1,0:T(8,128)(2,1)S(1)} %add_convert_fusion.5), channel_id=1, source_target_pairs={{0,8},{4,12},{8,16},{12,20},{16,24},{20,28},{24,0},{28,4},{1,9},{5... | collective-permute-start | bytes 516104 | tf_op jit(solution)/shard_map/ppermute | solution.py:83
  111.5 12.5 %collective-permute-start.44 = (bf16[96,1536]{1,0:T(8,128)(2,1)S(1)}, bf16[96,1536]{1,0:T(8,128)(2,1)S(1)}, u32[]{:S(2)}, u32[]{:S(2)}) collective-permute-start(bf16[96,1536]{1,0:T(8,128)(2,1)S(1)} %add_convert_fusion.1), channel_id=1, source_target_pairs={{0,4},{4,0},{8,12},{12,8},{16,20},{20,16},{24,28},{28,24},{1,5},{5... | collective-permute-start | bytes 884744 | tf_op jit(solution)/shard_map/ppermute | solution.py:83
  117.7 8.3 %collective-permute-start.36 = (bf16[96,896]{1,0:T(8,128)(2,1)S(1)}, bf16[96,896]{1,0:T(8,128)(2,1)S(1)}, u32[]{:S(2)}, u32[]{:S(2)}) collective-permute-start(bf16[96,896]{1,0:T(8,128)(2,1)S(1)} %get-tuple-element.128), channel_id=1, source_target_pairs={{0,24},{4,28},{8,0},{12,4},{16,8},{20,12},{24,16},{28,20},{1,25},{... | collective-permute-start | bytes 516104 | tf_op jit(solution)/shard_map/ppermute | solution.py:83
  (24 other events, 168.6 us)

commit v5 on v4

--- a/solution.py
+++ b/solution.py
@@ -12,7 +12,6 @@
 DIRECT_SIZE = 8
 STEPS = ((0, 0), (1, 0), (3, 1), (3, 0), (1, 1), (0, 1), (2, 0), (2, 1))
 VEC_COLS = 128
-FIRST_LIMIT = 40
 LOW = jnp.bfloat16
 F32 = jnp.float32
 GELU_SCALE = float(np.sqrt(2.0 / np.pi))
@@ -22,9 +21,9 @@
     return jax.ShapeDtypeStruct((rows, cols), dtype)
 
 
-def on_core(body, outs, scalars, arrays, scratch=(), flops=0, limit=40):
+def on_core(body, outs, scalars, arrays, scratch=(), flops=0, limit=40, far=0):
     specs = [pl.BlockSpec(memory_space=pltpu.SMEM)] * len(scalars)
-    specs += [pl.BlockSpec()] * len(arrays)
+    specs += [pl.BlockSpec(memory_space=pltpu.HBM)] * far + [pl.BlockSpec()] * (len(arrays) - far)
     moved = sum(int(np.prod(a.shape)) * a.dtype.itemsize for a in arrays) + sum(
         int(np.prod(o.shape)) * o.dtype.itemsize for o in outs
     )
@@ -142,77 +141,90 @@
     second[...] = jnp.concatenate([wfc[...], wproj[...]], axis=1)
 
 
-def open_second_body(size, scal, *refs):
+def open_second_body(size, *refs):
     pieces, (grad, wf, wp, da, cot) = refs[:size], refs[size:]
     chunk = pieces[-1].shape[0]
     cols = wf.shape[1]
     own = cot.shape[0] // 4
     for step, piece in enumerate(pieces):
-        place = pl.ds(row_start(scal[0], step, chunk) if size > 1 else 0, chunk)
+        place = pl.ds(row_start(lax.axis_index("fsdp"), step, chunk) if size > 1 else 0, chunk)
         wf[place, :] = piece[:, :cols]
         wp[place, :] = piece[:, cols:]
     for block in range(4):
-        start = pl.multiple_of((scal[1] ^ block) * own, own)
+        start = pl.multiple_of((core_place() ^ block) * own, own)
         cot[block * own : (block + 1) * own, :] = grad[pl.ds(start, own), :]
     da[...] = dot(cot[...], wp[...], 1, 0)
 
 
-def fill_mask(mask, doc_col, doc_row, pos_col, pos_row):
-    total = mask.shape[0]
-    for low in range(0, total, 128):
-        part = slice(low, low + 128)
-        seen = (doc_col[part, :] == doc_row[...]) & (pos_row[...] <= pos_col[part, :])
-        mask[part, :] = jnp.where(seen, 0.0, -1e30)
-
-
-def attend_body(size, scal, *refs):
+def prepare_body(tok0, tok1, tok2, tok3, doc_col, doc_row, pos_col, pos_row, scaled, mask):
+    part = tok0.shape[0]
+    for number, source in enumerate((tok0, tok1, tok2, tok3)):
+        here = slice(number * part, (number + 1) * part)
+        scaled[here, :] = norm_parts(source[...].astype(F32))[0]
+        seen = (doc_col[here, :] == doc_row[...]) & (pos_row[...] <= pos_col[here, :])
+        mask[here, :] = jnp.where(seen, 0.0, -1e30)
+
+
+def core_place():
+    return lax.axis_index("seq") * 2 + lax.axis_index("tensor")
+
+
+def halves(place, rows):
+    half = rows // 2
+    first = pl.multiple_of(lax.div(place, 2) * half, half)
+    return pl.ds(first, half), pl.ds(pl.multiple_of(half - first, half), half)
+
+
+def softmax(scores):
+    top = jnp.max(scores, axis=-1, keepdims=True)
+    raised = jnp.exp(scores - top)
+    total = jnp.sum(raised, axis=-1, keepdims=True)
+    return (raised * (1.0 / total)).astype(LOW), top + jnp.log(total)
+
+
+def attend_body(size, *refs):
     pieces, refs = refs[:size], refs[size:]
-    sel, tok0, tok1, tok2, tok3, doc_col, doc_row, pos_col, pos_row = refs[:9]
-    qkv, mixed, lse, wqkv, wo, rows, cols, normed, mask = refs[9:]
+    sel, scaled, mask = refs[:3]
+    qkv, mixed, lse, wqkv, wo, rows, opened, normed, arrived = refs[3:]
     chunk = pieces[0].shape[0]
     split = VEC_COLS + wqkv.shape[1]
     end = split + wo.shape[1]
+    copies = []
     for step, piece in enumerate(pieces):
-        place = pl.ds(row_start(scal[0], step, chunk) if size > 1 else 0, chunk)
-        value = piece[:, :end]
-        cols[place, :] = value[:, :VEC_COLS].astype(F32)
-        wqkv[place, :] = value[:, VEC_COLS:split]
-        wo[place, :] = value[:, split:]
-    wide = cols[...].T
+        place = pl.ds(row_start(lax.axis_index("fsdp"), step, chunk) if size > 1 else 0, chunk)
+        copies.append(pltpu.make_async_copy(piece, opened.at[place, :], arrived.at[step]))
+        copies[-1].start()
+    for copy in copies:
+        copy.wait()
+    wqkv[...] = opened[:, VEC_COLS:split]
+    wo[...] = opened[:, split:end]
+    wide = opened[:, :VEC_COLS].astype(F32).T
     rows[...] = wide[:8]
     spread = dot(wide[:16].astype(LOW), sel[...], 1, 0)
     col = lax.broadcasted_iota(jnp.int32, (1, qkv.shape[1]), 1)
     count = wo.shape[1]
     bias = jnp.where(col < count, spread[7:8], jnp.where(col >= 2 * count, spread[8:9], 0.0))
     total = qkv.shape[0]
-    part = tok0.shape[0]
-    gain, shift = wide[2:3], wide[3:4]
-    for number, source in enumerate((tok0, tok1, tok2, tok3)):
-        scaled, _ = norm_parts(source[...].astype(F32))
-        normed[number * part : (number + 1) * part, :] = (scaled * gain + shift).astype(LOW)
+    normed[...] = (scaled[...] * wide[2:3] + wide[3:4]).astype(LOW)
     qkv[...] = (dot(normed[...], wqkv[...], 1, 0) + bias).astype(LOW)
-    fill_mask(mask, doc_col, doc_row, pos_col, pos_row)
     width = qkv.shape[1] // 3
     heads = width // HEAD_DIM
-    step = total // 2
-    for low in range(0, total, step):
-        here = slice(low, low + step)
-        found, norms = [], []
-        for head in range(heads):
-            at = head * HEAD_DIM
-            query = qkv[here, at : at + HEAD_DIM]
-            key = qkv[:, width + at : width + at + HEAD_DIM]
-            value = qkv[:, 2 * width + at : 2 * width + at + HEAD_DIM]
-            scores = dot(query, key, 1, 1) * 0.125 + mask[here, :]
-            top = jnp.max(scores, axis=-1, keepdims=True)
-            raised = jnp.exp(scores - top)
-            total_raised = jnp.sum(raised, axis=-1, keepdims=True)
-            probs = (raised * (1.0 / total_raised)).astype(LOW)
-            found.append(dot(probs, value, 1, 0))
-            norms.append(top + jnp.log(total_raised))
-        mixed[here, :] = jnp.concatenate(found, axis=1).astype(LOW)
-        for head in range(heads):
-            lse[here, head : head + 1] = norms[head]
+    half = total // 2
+    found_low, found_high = [], []
+    low, high = halves(core_place(), total)
+    for head in range(heads):
+        at = head * HEAD_DIM
+        query_low, key_low, value_low = [qkv[low, n * width + at : n * width + at + HEAD_DIM] for n in range(3)]
+        query_high, key_high, value_high = [qkv[high, n * width + at : n * width + at + HEAD_DIM] for n in range(3)]
+        probs, norm = softmax(dot(query_low, key_low, 1, 1) * 0.125 + mask[:half, :half])
+        lse[:half, head : head + 1] = norm
+        found_low.append(dot(probs, value_low, 1, 0))
+        scores = jnp.concatenate([dot(query_high, key_low, 1, 1), dot(query_high, key_high, 1, 1)], axis=1)
+        probs, norm = softmax(scores * 0.125 + mask[half:, :])
+        lse[half:, head : head + 1] = norm
+        found_high.append(dot(probs[:, :half], value_low, 1, 0) + dot(probs[:, half:], value_high, 1, 0))
+    mixed[low, :] = jnp.concatenate(found_low, axis=1).astype(LOW)
+    mixed[high, :] = jnp.concatenate(found_high, axis=1).astype(LOW)
 
 
 def feed_body(
@@ -266,14 +278,14 @@
     return [shape(width // parts, cols, LOW if step else F32) for step in range(parts)]
 
 
-def feed_grad_body(scal, active, wp, normed, grad_hidden, cot, *refs):
+def feed_grad_body(active, wp, normed, grad_hidden, cot, *refs):
     keep, send, fc_sum = refs[:3]
     pieces, whole = refs[3:-1], refs[-1]
     half = keep.shape[0]
     cols = wp.shape[1]
     whole[:, :cols] = dot(normed[...], grad_hidden[...], 0, 0)
     whole[:, cols:] = dot(cot[...], active[...], 0, 0)
-    put_pieces(scal[0], pieces, [whole])
+    put_pieces(lax.axis_index("fsdp"), pieces, [whole])
     keep[...] = dot(active[:half, :], wp[...], 1, 1)
     send[...] = dot(active[half:, :], wp[...], 1, 1).astype(LOW)
     fc_sum[...] = jnp.sum(grad_hidden[...].astype(F32), axis=0, keepdims=True)
@@ -297,51 +309,47 @@
 
 
 def attend_back_body(
-    grad_half, grad_other, wo, wqkv, qkv, lse, tok0, tok1, tok2, tok3, early, doc_col, doc_row, pos_col, pos_row,
-    keep, send, grad_qkv, late, qkv_sum, mask,
+    grad_half, grad_other, wo, wqkv, qkv, lse, scaled, mask, early,
+    keep, send, grad_qkv, late, qkv_sum, grad_attn,
 ):
     total = qkv.shape[0]
     half = total // 2
-    toks = (tok0, tok1, tok2, tok3)
     width = qkv.shape[1] // 3
     heads = width // HEAD_DIM
-    fill_mask(mask, doc_col, doc_row, pos_col, pos_row)
-    grad_attn = [dot(g[...], wo[...], 1, 0).astype(LOW) for g in (grad_half, grad_other)]
-    query_grads = [[], []]
-    key_grads, value_grads = [], []
+    grad_attn[:half, :] = dot(grad_half[...], wo[...], 1, 0).astype(LOW)
+    grad_attn[half:, :] = dot(grad_other[...], wo[...], 1, 0).astype(LOW)
+    low, high = halves(core_place(), total)
+    found_low, found_high = [[], [], []], [[], [], []]
     for head in range(heads):
         at = head * HEAD_DIM
-        key = qkv[:, width + at : width + at + HEAD_DIM]
-        value = qkv[:, 2 * width + at : 2 * width + at + HEAD_DIM]
-        key_grad = value_grad = None
-        for number in range(2):
-            here = slice(number * half, (number + 1) * half)
-            query = qkv[here, at : at + HEAD_DIM]
-            grad = grad_attn[number][:, at : at + HEAD_DIM]
-            scores = dot(query, key, 1, 1) * 0.125 + mask[here, :]
-            probs = jnp.exp(scores - lse[here, head : head + 1])
-            grad_probs = dot(grad, value, 1, 1)
-            inner = jnp.sum(probs * grad_probs, axis=-1, keepdims=True)
-            grad_scores = (probs * (grad_probs - inner)).astype(LOW)
-            query_grads[number].append(dot(grad_scores, key, 1, 0) * 0.125)
-            more_key = dot(grad_scores, query, 0, 0)
-            more_value = dot(probs.astype(LOW), grad, 0, 0)
-            key_grad = more_key if key_grad is None else key_grad + more_key
-            value_grad = more_value if value_grad is None else value_grad + more_value
-        key_grads.append(key_grad * 0.125)
-        value_grads.append(value_grad)
-    for number in range(2):
-        here = slice(number * half, (number + 1) * half)
-        grad_qkv[here, :] = jnp.concatenate(
-            query_grads[number] + [k[here] for k in key_grads] + [v[here] for v in value_grads], axis=1
-        ).astype(LOW)
+        query_low, key_low, value_low = [qkv[low, n * width + at : n * width + at + HEAD_DIM] for n in range(3)]
+        query_high, key_high, value_high = [qkv[high, n * width + at : n * width + at + HEAD_DIM] for n in range(3)]
+        grad_low, grad_high = grad_attn[low, at : at + HEAD_DIM], grad_attn[high, at : at + HEAD_DIM]
+        scores = dot(query_low, key_low, 1, 1) * 0.125 + mask[:half, :half]
+        probs = jnp.exp(scores - lse[:half, head : head + 1])
+        grad_probs = dot(grad_low, value_low, 1, 1)
+        inner = jnp.sum(probs * grad_probs, axis=-1, keepdims=True)
+        first = (probs * (grad_probs - inner)).astype(LOW)
+        first_probs = probs.astype(LOW)
+        scores = jnp.concatenate([dot(query_high, key_low, 1, 1), dot(query_high, key_high, 1, 1)], axis=1)
+        probs = jnp.exp(scores * 0.125 + mask[half:, :] - lse[half:, head : head + 1])
+        grad_probs = jnp.concatenate([dot(grad_high, value_low, 1, 1), dot(grad_high, value_high, 1, 1)], axis=1)
+        inner = jnp.sum(probs * grad_probs, axis=-1, keepdims=True)
+        second = (probs * (grad_probs - inner)).astype(LOW)
+        second_probs = probs.astype(LOW)
+        found_low[0].append(dot(first, key_low, 1, 0) * 0.125)
+        found_high[0].append((dot(second[:, :half], key_low, 1, 0) + dot(second[:, half:], key_high, 1, 0)) * 0.125)
+        found_low[1].append((dot(first, query_low, 0, 0) + dot(second[:, :half], query_high, 0, 0)) * 0.125)
+        found_high[1].append(dot(second[:, half:], query_high, 0, 0) * 0.125)
+        found_low[2].append(dot(first_probs, grad_low, 0, 0) + dot(second_probs[:, :half], grad_high, 0, 0))
+        found_high[2].append(dot(second_probs[:, half:], grad_high, 0, 0))
+    grad_qkv[low, :] = jnp.concatenate(sum(found_low, []), axis=1).astype(LOW)
+    grad_qkv[high, :] = jnp.concatenate(sum(found_high, []), axis=1).astype(LOW)
     gain_sum = shift_sum = 0.0
     for number in range(2):
         here = slice(number * half, (number + 1) * half)
         back = dot(grad_qkv[here, :], wqkv[...], 1, 1)
-        source = jnp.concatenate([toks[2 * number][...], toks[2 * number + 1][...]], axis=0)
-        scaled, _ = norm_parts(source.astype(F32))
-        gain_sum += jnp.sum(back * scaled, axis=0, keepdims=True)
+        gain_sum += jnp.sum(back * scaled[here, :], axis=0, keepdims=True)
         shift_sum += jnp.sum(back, axis=0, keepdims=True)
         if number == 0:
             keep[...] = back
@@ -353,13 +361,10 @@
 
 
 def last_grad_body(
-    grad_half, grad_other, mixed, tok0, tok1, tok2, tok3, rows, grad_qkv, fc_sum, qkv_sum, sel, whole, lines, normed
+    grad_half, grad_other, mixed, scaled, rows, grad_qkv, fc_sum, qkv_sum, sel, whole, lines, normed
 ):
-    part = tok0.shape[0]
-    half = 2 * part
-    for number, source in enumerate((tok0, tok1, tok2, tok3)):
-        scaled, _ = norm_parts(source[...].astype(F32))
-        normed[number * part : (number + 1) * part, :] = (scaled * rows[2:3, :] + rows[3:4, :]).astype(LOW)
+    half = grad_half.shape[0]
+    normed[...] = (scaled[...] * rows[2:3, :] + rows[3:4, :]).astype(LOW)
     split = grad_qkv.shape[1]
     whole[:, :split] = dot(normed[...], grad_qkv[...], 0, 0)
     whole[:, split:] = dot(grad_half[...], mixed[:half, :], 0, 0) + dot(grad_other[...], mixed[half:, :], 0, 0)
@@ -375,12 +380,12 @@
     lines[...] = jnp.concatenate([fc_sum[...], placed[:7]], axis=0)
 
 
-def last_cut_body(scal, whole, late, lines, *refs):
+def last_cut_body(whole, late, lines, *refs):
     pieces, cols = refs[:-1], refs[-1]
     line = jnp.concatenate([late[:6, :], lines[:3, :]], axis=0)
     lack = jnp.zeros((VEC_COLS - line.shape[0], line.shape[1]), F32)
     cols[...] = jnp.concatenate([line, lack], axis=0).T
-    put_pieces(scal[0], pieces, [cols, whole])
+    put_pieces(lax.axis_index("fsdp"), pieces, [cols, whole])
 
 
 def input_body(keep, far, middle_grad, own, rows, out):
@@ -438,7 +443,6 @@
 ):
     size = lax.axis_size("fsdp")
     direct = size == DIRECT_SIZE
-    me = lax.axis_index("fsdp")
     chunk, hidden_cols = w_fc.shape
     own_rows, width = tokens.shape
     seq_rows = segments.shape[0]
@@ -446,8 +450,6 @@
     head_cols = w_out.shape[0]
     qkv_cols = 3 * head_cols
     qv_count = b_qv.shape[1]
-    place = lax.axis_index("seq") * 2 + lax.axis_index("tensor")
-    scal = jnp.stack([me, place]).astype(jnp.int32)
     parts = size if direct else 1
 
     near = swap(tokens, "tensor")
@@ -460,6 +462,16 @@
     row_number = lax.broadcasted_iota(jnp.int32, (width, qkv_cols), 0)
     sel = (row_number == jnp.asarray(source, jnp.int32)[None, :]).astype(LOW)
 
+    blocks = [lax.axis_index("tensor") ^ b for b in range(4)]
+    docs = jnp.concatenate([lax.dynamic_slice_in_dim(segments, b * own_rows, own_rows, 0) for b in blocks])
+    spots = jnp.concatenate([b * own_rows + jnp.arange(own_rows, dtype=jnp.int32) for b in blocks])
+    marks = [docs[:, None], docs[None, :], spots[:, None], spots[None, :]]
+    scaled_one, mask = on_core(
+        prepare_body,
+        [shape(seq_rows, width, F32), shape(seq_rows, seq_rows, F32)],
+        [],
+        [*toks, *marks],
+    )
     rows_shape = shape(8, width, F32)
     bias_shape = shape(8, qkv_cols, F32)
     if direct:
@@ -479,13 +491,6 @@
         second = jnp.concatenate([w_fc, w_proj.T], axis=1)
         firsts = [lax.all_gather(first, "fsdp", axis=0, tiled=True)]
         seconds = [lax.all_gather(second, "fsdp", axis=0, tiled=True)]
-        scal = scal * jnp.asarray([0, 1], jnp.int32)
-    blocks = [place ^ b for b in range(4)]
-    docs = jnp.concatenate([lax.dynamic_slice_in_dim(segments, b * own_rows, own_rows, 0) for b in blocks])
-    spots = jnp.concatenate([b * own_rows + jnp.arange(own_rows, dtype=jnp.int32) for b in blocks])
-    marks = [docs[:, None], docs[None, :], spots[:, None], spots[None, :]]
-
-    mask_scratch = pltpu.VMEM((seq_rows, seq_rows), F32)
     normed_scratch = pltpu.VMEM((seq_rows, width), LOW)
     qkv, mixed, lse, wqkv, wo, rows = on_core(
         functools.partial(attend_body, parts),
@@ -497,9 +502,14 @@
             shape(width, head_cols, LOW),
             rows_shape,
         ],
-        [scal],
-        [*firsts, sel, *toks, *marks],
-        [pltpu.VMEM((width, VEC_COLS), F32), normed_scratch, mask_scratch],
+        [],
+        [*firsts, sel, scaled_one, mask],
+        [
+            pltpu.VMEM((width, VEC_COLS + qkv_cols + head_cols), LOW),
+            normed_scratch,
+            pltpu.SemaphoreType.DMA((parts,)),
+        ],
+        far=parts,
         flops=2 * seq_rows * (width * qkv_cols + 2 * head_cols * seq_rows),
     )
     wo_near = swap(after(wo, mixed), "tensor")
@@ -516,7 +526,7 @@
             shape(seq_rows, hidden_cols, F32),
             shape(seq_rows, width, LOW),
         ],
-        [scal],
+        [],
         [*seconds, grad_out],
         flops=square,
     )
@@ -534,22 +544,22 @@
         [*toks, *mixeds, *wos, wf, rows, da],
         flops=3 * square,
     )
-    part_two = keep + swap(send, "seq").astype(F32)
-    far = swap(part_two.astype(LOW), "tensor")
+    from_core = swap(send, "seq")
 
     piece_cols = 2 * hidden_cols
     out_keep, out_send, fc_sum, *grad_ff = on_core(
         feed_grad_body,
         [shape(half, width, F32), shape(half, width, LOW), shape(1, hidden_cols, F32), *piece_shapes(parts, width, piece_cols)],
-        [scal],
-        [active, wp, normed_two, grad_hidden, after(cot, part_two)],
+        [],
+        [active, wp, normed_two, grad_hidden, cot],
         [pltpu.VMEM((width, piece_cols), F32)],
         flops=3 * square,
     )
     out_half = out_keep + swap(out_send, "seq").astype(F32)
     out_far = swap(out_half[own_rows:].astype(LOW), "tensor")
     result = (middle[:own_rows] + out_half[:own_rows] + out_far.astype(F32) + rows[1:2]).astype(LOW)
-    far = after(far, fc_sum)
+    part_two = keep + after(from_core, fc_sum).astype(F32)
+    far = swap(part_two.astype(LOW), "tensor")
     if direct:
         begun = sums_begin(grad_ff)
         far = after(far, begun[0], begun[2])
@@ -573,8 +583,8 @@
             bias_shape,
         ],
         [],
-        [grad_mid_half, grad_mid_other, wo, wqkv, qkv, lse, *toks, early, *marks],
-        [mask_scratch],
+        [grad_mid_half, grad_mid_other, wo, wqkv, qkv, lse, scaled_one, mask, early],
+        [pltpu.VMEM((seq_rows, head_cols), LOW)],
         flops=2 * seq_rows * (width * (qkv_cols + head_cols) + 5 * head_cols * seq_rows),
     )
     part_one = keep_one + swap(send_one, "seq").astype(F32)
@@ -591,7 +601,7 @@
         last_grad_body,
         [shape(width, qkv_cols + head_cols, F32), rows_shape],
         [],
-        [grad_mid_half, grad_mid_other, mixed, *toks, rows, grad_qkv, fc_sum, qkv_sum, sel],
+        [grad_mid_half, grad_mid_other, mixed, scaled_one, rows, grad_qkv, fc_sum, qkv_sum, sel],
         [normed_scratch],
         flops=2 * seq_rows * width * (qkv_cols + head_cols),
     )
@@ -603,7 +613,7 @@
     grad_last = on_core(
         last_cut_body,
         piece_shapes(parts, width, last_cols),
-        [scal],
+        [],
         [whole, late, lines],
         [pltpu.VMEM((width, VEC_COLS), F32)],
     )

time: 130 us -> 127 us (0.977)
  local copies, waits for them, and re-layouts: 6.03 us -> 2.87 us
  Pallas kernels: 28.7 us -> 26.2 us
  waiting for transfers between devices: 42.3 us -> 43.9 us
  starting transfers between devices: 48.8 us -> 50.1 us
    unnamed x20 -> x12, local copies, waits for them, and re-layouts: 4.76 us -> 1.6 us
    ppermute x28, waiting for transfers between devices: 31.7 us -> 34.7 us  [send(): return lax.ppermute(value, 'fsdp', pairs)]
    pallas_call x12 -> x13, Pallas kernels: 28.7 us -> 26.2 us  [on_core(): pl.pallas_call(body, out_shape=tuple(outs), in_specs=specs, out_specs=tup...]
    ppermute x18, waiting for transfers between devices: 10.6 us -> 9.12 us  [swap(): return lax.ppermute(value, axis, [(0, 1), (1, 0)])]
  transfers between devices with their start and end apart: 46 -> 46, of which waited for: 19 -> 18; matrix products, arithmetic and copies ran while one was open for 3% -> 3% of each run, Pallas kernels for 16% -> 14%
where the time goes in v5:
time: 127 us; the launch traced here: 126 us
  starting transfers between devices  50.1 us (39%)
  waiting for transfers between devices  43.9 us (35%)
  Pallas kernels  26.2 us (21%)
  local copies, waits for them, and re-layouts  2.87 us (2%)
  other arithmetic  2.46 us (2%)
    ppermute x28, starting transfers between devices, send(): return lax.ppermute(value, 'fsdp', pairs)  40.7 us
    ppermute x28, waiting for transfers between devices, send(): return lax.ppermute(value, 'fsdp', pairs)  34.7 us
    pallas_call x13, Pallas kernels, on_core(): pl.pallas_call(body, out_shape=tuple(outs), in_specs=specs, out_specs=tup...  26.2 us
    ppermute x18, starting transfers between devices, swap(): return lax.ppermute(value, axis, [(0, 1), (1, 0)])  9.4 us
    ppermute x18, waiting for transfers between devices, swap(): return lax.ppermute(value, axis, [(0, 1), (1, 0)])  9.12 us
  transfers between devices with their start and end apart: 46, of which 18 were waited for; matrix products, arithmetic and copies ran while one was open for 3% of the time, Pallas kernels for 14%

profile of v5, /device:TPU:0, one launch (start us, length us, event | category | flops | bytes accessed | tf_op | source)
XLA Modules:
  0.0 126.4 jit_solution(7046581887595136846)
XLA Ops:
  0.7 2.1 %shard_map.263 = (bf16[96,896]{1,0:T(8,128)(2,1)}, bf16[96,1536]{1,0:T(8,128)(2,1)}) custom-call(bf16[3,96,192]{2,1,0:T(8,128)(2,1)} %wqkv.1, bf16[192,96]{1,0:T(8,128)(2,1)} %wout.1, bf16[96,768]{1,0:T(8,128)(2,1)} %wfc.1, bf16[96,768]{1,0:T(8,128)(2,1)} %bitcast.17, bf16[2,24]{1,0:T(2,128)(2,1)} %bqv.1, bf16[96]{0:T(256)(128)(2,1)} %refs_0_.1, ...), custom_call_target="tpu_custom_call" | custom-call | bytes 910752 | tf_op jit(solution)/shard_map/pallas_call | solution.py:30
  2.8 5.0 %collective-permute-start.3 = (bf16[96,896]{1,0:T(8,128)(2,1)}, bf16[96,896]{1,0:T(8,128)(2,1)S(1)}, u32[]{:S(2)}, u32[]{:S(2)}) collective-permute-start(bf16[96,896]{1,0:T(8,128)(2,1)} %get-tuple-element.86.refs_0_), channel_id=1, source_target_pairs={{0,24},{4,28},{8,0},{12,4},{16,8},{20,12},{24,16},{28,20},{1,25},{... | collective-permute-start | bytes 516104 | tf_op jit(solution)/shard_map/ppermute | solution.py:82
  7.9 1.5 %collective-permute-start.7 = (bf16[96,896]{1,0:T(8,128)(2,1)}, bf16[96,896]{1,0:T(8,128)(2,1)S(1)}, u32[]{:S(2)}, u32[]{:S(2)}) collective-permute-start(bf16[96,896]{1,0:T(8,128)(2,1)} %get-tuple-element.86.refs_0_), channel_id=1, source_target_pairs={{0,4},{4,0},{8,12},{12,8},{16,20},{20,16},{24,28},{28,24},{1,5},{5... | collective-permute-start | bytes 516104 | tf_op jit(solution)/shard_map/ppermute | solution.py:82
  9.3 1.5 %collective-permute-start = (bf16[128,768]{1,0:T(8,128)(2,1)}, bf16[128,768]{1,0:T(8,128)(2,1)S(1)}, u32[]{:S(2)}, u32[]{:S(2)}) collective-permute-start(bf16[128,768]{1,0:T(8,128)(2,1)} %own.1), channel_id=1, source_target_pairs={{0,1},{1,0},{2,3},{3,2},{4,5},{5,4},{6,7},{7,6},{8,9},{9,8},{10,11... | collective-permute-start | bytes 589832 | tf_op jit(solution)/shard_map/ppermute | solution.py:77
  13.4 3.0 %collective-permute-done.4.refs_3_ = bf16[96,896]{1,0:T(8,128)(2,1)} collective-permute-done((bf16[96,896]{1,0:T(8,128)(2,1)}, bf16[96,896]{1,0:T(8,128)(2,1)}, u32[]{:S(2)}, u32[]{:S(2)}) %collective-permute-start.4) | collective-permute-done | bytes 172064 | tf_op jit(solution)/shard_map/ppermute | solution.py:82
  16.4 1.7 %collective-permute-start.8 = (bf16[96,896]{1,0:T(8,128)(2,1)S(1)}, bf16[96,896]{1,0:T(8,128)(2,1)}, u32[]{:S(2)}, u32[]{:S(2)}) collective-permute-start(bf16[96,896]{1,0:T(8,128)(2,1)S(1)} %collective-permute-done.3.refs_1_), channel_id=1, source_target_pairs={{0,24},{4,28},{8,0},{12,4},{16,8},{20,12},{24,16},{28,20},{1,25},{... | collective-permute-start | bytes 516104 | tf_op jit(solution)/shard_map/ppermute | solution.py:82
  19.4 2.0 %collective-permute-start.6 = (bf16[96,896]{1,0:T(8,128)(2,1)S(1)}, bf16[96,896]{1,0:T(8,128)(2,1)}, u32[]{:S(2)}, u32[]{:S(2)}) collective-permute-start(bf16[96,896]{1,0:T(8,128)(2,1)S(1)} %collective-permute-done.3.refs_1_), channel_id=1, source_target_pairs={{0,4},{4,0},{8,12},{12,8},{16,20},{20,16},{24,28},{28,24},{1,5},{5... | collective-permute-start | bytes 516104 | tf_op jit(solution)/shard_map/ppermute | solution.py:82
  23.0 1.5 %collective-permute-start.9 = (bf16[96,896]{1,0:T(8,128)(2,1)}, bf16[96,896]{1,0:T(8,128)(2,1)}, u32[]{:S(2)}, u32[]{:S(2)}) collective-permute-start(bf16[96,896]{1,0:T(8,128)(2,1)} %collective-permute-done.8.refs_6_), channel_id=1, source_target_pairs={{0,4},{4,0},{8,12},{12,8},{16,20},{20,16},{24,28},{28,24},{1,5},{5... | collective-permute-start | bytes 516104 | tf_op jit(solution)/shard_map/ppermute | solution.py:82
  24.5 2.4 %collective-permute-start.19 = (bf16[96,1536]{1,0:T(8,128)(2,1)}, bf16[96,1536]{1,0:T(8,128)(2,1)S(1)}, u32[]{:S(2)}, u32[]{:S(2)}) collective-permute-start(bf16[96,1536]{1,0:T(8,128)(2,1)} %get-tuple-element.93.refs_0_), channel_id=1, source_target_pairs={{0,8},{4,12},{8,16},{12,20},{16,24},{20,28},{24,0},{28,4},{1,9},{5... | collective-permute-start | bytes 884744 | tf_op jit(solution)/shard_map/ppermute | solution.py:82
  29.4 4.2 %collective-permute-start.21 = (bf16[96,1536]{1,0:T(8,128)(2,1)S(1)}, bf16[96,1536]{1,0:T(8,128)(2,1)S(1)}, u32[]{:S(2)}, u32[]{:S(2)}) collective-permute-start(bf16[96,1536]{1,0:T(8,128)(2,1)S(1)} %collective-permute-done.16.refs_1_), channel_id=1, source_target_pairs={{0,24},{4,28},{8,0},{12,4},{16,8},{20,12},{24,16},{28,20},{1,25},{... | collective-permute-start | bytes 884744 | tf_op jit(solution)/shard_map/ppermute | solution.py:82
  34.8 5.6 %shard_map.265 = (bf16[512,576]{1,0:T(8,128)(2,1)S(1)}, bf16[512,192]{1,0:T(8,128)(2,1)S(1)}, f32[512,128]{1,0:T(8,128)S(1)}, bf16[768,576]{1,0:T(8,128)(2,1)S(1...) custom-call(bf16[96,896]{1,0:T(8,128)(2,1)S(1)} %copy-done.3, bf16[96,896]{1,0:T(8,128)(2,1)S(1)} %collective-permute-done.3.refs_1_, ...), custom_call_target="tpu_custom_call" | custom-call | flops 654311424 | bytes 7135232 | tf_op jit(solution)/shard_map/pallas_call | solution.py:30
  40.4 1.9 %collective-permute-start.13 = (bf16[768,192]{1,0:T(8,128)(2,1)S(1)}, bf16[768,192]{1,0:T(8,128)(2,1)S(1)}, u32[]{:S(2)}, u32[]{:S(2)}) collective-permute-start(bf16[768,192]{1,0:T(8,128)(2,1)S(1)} %get-tuple-element.91.wo0.wo), channel_id=1, source_target_pairs={{0,1},{1,0},{2,3},{3,2},{4,5},{5,4},{6,7},{7,6},{8,9},{9,8},{10,11... | collective-permute-start | bytes 884744 | tf_op jit(solution)/shard_map/ppermute | solution.py:77
  44.3 3.4 %collective-permute-done.21.refs_6_ = bf16[96,1536]{1,0:T(8,128)(2,1)S(1)} collective-permute-done((bf16[96,1536]{1,0:T(8,128)(2,1)S(1)}, bf16[96,1536]{1,0:T(8,128)(2,1)S(1)}, u32[]{:S(2)}, u32[]{:S(2)}) %collective-permute-start.21) | collective-permute-done | bytes 294944 | tf_op jit(solution)/shard_map/ppermute | solution.py:82
  49.1 3.3 %collective-permute-done.13.wo1 = bf16[768,192]{1,0:T(8,128)(2,1)S(1)} collective-permute-done((bf16[768,192]{1,0:T(8,128)(2,1)S(1)}, bf16[768,192]{1,0:T(8,128)(2,1)S(1)}, u32[]{:S(2)}, u32[]{:S(2)}) %collective-permute-start.13) | collective-permute-done | bytes 294944 | tf_op jit(solution)/shard_map/ppermute | solution.py:77
  52.5 4.5 %collective-permute-done.10.mixed1 = bf16[512,192]{1,0:T(8,128)(2,1)S(1)} collective-permute-done((bf16[512,192]{1,0:T(8,128)(2,1)S(1)}, bf16[512,192]{1,0:T(8,128)(2,1)S(1)}, u32[]{:S(2)}, u32[]{:S(2)}) %collective-permute-start.10) | collective-permute-done | bytes 196640 | tf_op jit(solution)/shard_map/ppermute | solution.py:77
  58.8 4.3 %shard_map.267 = (f32[256,768]{1,0:T(8,128)S(1)}, bf16[256,768]{1,0:T(8,128)(2,1)S(1)}, f32[256,768]{1,0:T(8,128)S(1)}, bf16[512,768]{1,0:T(8,128)(2,1)S(1)}, bf...) custom-call(bf16[128,768]{1,0:T(8,128)(2,1)S(1)} %copy-done.1, bf16[128,768]{1,0:T(8,128)(2,1)S(1)} %collective-permute-done.tok1, ...), custom_call_target="tpu_custom_call" | custom-call | flops 1811939328 | bytes 9854976 | tf_op jit(solution)/shard_map/pallas_call | solution.py:30
  63.4 2.3 %shard_map.268 = (f32[256,768]{1,0:T(8,128)S(1)}, bf16[256,768]{1,0:T(8,128)(2,1)S(1)}, f32[1,768]{1,0:T(1,128)S(1)}, f32[96,1536]{1,0:T(8,128)S(1)}, bf16[96,15...) custom-call(bf16[512,768]{1,0:T(8,128)(2,1)S(1)} %get-tuple-element., ...), custom_call_target="tpu_custom_call" | custom-call | flops 1811939328 | bytes 8162304 | tf_op jit(solution)/shard_map/pallas_call | solution.py:30
  65.8 1.7 %collective-permute-start.26 = (bf16[256,768]{1,0:T(8,128)(2,1)S(1)}, bf16[256,768]{1,0:T(8,128)(2,1)S(1)}, u32[]{:S(2)}, u32[]{:S(2)}) collective-permute-start(bf16[256,768]{1,0:T(8,128)(2,1)S(1)} %get-tuple-element.158), channel_id=1, source_target_pairs={{0,1},{1,0},{2,3},{3,2},{4,5},{5,4},{6,7},{7,6},{8,9},{9,8},{10,11... | collective-permute-start | bytes 1179656 | tf_op jit(solution)/shard_map/ppermute | solution.py:77
  67.5 3.7 %collective-permute-start.28 = (bf16[96,1536]{1,0:T(8,128)(2,1)S(1)}, bf16[96,1536]{1,0:T(8,128)(2,1)S(1)}, u32[]{:S(2)}, u32[]{:S(2)}) collective-permute-start(bf16[96,1536]{1,0:T(8,128)(2,1)S(1)} %get-tuple-element.110), channel_id=1, source_target_pairs={{0,24},{4,28},{8,0},{12,4},{16,8},{20,12},{24,16},{28,20},{1,25},{... | collective-permute-start | bytes 884744 | tf_op jit(solution)/shard_map/ppermute | solution.py:82
  72.7 5.2 %collective-permute-done.28 = bf16[96,1536]{1,0:T(8,128)(2,1)S(1)} collective-permute-done((bf16[96,1536]{1,0:T(8,128)(2,1)S(1)}, bf16[96,1536]{1,0:T(8,128)(2,1)S(1)}, u32[]{:S(2)}, u32[]{:S(2)}) %collective-permute-start.28) | collective-permute-done | bytes 294944 | tf_op jit(solution)/shard_map/ppermute | solution.py:82
  77.8 2.2 %collective-permute-done.27 = bf16[96,1536]{1,0:T(8,128)(2,1)S(1)} collective-permute-done((bf16[96,1536]{1,0:T(8,128)(2,1)S(1)}, bf16[96,1536]{1,0:T(8,128)(2,1)S(1)}, u32[]{:S(2)}, u32[]{:S(2)}) %collective-permute-start.27) | collective-permute-done | bytes 294944 | tf_op jit(solution)/shard_map/ppermute | solution.py:82
  80.8 1.5 %collective-permute-start.34 = (bf16[96,1536]{1,0:T(8,128)(2,1)S(1)}, bf16[96,1536]{1,0:T(8,128)(2,1)S(1)}, u32[]{:S(2)}, u32[]{:S(2)}) collective-permute-start(bf16[96,1536]{1,0:T(8,128)(2,1)S(1)} %get-tuple-element.126), channel_id=1, source_target_pairs={{0,4},{4,0},{8,12},{12,8},{16,20},{20,16},{24,28},{28,24},{1,5},{5... | collective-permute-start | bytes 884744 | tf_op jit(solution)/shard_map/ppermute | solution.py:82
  82.3 2.1 %collective-permute-start.35 = (bf16[96,1536]{1,0:T(8,128)(2,1)S(1)}, bf16[96,1536]{1,0:T(8,128)(2,1)S(1)}, u32[]{:S(2)}, u32[]{:S(2)}) collective-permute-start(bf16[96,1536]{1,0:T(8,128)(2,1)S(1)} %get-tuple-element.127), channel_id=1, source_target_pairs={{0,24},{4,28},{8,0},{12,4},{16,8},{20,12},{24,16},{28,20},{1,25},{... | collective-permute-start | bytes 884744 | tf_op jit(solution)/shard_map/ppermute | solution.py:82
  84.4 3.9 %shard_map.270 = (f32[256,768]{1,0:T(8,128)S(1)}, bf16[256,768]{1,0:T(8,128)(2,1)S(1)}, bf16[512,576]{1,0:T(8,128)(2,1)S(1)}, f32[8,768]{1,0:T(8,128)S(1)}, f32[8,576]{1,0:T(8,128)S(1)}) custom-call(bf16[256,768]{1,0:T(8,128)(2,1)S(1)} %get-tuple-element.112.grad_half, bf16[256,768]{1,0:T(8,128)(2,1)S(1)} %collective-permute-done.29.grad_other, ...), custom_call_target="tpu_custom_call" | custom-call | flops 1107296256 | bytes 7276544 | tf_op jit(solution)/shard_map/pallas_call | solution.py:30
  89.7 2.5 %shard_map.272 = (f32[768,768]{1,0:T(8,128)S(1)}, f32[8,768]{1,0:T(8,128)S(1)}) custom-call(bf16[256,768]{1,0:T(8,128)(2,1)S(1)} %get-tuple-element.112.grad_half, bf16[256,768]{1,0:T(8,128)(2,1)S(1)} %collective-permute-done.29.grad_other, bf16[512,192]{1,0:T(8,128)(2,1)S(1)} %get-tuple-element.89.mixed0.mixed, ...), custom_call_target="tpu_custom_call" | custom-call | flops 603979776 | bytes 6460416 | tf_op jit(solution)/shard_map/pallas_call | solution.py:30
  94.5 3.9 %collective-permute-start.37 = (bf16[96,896]{1,0:T(8,128)(2,1)S(1)}, bf16[96,896]{1,0:T(8,128)(2,1)S(1)}, u32[]{:S(2)}, u32[]{:S(2)}) collective-permute-start(bf16[96,896]{1,0:T(8,128)(2,1)S(1)} %get-tuple-element.133), channel_id=1, source_target_pairs={{0,24},{4,28},{8,0},{12,4},{16,8},{20,12},{24,16},{28,20},{1,25},{... | collective-permute-start | bytes 516104 | tf_op jit(solution)/shard_map/ppermute | solution.py:82
  98.9 5.6 %collective-permute-done.43 = bf16[96,1536]{1,0:T(8,128)(2,1)S(1)} collective-permute-done((bf16[96,1536]{1,0:T(8,128)(2,1)S(1)}, bf16[96,1536]{1,0:T(8,128)(2,1)S(1)}, u32[]{:S(2)}, u32[]{:S(2)}) %collective-permute-start.43) | collective-permute-done | bytes 294944 | tf_op jit(solution)/shard_map/ppermute | solution.py:82
  105.6 1.6 %collective-permute-done.37 = bf16[96,896]{1,0:T(8,128)(2,1)S(1)} collective-permute-done((bf16[96,896]{1,0:T(8,128)(2,1)S(1)}, bf16[96,896]{1,0:T(8,128)(2,1)S(1)}, u32[]{:S(2)}, u32[]{:S(2)}) %collective-permute-start.37) | collective-permute-done | bytes 172064 | tf_op jit(solution)/shard_map/ppermute | solution.py:82
  108.5 1.5 %collective-permute-start.44 = (bf16[96,1536]{1,0:T(8,128)(2,1)S(1)}, bf16[96,1536]{1,0:T(8,128)(2,1)S(1)}, u32[]{:S(2)}, u32[]{:S(2)}) collective-permute-start(bf16[96,1536]{1,0:T(8,128)(2,1)S(1)} %add_convert_fusion.1), channel_id=1, source_target_pairs={{0,4},{4,0},{8,12},{12,8},{16,20},{20,16},{24,28},{28,24},{1,5},{5... | collective-permute-start | bytes 884744 | tf_op jit(solution)/shard_map/ppermute | solution.py:82
  110.0 4.4 %collective-permute-done.41 = bf16[96,896]{1,0:T(8,128)(2,1)S(1)} collective-permute-done((bf16[96,896]{1,0:T(8,128)(2,1)S(1)}, bf16[96,896]{1,0:T(8,128)(2,1)S(1)}, u32[]{:S(2)}, u32[]{:S(2)}) %collective-permute-start.41) | collective-permute-done | bytes 172064 | tf_op jit(solution)/shard_map/ppermute | solution.py:82
  115.8 2.4 %collective-permute-done.39 = bf16[96,896]{1,0:T(8,128)(2,1)S(1)} collective-permute-done((bf16[96,896]{1,0:T(8,128)(2,1)S(1)}, bf16[96,896]{1,0:T(8,128)(2,1)S(1)}, u32[]{:S(2)}, u32[]{:S(2)}) %collective-permute-start.39) | collective-permute-done | bytes 172064 | tf_op jit(solution)/shard_map/ppermute | solution.py:82
  122.7 2.8 %collective-permute-done.42.refs_3_ = bf16[96,896]{1,0:T(8,128)(2,1)S(1)} collective-permute-done((bf16[96,896]{1,0:T(8,128)(2,1)S(1)}, bf16[96,896]{1,0:T(8,128)(2,1)S(1)}, u32[]{:S(2)}, u32[]{:S(2)}) %collective-permute-start.42) | collective-permute-done | bytes 172064 | tf_op jit(solution)/shard_map/ppermute | solution.py:82
  (108 shorter events, 30.1 us)
Async XLA Ops:
  2.8 10.6 %collective-permute-start.3 = (bf16[96,896]{1,0:T(8,128)(2,1)}, bf16[96,896]{1,0:T(8,128)(2,1)S(1)}, u32[]{:S(2)}, u32[]{:S(2)}) collective-permute-start(bf16[96,896]{1,0:T(8,128)(2,1)} %get-tuple-element.86.refs_0_), channel_id=1, source_target_pairs={{0,24},{4,28},{8,0},{12,4},{16,8},{20,12},{24,16},{28,20},{1,25},{... | collective-permute-start | bytes 516104 | tf_op jit(solution)/shard_map/ppermute | solution.py:82
  7.9 8.5 %collective-permute-start.4 = (bf16[96,896]{1,0:T(8,128)(2,1)}, bf16[96,896]{1,0:T(8,128)(2,1)}, u32[]{:S(2)}, u32[]{:S(2)}) collective-permute-start(bf16[96,896]{1,0:T(8,128)(2,1)} %get-tuple-element.86.refs_0_), channel_id=1, source_target_pairs={{0,8},{4,12},{8,16},{12,20},{16,24},{20,28},{24,0},{28,4},{1,9},{5... | collective-permute-start | bytes 516104 | tf_op jit(solution)/shard_map/ppermute | solution.py:82
  7.9 10.3 %collective-permute-start.7 = (bf16[96,896]{1,0:T(8,128)(2,1)}, bf16[96,896]{1,0:T(8,128)(2,1)S(1)}, u32[]{:S(2)}, u32[]{:S(2)}) collective-permute-start(bf16[96,896]{1,0:T(8,128)(2,1)} %get-tuple-element.86.refs_0_), channel_id=1, source_target_pairs={{0,4},{4,0},{8,12},{12,8},{16,20},{20,16},{24,28},{28,24},{1,5},{5... | collective-permute-start | bytes 516104 | tf_op jit(solution)/shard_map/ppermute | solution.py:82
  9.3 10.0 %collective-permute-start = (bf16[128,768]{1,0:T(8,128)(2,1)}, bf16[128,768]{1,0:T(8,128)(2,1)S(1)}, u32[]{:S(2)}, u32[]{:S(2)}) collective-permute-start(bf16[128,768]{1,0:T(8,128)(2,1)} %own.1), channel_id=1, source_target_pairs={{0,1},{1,0},{2,3},{3,2},{4,5},{5,4},{6,7},{7,6},{8,9},{9,8},{10,11... | collective-permute-start | bytes 589832 | tf_op jit(solution)/shard_map/ppermute | solution.py:77
  10.9 10.6 %collective-permute-start.17 = (bf16[96,1536]{1,0:T(8,128)(2,1)}, bf16[96,1536]{1,0:T(8,128)(2,1)S(1)}, u32[]{:S(2)}, u32[]{:S(2)}) collective-permute-start(bf16[96,1536]{1,0:T(8,128)(2,1)} %get-tuple-element.93.refs_0_), channel_id=1, source_target_pairs={{0,4},{4,0},{8,12},{12,8},{16,20},{20,16},{24,28},{28,24},{1,5},{5... | collective-permute-start | bytes 884744 | tf_op jit(solution)/shard_map/ppermute | solution.py:82
  18.8 10.6 %collective-permute-start.16 = (bf16[96,1536]{1,0:T(8,128)(2,1)}, bf16[96,1536]{1,0:T(8,128)(2,1)S(1)}, u32[]{:S(2)}, u32[]{:S(2)}) collective-permute-start(bf16[96,1536]{1,0:T(8,128)(2,1)} %get-tuple-element.93.refs_0_), channel_id=1, source_target_pairs={{0,24},{4,28},{8,0},{12,4},{16,8},{20,12},{24,16},{28,20},{1,25},{... | collective-permute-start | bytes 884744 | tf_op jit(solution)/shard_map/ppermute | solution.py:82
  19.4 8.6 %collective-permute-start.6 = (bf16[96,896]{1,0:T(8,128)(2,1)S(1)}, bf16[96,896]{1,0:T(8,128)(2,1)}, u32[]{:S(2)}, u32[]{:S(2)}) collective-permute-start(bf16[96,896]{1,0:T(8,128)(2,1)S(1)} %collective-permute-done.3.refs_1_), channel_id=1, source_target_pairs={{0,4},{4,0},{8,12},{12,8},{16,20},{20,16},{24,28},{28,24},{1,5},{5... | collective-permute-start | bytes 516104 | tf_op jit(solution)/shard_map/ppermute | solution.py:82
  21.5 12.2 %collective-permute-start.5 = (bf16[96,896]{1,0:T(8,128)(2,1)}, bf16[96,896]{1,0:T(8,128)(2,1)}, u32[]{:S(2)}, u32[]{:S(2)}) collective-permute-start(bf16[96,896]{1,0:T(8,128)(2,1)} %collective-permute-done.4.refs_3_), channel_id=1, source_target_pairs={{0,4},{4,0},{8,12},{12,8},{16,20},{20,16},{24,28},{28,24},{1,5},{5... | collective-permute-start | bytes 516104 | tf_op jit(solution)/shard_map/ppermute | solution.py:82
  23.0 10.9 %collective-permute-start.9 = (bf16[96,896]{1,0:T(8,128)(2,1)}, bf16[96,896]{1,0:T(8,128)(2,1)}, u32[]{:S(2)}, u32[]{:S(2)}) collective-permute-start(bf16[96,896]{1,0:T(8,128)(2,1)} %collective-permute-done.8.refs_6_), channel_id=1, source_target_pairs={{0,4},{4,0},{8,12},{12,8},{16,20},{20,16},{24,28},{28,24},{1,5},{5... | collective-permute-start | bytes 516104 | tf_op jit(solution)/shard_map/ppermute | solution.py:82
  24.5 19.3 %collective-permute-start.19 = (bf16[96,1536]{1,0:T(8,128)(2,1)}, bf16[96,1536]{1,0:T(8,128)(2,1)S(1)}, u32[]{:S(2)}, u32[]{:S(2)}) collective-permute-start(bf16[96,1536]{1,0:T(8,128)(2,1)} %get-tuple-element.93.refs_0_), channel_id=1, source_target_pairs={{0,8},{4,12},{8,16},{12,20},{16,24},{20,28},{24,0},{28,4},{1,9},{5... | collective-permute-start | bytes 884744 | tf_op jit(solution)/shard_map/ppermute | solution.py:82
  28.0 21.1 %collective-permute-start.18 = (bf16[96,1536]{1,0:T(8,128)(2,1)S(1)}, bf16[96,1536]{1,0:T(8,128)(2,1)S(1)}, u32[]{:S(2)}, u32[]{:S(2)}) collective-permute-start(bf16[96,1536]{1,0:T(8,128)(2,1)S(1)} %collective-permute-done.17.refs_5_), channel_id=1, source_target_pairs={{0,8},{4,12},{8,16},{12,20},{16,24},{20,28},{24,0},{28,4},{1,9},{5... | collective-permute-start | bytes 884744 | tf_op jit(solution)/shard_map/ppermute | solution.py:82
  29.4 18.2 %collective-permute-start.21 = (bf16[96,1536]{1,0:T(8,128)(2,1)S(1)}, bf16[96,1536]{1,0:T(8,128)(2,1)S(1)}, u32[]{:S(2)}, u32[]{:S(2)}) collective-permute-start(bf16[96,1536]{1,0:T(8,128)(2,1)S(1)} %collective-permute-done.16.refs_1_), channel_id=1, source_target_pairs={{0,24},{4,28},{8,0},{12,4},{16,8},{20,12},{24,16},{28,20},{1,25},{... | collective-permute-start | bytes 884744 | tf_op jit(solution)/shard_map/ppermute | solution.py:82
  40.4 12.1 %collective-permute-start.13 = (bf16[768,192]{1,0:T(8,128)(2,1)S(1)}, bf16[768,192]{1,0:T(8,128)(2,1)S(1)}, u32[]{:S(2)}, u32[]{:S(2)}) collective-permute-start(bf16[768,192]{1,0:T(8,128)(2,1)S(1)} %get-tuple-element.91.wo0.wo), channel_id=1, source_target_pairs={{0,1},{1,0},{2,3},{3,2},{4,5},{5,4},{6,7},{7,6},{8,9},{9,8},{10,11... | collective-permute-start | bytes 884744 | tf_op jit(solution)/shard_map/ppermute | solution.py:77
  42.3 14.7 %collective-permute-start.20 = (bf16[96,1536]{1,0:T(8,128)(2,1)S(1)}, bf16[96,1536]{1,0:T(8,128)(2,1)S(1)}, u32[]{:S(2)}, u32[]{:S(2)}) collective-permute-start(bf16[96,1536]{1,0:T(8,128)(2,1)S(1)} %collective-permute-done.16.refs_1_), channel_id=1, source_target_pairs={{0,4},{4,0},{8,12},{12,8},{16,20},{20,16},{24,28},{28,24},{1,5},{5... | collective-permute-start | bytes 884744 | tf_op jit(solution)/shard_map/ppermute | solution.py:82
  43.8 13.2 %collective-permute-start.10 = (bf16[512,192]{1,0:T(8,128)(2,1)S(1)}, bf16[512,192]{1,0:T(8,128)(2,1)S(1)}, u32[]{:S(2)}, u32[]{:S(2)}) collective-permute-start(bf16[512,192]{1,0:T(8,128)(2,1)S(1)} %get-tuple-element.89.mixed0.mixed), channel_id=1, source_target_pairs={{0,1},{1,0},{2,3},{3,2},{4,5},{5,4},{6,7},{7,6},{8,9},{9,8},{10,11... | collective-permute-start | bytes 589832 | tf_op jit(solution)/shard_map/ppermute | solution.py:77
  47.6 9.8 %collective-permute-start.22 = (bf16[96,1536]{1,0:T(8,128)(2,1)S(1)}, bf16[96,1536]{1,0:T(8,128)(2,1)S(1)}, u32[]{:S(2)}, u32[]{:S(2)}) collective-permute-start(bf16[96,1536]{1,0:T(8,128)(2,1)S(1)} %collective-permute-done.21.refs_6_), channel_id=1, source_target_pairs={{0,4},{4,0},{8,12},{12,8},{16,20},{20,16},{24,28},{28,24},{1,5},{5... | collective-permute-start | bytes 884744 | tf_op jit(solution)/shard_map/ppermute | solution.py:82
  49.1 9.3 %collective-permute-start.14 = (bf16[768,192]{1,0:T(8,128)(2,1)S(1)}, bf16[768,192]{1,0:T(8,128)(2,1)S(1)}, u32[]{:S(2)}, u32[]{:S(2)}) collective-permute-start(bf16[768,192]{1,0:T(8,128)(2,1)S(1)} %get-tuple-element.91.wo0.wo), channel_id=1, source_target_pairs={{0,2},{2,0},{1,3},{3,1},{4,6},{6,4},{5,7},{7,5},{8,10},{10,8},{9,1... | collective-permute-start | bytes 884744 | tf_op jit(solution)/shard_map/ppermute | solution.py:77
  65.8 14.2 %collective-permute-start.26 = (bf16[256,768]{1,0:T(8,128)(2,1)S(1)}, bf16[256,768]{1,0:T(8,128)(2,1)S(1)}, u32[]{:S(2)}, u32[]{:S(2)}) collective-permute-start(bf16[256,768]{1,0:T(8,128)(2,1)S(1)} %get-tuple-element.158), channel_id=1, source_target_pairs={{0,1},{1,0},{2,3},{3,2},{4,5},{5,4},{6,7},{7,6},{8,9},{9,8},{10,11... | collective-permute-start | bytes 1179656 | tf_op jit(solution)/shard_map/ppermute | solution.py:77
  67.5 10.3 %collective-permute-start.28 = (bf16[96,1536]{1,0:T(8,128)(2,1)S(1)}, bf16[96,1536]{1,0:T(8,128)(2,1)S(1)}, u32[]{:S(2)}, u32[]{:S(2)}) collective-permute-start(bf16[96,1536]{1,0:T(8,128)(2,1)S(1)} %get-tuple-element.110), channel_id=1, source_target_pairs={{0,24},{4,28},{8,0},{12,4},{16,8},{20,12},{24,16},{28,20},{1,25},{... | collective-permute-start | bytes 884744 | tf_op jit(solution)/shard_map/ppermute | solution.py:82
  71.2 8.8 %collective-permute-start.27 = (bf16[96,1536]{1,0:T(8,128)(2,1)S(1)}, bf16[96,1536]{1,0:T(8,128)(2,1)S(1)}, u32[]{:S(2)}, u32[]{:S(2)}) collective-permute-start(bf16[96,1536]{1,0:T(8,128)(2,1)S(1)} %get-tuple-element.109), channel_id=1, source_target_pairs={{0,4},{4,0},{8,12},{12,8},{16,20},{20,16},{24,28},{28,24},{1,5},{5... | collective-permute-start | bytes 884744 | tf_op jit(solution)/shard_map/ppermute | solution.py:82
  80.8 13.4 %collective-permute-start.34 = (bf16[96,1536]{1,0:T(8,128)(2,1)S(1)}, bf16[96,1536]{1,0:T(8,128)(2,1)S(1)}, u32[]{:S(2)}, u32[]{:S(2)}) collective-permute-start(bf16[96,1536]{1,0:T(8,128)(2,1)S(1)} %get-tuple-element.126), channel_id=1, source_target_pairs={{0,4},{4,0},{8,12},{12,8},{16,20},{20,16},{24,28},{28,24},{1,5},{5... | collective-permute-start | bytes 884744 | tf_op jit(solution)/shard_map/ppermute | solution.py:82
  82.3 11.9 %collective-permute-start.35 = (bf16[96,1536]{1,0:T(8,128)(2,1)S(1)}, bf16[96,1536]{1,0:T(8,128)(2,1)S(1)}, u32[]{:S(2)}, u32[]{:S(2)}) collective-permute-start(bf16[96,1536]{1,0:T(8,128)(2,1)S(1)} %get-tuple-element.127), channel_id=1, source_target_pairs={{0,24},{4,28},{8,0},{12,4},{16,8},{20,12},{24,16},{28,20},{1,25},{... | collective-permute-start | bytes 884744 | tf_op jit(solution)/shard_map/ppermute | solution.py:82
  84.4 8.6 %collective-permute-start.23 = (bf16[256,768]{1,0:T(8,128)(2,1)S(1)}, bf16[256,768]{1,0:T(8,128)(2,1)S(1)}, u32[]{:S(2)}, u32[]{:S(2)}) collective-permute-start(bf16[256,768]{1,0:T(8,128)(2,1)S(1)} %get-tuple-element.104), channel_id=1, source_target_pairs={{0,2},{2,0},{1,3},{3,1},{4,6},{6,4},{5,7},{7,5},{8,10},{10,8},{9,1... | collective-permute-start | bytes 1179656 | tf_op jit(solution)/shard_map/ppermute | solution.py:77
  92.9 11.7 %collective-permute-start.43 = (bf16[96,1536]{1,0:T(8,128)(2,1)S(1)}, bf16[96,1536]{1,0:T(8,128)(2,1)S(1)}, u32[]{:S(2)}, u32[]{:S(2)}) collective-permute-start(bf16[96,1536]{1,0:T(8,128)(2,1)S(1)} %add_convert_fusion.2), channel_id=1, source_target_pairs={{0,8},{4,12},{8,16},{12,20},{16,24},{20,28},{24,0},{28,4},{1,9},{5... | collective-permute-start | bytes 884744 | tf_op jit(solution)/shard_map/ppermute | solution.py:82
  93.2 15.3 %collective-permute-start.24 = (bf16[128,768]{1,0:T(8,128)(2,1)S(1)}, bf16[128,768]{1,0:T(8,128)(2,1)S(1)}, u32[]{:S(2)}, u32[]{:S(2)}) collective-permute-start(bf16[128,768]{1,0:T(8,128)(2,1)S(1)} %slice.37), channel_id=1, source_target_pairs={{0,1},{1,0},{2,3},{3,2},{4,5},{5,4},{6,7},{7,6},{8,9},{9,8},{10,11... | collective-permute-start | bytes 589832 | tf_op jit(solution)/shard_map/ppermute | solution.py:77
  94.5 12.7 %collective-permute-start.37 = (bf16[96,896]{1,0:T(8,128)(2,1)S(1)}, bf16[96,896]{1,0:T(8,128)(2,1)S(1)}, u32[]{:S(2)}, u32[]{:S(2)}) collective-permute-start(bf16[96,896]{1,0:T(8,128)(2,1)S(1)} %get-tuple-element.133), channel_id=1, source_target_pairs={{0,24},{4,28},{8,0},{12,4},{16,8},{20,12},{24,16},{28,20},{1,25},{... | collective-permute-start | bytes 516104 | tf_op jit(solution)/shard_map/ppermute | solution.py:82
  98.4 9.4 %collective-permute-start.38 = (bf16[96,896]{1,0:T(8,128)(2,1)S(1)}, bf16[96,896]{1,0:T(8,128)(2,1)S(1)}, u32[]{:S(2)}, u32[]{:S(2)}) collective-permute-start(bf16[96,896]{1,0:T(8,128)(2,1)S(1)} %get-tuple-element.135), channel_id=1, source_target_pairs={{0,4},{4,0},{8,12},{12,8},{16,20},{20,16},{24,28},{28,24},{1,5},{5... | collective-permute-start | bytes 516104 | tf_op jit(solution)/shard_map/ppermute | solution.py:82
  104.7 14.7 %collective-permute-start.45 = (bf16[96,1536]{1,0:T(8,128)(2,1)S(1)}, bf16[96,1536]{1,0:T(8,128)(2,1)S(1)}, u32[]{:S(2)}, u32[]{:S(2)}) collective-permute-start(bf16[96,1536]{1,0:T(8,128)(2,1)S(1)} %add_convert_fusion), channel_id=1, source_target_pairs={{0,8},{4,12},{8,16},{12,20},{16,24},{20,28},{24,0},{28,4},{1,9},{5... | collective-permute-start | bytes 884744 | tf_op jit(solution)/shard_map/ppermute | solution.py:82
  104.8 11.1 %collective-permute-start.31 = (bf16[128,768]{1,0:T(8,128)(2,1)S(1)}, bf16[128,768]{1,0:T(8,128)(2,1)S(1)}, u32[]{:S(2)}, u32[]{:S(2)}) collective-permute-start(bf16[128,768]{1,0:T(8,128)(2,1)S(1)} %slice.36), channel_id=1, source_target_pairs={{0,1},{1,0},{2,3},{3,2},{4,5},{5,4},{6,7},{7,6},{8,9},{9,8},{10,11... | collective-permute-start | bytes 589832 | tf_op jit(solution)/shard_map/ppermute | solution.py:77
  107.8 10.4 %collective-permute-start.39 = (bf16[96,896]{1,0:T(8,128)(2,1)S(1)}, bf16[96,896]{1,0:T(8,128)(2,1)S(1)}, u32[]{:S(2)}, u32[]{:S(2)}) collective-permute-start(bf16[96,896]{1,0:T(8,128)(2,1)S(1)} %add_convert_fusion.5), channel_id=1, source_target_pairs={{0,8},{4,12},{8,16},{12,20},{16,24},{20,28},{24,0},{28,4},{1,9},{5... | collective-permute-start | bytes 516104 | tf_op jit(solution)/shard_map/ppermute | solution.py:82
  108.5 12.3 %collective-permute-start.44 = (bf16[96,1536]{1,0:T(8,128)(2,1)S(1)}, bf16[96,1536]{1,0:T(8,128)(2,1)S(1)}, u32[]{:S(2)}, u32[]{:S(2)}) collective-permute-start(bf16[96,1536]{1,0:T(8,128)(2,1)S(1)} %add_convert_fusion.1), channel_id=1, source_target_pairs={{0,4},{4,0},{8,12},{12,8},{16,20},{20,16},{24,28},{28,24},{1,5},{5... | collective-permute-start | bytes 884744 | tf_op jit(solution)/shard_map/ppermute | solution.py:82
  114.4 8.3 %collective-permute-start.36 = (bf16[96,896]{1,0:T(8,128)(2,1)S(1)}, bf16[96,896]{1,0:T(8,128)(2,1)S(1)}, u32[]{:S(2)}, u32[]{:S(2)}) collective-permute-start(bf16[96,896]{1,0:T(8,128)(2,1)S(1)} %get-tuple-element.130), channel_id=1, source_target_pairs={{0,24},{4,28},{8,0},{12,4},{16,8},{20,12},{24,16},{28,20},{1,25},{... | collective-permute-start | bytes 516104 | tf_op jit(solution)/shard_map/ppermute | solution.py:82
  (20 other events, 169.7 us)

commit v6 on v5

--- a/solution.py
+++ b/solution.py
@@ -94,10 +94,10 @@
     return [chunk, ahead, across[0], behind, across[1], other, far, send(far, 0, 1)]
 
 
-def pieces_mixed(chunk, ring_free):
+def pieces_mixed(chunk, ring_free, ready):
     ahead, behind = [send(after(chunk, *ring_free), turn, 0) for turn in (3, 1)]
     other = send(chunk, 0, 1)
-    far = send(ahead, 3, 0)
+    far = send(after(ahead, ready), 3, 0)
     return [chunk, ahead, send(other, 1, 0), behind, send(ahead, 0, 1), other, far, send(far, 0, 1)]
 
 
@@ -125,8 +125,8 @@
     return pl.multiple_of((pair * 2 + (lax.rem(me, 2) ^ flip)) * rows, rows)
 
 
-def pack_body(wqkv, wout, wfc, wproj, bqv, *refs):
-    vecs, first, second = refs[:-2], refs[-2], refs[-1]
+def pack_body(wqkv, wout, bqv, *refs):
+    vecs, first = refs[:-1], refs[-1]
     rows = wqkv.shape[1]
     lines = [vec[...].astype(F32).reshape(1, rows) for vec in vecs]
     lack = jnp.zeros((2, rows - bqv.shape[1]), F32)
@@ -138,7 +138,11 @@
         cols = jnp.concatenate([cols, jnp.zeros((VEC_COLS, lack), F32)], axis=1)
     cols = cols.T[:rows].astype(LOW)
     first[...] = jnp.concatenate([cols, wqkv[0], wqkv[1], wqkv[2], turned(wout[...])], axis=1)
-    second[...] = jnp.concatenate([wfc[...], wproj[...]], axis=1)
+
+
+def pack_second_body(wfc, wproj, second):
+    second[:, : wfc.shape[1]] = wfc[...]
+    second[:, wfc.shape[1] :] = wproj[...]
 
 
 def open_second_body(size, *refs):
@@ -475,15 +479,16 @@
     rows_shape = shape(8, width, F32)
     bias_shape = shape(8, qkv_cols, F32)
     if direct:
-        first, second = on_core(
+        (first,) = on_core(
             pack_body,
-            [shape(chunk, VEC_COLS + qkv_cols + head_cols, LOW), shape(chunk, 2 * hidden_cols, LOW)],
+            [shape(chunk, VEC_COLS + qkv_cols + head_cols, LOW)],
             [],
-            [w_qkv, w_out, w_fc, w_proj.T, b_qv, *vecs],
+            [w_qkv, w_out, b_qv, *vecs],
             limit=62,
         )
+        (second,) = on_core(pack_second_body, [shape(chunk, 2 * hidden_cols, LOW)], [], [w_fc, w_proj.T])
         firsts = pieces_ring_first(first)
-        seconds = pieces_mixed(second, [firsts[1], firsts[3]])
+        seconds = pieces_mixed(second, [firsts[6]], mask)
     else:
         lines = jnp.stack([*vecs, *jnp.pad(b_qv, ((0, 0), (0, chunk - qv_count)))])
         lack = jnp.zeros((chunk, VEC_COLS - lines.shape[0]), LOW)

time: 127 us -> 127 us (level)
  starting transfers between devices: 50.1 us -> 44.8 us
  waiting for transfers between devices: 43.9 us -> 48.5 us
    ppermute x28, waiting for transfers between devices: 34.7 us -> 41.6 us  [send(): return lax.ppermute(value, 'fsdp', pairs)]
    ppermute x28, starting transfers between devices: 40.7 us -> 36.1 us  [send(): return lax.ppermute(value, 'fsdp', pairs)]
    ppermute x18, waiting for transfers between devices: 9.12 us -> 6.91 us  [swap(): return lax.ppermute(value, axis, [(0, 1), (1, 0)])]
    unnamed x12 -> x16, local copies, waits for them, and re-layouts: 1.6 us -> 3.43 us
    pallas_call x13 -> x14, Pallas kernels: 26.2 us -> 25.8 us  [on_core(): pl.pallas_call(body, out_shape=tuple(outs), in_specs=specs, out_specs=tup...]
  transfers between devices with their start and end apart: 46 -> 46, of which waited for: 18 -> 19; matrix products, arithmetic and copies ran while one was open for 3% -> 2% of each run, Pallas kernels for 14% -> 14%
where the time goes in v6:
time: 127 us; the launch traced here: 126 us
  waiting for transfers between devices  48.5 us (38%)
  starting transfers between devices  44.8 us (35%)
  Pallas kernels  25.8 us (20%)
  local copies, waits for them, and re-layouts  3.87 us (3%)
  other arithmetic  2.45 us (2%)
    ppermute x28, waiting for transfers between devices, send(): return lax.ppermute(value, 'fsdp', pairs)  41.6 us
    ppermute x28, starting transfers between devices, send(): return lax.ppermute(value, 'fsdp', pairs)  36.1 us
    pallas_call x14, Pallas kernels, on_core(): pl.pallas_call(body, out_shape=tuple(outs), in_specs=specs, out_specs=tup...  25.8 us
    ppermute x18, starting transfers between devices, swap(): return lax.ppermute(value, axis, [(0, 1), (1, 0)])  8.68 us
    ppermute x18, waiting for transfers between devices, swap(): return lax.ppermute(value, axis, [(0, 1), (1, 0)])  6.91 us
    unnamed x16, local copies, waits for them, and re-layouts  3.43 us
  transfers between devices with their start and end apart: 46, of which 19 were waited for; matrix products, arithmetic and copies ran while one was open for 2% of the time, Pallas kernels for 14%

profile of v6, /device:TPU:0, one launch (start us, length us, event | category | flops | bytes accessed | tf_op | source)
XLA Modules:
  0.0 126.4 jit_solution(4162137864830261744)
XLA Ops:
  0.7 2.0 %shard_map.263.refs_0_ = bf16[96,896]{1,0:T(8,128)(2,1)} custom-call(bf16[3,96,192]{2,1,0:T(8,128)(2,1)} %wqkv.1, bf16[192,96]{1,0:T(8,128)(2,1)} %wout.1, bf16[2,24]{1,0:T(2,128)(2,1)} %bqv.1, bf16[96]{0:T(256)(128)(2,1)} %refs_0_.1, bf16[96]{0:T(256)(128)(2,1)} %refs_1_.1, bf16[96]{0:T(256)(128)(2,1)} %refs_2_.1, bf16[96]{0:T(256)(128)(2,1)} %refs_3_.1, ...), custom_call_target="tpu_custom_call" | custom-call | bytes 320928 | tf_op jit(solution)/shard_map/pallas_call | solution.py:30
  2.6 5.0 %collective-permute-start.3 = (bf16[96,896]{1,0:T(8,128)(2,1)}, bf16[96,896]{1,0:T(8,128)(2,1)}, u32[]{:S(2)}, u32[]{:S(2)}) collective-permute-start(bf16[96,896]{1,0:T(8,128)(2,1)} %shard_map.263.refs_0_), channel_id=1, source_target_pairs={{0,24},{4,28},{8,0},{12,4},{16,8},{20,12},{24,16},{28,20},{1,25},{... | collective-permute-start | bytes 516104 | tf_op jit(solution)/shard_map/ppermute | solution.py:82
  7.7 1.5 %collective-permute-start = (bf16[128,768]{1,0:T(8,128)(2,1)}, bf16[128,768]{1,0:T(8,128)(2,1)S(1)}, u32[]{:S(2)}, u32[]{:S(2)}) collective-permute-start(bf16[128,768]{1,0:T(8,128)(2,1)} %own.1), channel_id=1, source_target_pairs={{0,1},{1,0},{2,3},{3,2},{4,5},{5,4},{6,7},{7,6},{8,9},{9,8},{10,11... | collective-permute-start | bytes 589832 | tf_op jit(solution)/shard_map/ppermute | solution.py:77
  11.1 1.6 %collective-permute-start.17 = (bf16[96,1536]{1,0:T(8,128)(2,1)S(1)}, bf16[96,1536]{1,0:T(8,128)(2,1)S(1)}, u32[]{:S(2)}, u32[]{:S(2)}) collective-permute-start(bf16[96,1536]{1,0:T(8,128)(2,1)S(1)} %shard_map.266.refs_0_), channel_id=1, source_target_pairs={{0,4},{4,0},{8,12},{12,8},{16,20},{20,16},{24,28},{28,24},{1,5},{5... | collective-permute-start | bytes 884744 | tf_op jit(solution)/shard_map/ppermute | solution.py:82
  12.8 4.3 %collective-permute-start.8 = (bf16[96,896]{1,0:T(8,128)(2,1)}, bf16[96,896]{1,0:T(8,128)(2,1)}, u32[]{:S(2)}, u32[]{:S(2)}) collective-permute-start(bf16[96,896]{1,0:T(8,128)(2,1)} %collective-permute-done.3.refs_1_), channel_id=1, source_target_pairs={{0,24},{4,28},{8,0},{12,4},{16,8},{20,12},{24,16},{28,20},{1,25},{... | collective-permute-start | bytes 516104 | tf_op jit(solution)/shard_map/ppermute | solution.py:82
  18.3 3.6 %collective-permute-done.8.refs_6_ = bf16[96,896]{1,0:T(8,128)(2,1)} collective-permute-done((bf16[96,896]{1,0:T(8,128)(2,1)}, bf16[96,896]{1,0:T(8,128)(2,1)}, u32[]{:S(2)}, u32[]{:S(2)}) %collective-permute-start.8) | collective-permute-done | bytes 172064 | tf_op jit(solution)/shard_map/ppermute | solution.py:82
  21.9 2.9 %collective-permute-start.16 = (bf16[96,1536]{1,0:T(8,128)(2,1)S(1)}, bf16[96,1536]{1,0:T(8,128)(2,1)S(1)}, u32[]{:S(2)}, u32[]{:S(2)}) collective-permute-start(bf16[96,1536]{1,0:T(8,128)(2,1)S(1)} %shard_map.266.refs_0_), channel_id=1, source_target_pairs={{0,24},{4,28},{8,0},{12,4},{16,8},{20,12},{24,16},{28,20},{1,25},{... | collective-permute-start | bytes 884744 | tf_op jit(solution)/shard_map/ppermute | solution.py:82
  24.8 1.4 %collective-permute-start.7 = (bf16[96,896]{1,0:T(8,128)(2,1)S(1)}, bf16[96,896]{1,0:T(8,128)(2,1)}, u32[]{:S(2)}, u32[]{:S(2)}) collective-permute-start(bf16[96,896]{1,0:T(8,128)(2,1)S(1)} %copy-done.2), channel_id=1, source_target_pairs={{0,4},{4,0},{8,12},{12,8},{16,20},{20,16},{24,28},{28,24},{1,5},{5... | collective-permute-start | bytes 516104 | tf_op jit(solution)/shard_map/ppermute | solution.py:82
  33.5 2.5 %collective-permute-done.6.refs_4_ = bf16[96,896]{1,0:T(8,128)(2,1)} collective-permute-done((bf16[96,896]{1,0:T(8,128)(2,1)}, bf16[96,896]{1,0:T(8,128)(2,1)}, u32[]{:S(2)}, u32[]{:S(2)}) %collective-permute-start.6) | collective-permute-done | bytes 172064 | tf_op jit(solution)/shard_map/ppermute | solution.py:82
  37.2 1.4 %collective-permute-done.5.refs_2_ = bf16[96,896]{1,0:T(8,128)(2,1)} collective-permute-done((bf16[96,896]{1,0:T(8,128)(2,1)}, bf16[96,896]{1,0:T(8,128)(2,1)}, u32[]{:S(2)}, u32[]{:S(2)}) %collective-permute-start.5) | collective-permute-done | bytes 172064 | tf_op jit(solution)/shard_map/ppermute | solution.py:82
  38.6 1.8 %collective-permute-done.9.refs_7_ = bf16[96,896]{1,0:T(8,128)(2,1)} collective-permute-done((bf16[96,896]{1,0:T(8,128)(2,1)}, bf16[96,896]{1,0:T(8,128)(2,1)}, u32[]{:S(2)}, u32[]{:S(2)}) %collective-permute-start.9) | collective-permute-done | bytes 172064 | tf_op jit(solution)/shard_map/ppermute | solution.py:82
  40.4 5.4 %shard_map.265 = (bf16[512,576]{1,0:T(8,128)(2,1)S(1)}, bf16[512,192]{1,0:T(8,128)(2,1)S(1)}, f32[512,128]{1,0:T(8,128)S(1)}, bf16[768,576]{1,0:T(8,128)(2,1)S(1...) custom-call(bf16[96,896]{1,0:T(8,128)(2,1)S(1)} %copy-done.2, bf16[96,896]{1,0:T(8,128)(2,1)} %collective-permute-done.3.refs_1_, ...), custom_call_target="tpu_custom_call" | custom-call | flops 654311424 | bytes 7135232 | tf_op jit(solution)/shard_map/pallas_call | solution.py:30
  48.5 5.0 %collective-permute-done.21.refs_6_ = bf16[96,1536]{1,0:T(8,128)(2,1)S(1)} collective-permute-done((bf16[96,1536]{1,0:T(8,128)(2,1)S(1)}, bf16[96,1536]{1,0:T(8,128)(2,1)S(1)}, u32[]{:S(2)}, u32[]{:S(2)}) %collective-permute-start.21) | collective-permute-done | bytes 294944 | tf_op jit(solution)/shard_map/ppermute | solution.py:82
  53.5 1.5 %collective-permute-start.22 = (bf16[96,1536]{1,0:T(8,128)(2,1)S(1)}, bf16[96,1536]{1,0:T(8,128)(2,1)S(1)}, u32[]{:S(2)}, u32[]{:S(2)}) collective-permute-start(bf16[96,1536]{1,0:T(8,128)(2,1)S(1)} %collective-permute-done.21.refs_6_), channel_id=1, source_target_pairs={{0,4},{4,0},{8,12},{12,8},{16,20},{20,16},{24,28},{28,24},{1,5},{5... | collective-permute-start | bytes 884744 | tf_op jit(solution)/shard_map/ppermute | solution.py:82
  55.0 1.9 %collective-permute-done.13.wo1 = bf16[768,192]{1,0:T(8,128)(2,1)S(1)} collective-permute-done((bf16[768,192]{1,0:T(8,128)(2,1)S(1)}, bf16[768,192]{1,0:T(8,128)(2,1)S(1)}, u32[]{:S(2)}, u32[]{:S(2)}) %collective-permute-start.13) | collective-permute-done | bytes 294944 | tf_op jit(solution)/shard_map/ppermute | solution.py:77
  56.9 2.8 %collective-permute-done.10.mixed1 = bf16[512,192]{1,0:T(8,128)(2,1)S(1)} collective-permute-done((bf16[512,192]{1,0:T(8,128)(2,1)S(1)}, bf16[512,192]{1,0:T(8,128)(2,1)S(1)}, u32[]{:S(2)}, u32[]{:S(2)}) %collective-permute-start.10) | collective-permute-done | bytes 196640 | tf_op jit(solution)/shard_map/ppermute | solution.py:77
  60.2 2.1 %collective-permute-done.22.refs_7_ = bf16[96,1536]{1,0:T(8,128)(2,1)S(1)} collective-permute-done((bf16[96,1536]{1,0:T(8,128)(2,1)S(1)}, bf16[96,1536]{1,0:T(8,128)(2,1)S(1)}, u32[]{:S(2)}, u32[]{:S(2)}) %collective-permute-start.22) | collective-permute-done | bytes 294944 | tf_op jit(solution)/shard_map/ppermute | solution.py:82
  63.3 4.3 %shard_map.268 = (f32[256,768]{1,0:T(8,128)S(1)}, bf16[256,768]{1,0:T(8,128)(2,1)S(1)}, f32[256,768]{1,0:T(8,128)S(1)}, bf16[512,768]{1,0:T(8,128)(2,1)S(1)}, bf...) custom-call(bf16[128,768]{1,0:T(8,128)(2,1)S(1)} %copy-done.1, bf16[128,768]{1,0:T(8,128)(2,1)S(1)} %collective-permute-done.tok1, ...), custom_call_target="tpu_custom_call" | custom-call | flops 1811939328 | bytes 9854976 | tf_op jit(solution)/shard_map/pallas_call | solution.py:30
  67.8 2.3 %shard_map.269 = (f32[256,768]{1,0:T(8,128)S(1)}, bf16[256,768]{1,0:T(8,128)(2,1)S(1)}, f32[1,768]{1,0:T(1,128)S(1)}, f32[96,1536]{1,0:T(8,128)S(1)}, bf16[96,15...) custom-call(bf16[512,768]{1,0:T(8,128)(2,1)S(1)} %get-tuple-element., ...), custom_call_target="tpu_custom_call" | custom-call | flops 1811939328 | bytes 8162304 | tf_op jit(solution)/shard_map/pallas_call | solution.py:30
  70.8 1.5 %collective-permute-start.27 = (bf16[96,1536]{1,0:T(8,128)(2,1)S(1)}, bf16[96,1536]{1,0:T(8,128)(2,1)S(1)}, u32[]{:S(2)}, u32[]{:S(2)}) collective-permute-start(bf16[96,1536]{1,0:T(8,128)(2,1)S(1)} %get-tuple-element.107), channel_id=1, source_target_pairs={{0,4},{4,0},{8,12},{12,8},{16,20},{20,16},{24,28},{28,24},{1,5},{5... | collective-permute-start | bytes 884744 | tf_op jit(solution)/shard_map/ppermute | solution.py:82
  72.3 7.6 %collective-permute-done.28 = bf16[96,1536]{1,0:T(8,128)(2,1)S(1)} collective-permute-done((bf16[96,1536]{1,0:T(8,128)(2,1)S(1)}, bf16[96,1536]{1,0:T(8,128)(2,1)S(1)}, u32[]{:S(2)}, u32[]{:S(2)}) %collective-permute-start.28) | collective-permute-done | bytes 294944 | tf_op jit(solution)/shard_map/ppermute | solution.py:82
  79.9 1.9 %collective-permute-done.26.far = bf16[256,768]{1,0:T(8,128)(2,1)S(1)} collective-permute-done((bf16[256,768]{1,0:T(8,128)(2,1)S(1)}, bf16[256,768]{1,0:T(8,128)(2,1)S(1)}, u32[]{:S(2)}, u32[]{:S(2)}) %collective-permute-start.26) | collective-permute-done | bytes 393248 | tf_op jit(solution)/shard_map/ppermute | solution.py:77
  82.5 1.5 %collective-permute-start.34 = (bf16[96,1536]{1,0:T(8,128)(2,1)S(1)}, bf16[96,1536]{1,0:T(8,128)(2,1)S(1)}, u32[]{:S(2)}, u32[]{:S(2)}) collective-permute-start(bf16[96,1536]{1,0:T(8,128)(2,1)S(1)} %get-tuple-element.124), channel_id=1, source_target_pairs={{0,4},{4,0},{8,12},{12,8},{16,20},{20,16},{24,28},{28,24},{1,5},{5... | collective-permute-start | bytes 884744 | tf_op jit(solution)/shard_map/ppermute | solution.py:82
  84.3 3.9 %shard_map.271 = (f32[256,768]{1,0:T(8,128)S(1)}, bf16[256,768]{1,0:T(8,128)(2,1)S(1)}, bf16[512,576]{1,0:T(8,128)(2,1)S(1)}, f32[8,768]{1,0:T(8,128)S(1)}, f32[8,576]{1,0:T(8,128)S(1)}) custom-call(bf16[256,768]{1,0:T(8,128)(2,1)S(1)} %get-tuple-element.110.grad_half, bf16[256,768]{1,0:T(8,128)(2,1)S(1)} %collective-permute-done.29.grad_other, ...), custom_call_target="tpu_custom_call" | custom-call | flops 1107296256 | bytes 7276544 | tf_op jit(solution)/shard_map/pallas_call | solution.py:30
  88.8 1.6 %collective-permute-start.32 = (f32[8,768]{1,0:T(8,128)S(1)}, f32[8,768]{1,0:T(8,128)S(1)}, u32[]{:S(2)}, u32[]{:S(2)}) collective-permute-start(f32[8,768]{1,0:T(8,128)S(1)} %get-tuple-element.121), channel_id=1, source_target_pairs={{0,1},{1,0},{2,3},{3,2},{4,5},{5,4},{6,7},{7,6},{8,9},{9,8},{10,11... | collective-permute-start | bytes 73736 | tf_op jit(solution)/shard_map/ppermute | solution.py:77
  90.4 2.5 %shard_map.273 = (f32[768,768]{1,0:T(8,128)S(1)}, f32[8,768]{1,0:T(8,128)S(1)}) custom-call(bf16[256,768]{1,0:T(8,128)(2,1)S(1)} %get-tuple-element.110.grad_half, bf16[256,768]{1,0:T(8,128)(2,1)S(1)} %collective-permute-done.29.grad_other, bf16[512,192]{1,0:T(8,128)(2,1)S(1)} %get-tuple-element.87.mixed0.mixed, ...), custom_call_target="tpu_custom_call" | custom-call | flops 603979776 | bytes 6460416 | tf_op jit(solution)/shard_map/pallas_call | solution.py:30
  92.9 1.6 %collective-permute-start.43 = (bf16[96,1536]{1,0:T(8,128)(2,1)S(1)}, bf16[96,1536]{1,0:T(8,128)(2,1)S(1)}, u32[]{:S(2)}, u32[]{:S(2)}) collective-permute-start(bf16[96,1536]{1,0:T(8,128)(2,1)S(1)} %add_convert_fusion.2), channel_id=1, source_target_pairs={{0,8},{4,12},{8,16},{12,20},{16,24},{20,28},{24,0},{28,4},{1,9},{5... | collective-permute-start | bytes 884744 | tf_op jit(solution)/shard_map/ppermute | solution.py:82
  96.2 2.6 %collective-permute-start.37 = (bf16[96,896]{1,0:T(8,128)(2,1)S(1)}, bf16[96,896]{1,0:T(8,128)(2,1)S(1)}, u32[]{:S(2)}, u32[]{:S(2)}) collective-permute-start(bf16[96,896]{1,0:T(8,128)(2,1)S(1)} %get-tuple-element.131), channel_id=1, source_target_pairs={{0,24},{4,28},{8,0},{12,4},{16,8},{20,12},{24,16},{28,20},{1,25},{... | collective-permute-start | bytes 516104 | tf_op jit(solution)/shard_map/ppermute | solution.py:82
  99.3 5.4 %collective-permute-done.43 = bf16[96,1536]{1,0:T(8,128)(2,1)S(1)} collective-permute-done((bf16[96,1536]{1,0:T(8,128)(2,1)S(1)}, bf16[96,1536]{1,0:T(8,128)(2,1)S(1)}, u32[]{:S(2)}, u32[]{:S(2)}) %collective-permute-start.43) | collective-permute-done | bytes 294944 | tf_op jit(solution)/shard_map/ppermute | solution.py:82
  110.1 4.4 %collective-permute-done.41 = bf16[96,896]{1,0:T(8,128)(2,1)S(1)} collective-permute-done((bf16[96,896]{1,0:T(8,128)(2,1)S(1)}, bf16[96,896]{1,0:T(8,128)(2,1)S(1)}, u32[]{:S(2)}, u32[]{:S(2)}) %collective-permute-start.41) | collective-permute-done | bytes 172064 | tf_op jit(solution)/shard_map/ppermute | solution.py:82
  114.5 2.4 %collective-permute-start.36 = (bf16[96,896]{1,0:T(8,128)(2,1)S(1)}, bf16[96,896]{1,0:T(8,128)(2,1)S(1)}, u32[]{:S(2)}, u32[]{:S(2)}) collective-permute-start(bf16[96,896]{1,0:T(8,128)(2,1)S(1)} %get-tuple-element.128), channel_id=1, source_target_pairs={{0,24},{4,28},{8,0},{12,4},{16,8},{20,12},{24,16},{28,20},{1,25},{... | collective-permute-start | bytes 516104 | tf_op jit(solution)/shard_map/ppermute | solution.py:82
  122.5 3.0 %collective-permute-done.42.refs_3_ = bf16[96,896]{1,0:T(8,128)(2,1)S(1)} collective-permute-done((bf16[96,896]{1,0:T(8,128)(2,1)S(1)}, bf16[96,896]{1,0:T(8,128)(2,1)S(1)}, u32[]{:S(2)}, u32[]{:S(2)}) %collective-permute-start.42) | collective-permute-done | bytes 172064 | tf_op jit(solution)/shard_map/ppermute | solution.py:82
  (113 shorter events, 32.1 us)
Async XLA Ops:
  2.6 10.2 %collective-permute-start.3 = (bf16[96,896]{1,0:T(8,128)(2,1)}, bf16[96,896]{1,0:T(8,128)(2,1)}, u32[]{:S(2)}, u32[]{:S(2)}) collective-permute-start(bf16[96,896]{1,0:T(8,128)(2,1)} %shard_map.263.refs_0_), channel_id=1, source_target_pairs={{0,24},{4,28},{8,0},{12,4},{16,8},{20,12},{24,16},{28,20},{1,25},{... | collective-permute-start | bytes 516104 | tf_op jit(solution)/shard_map/ppermute | solution.py:82
  7.7 10.6 %collective-permute-start = (bf16[128,768]{1,0:T(8,128)(2,1)}, bf16[128,768]{1,0:T(8,128)(2,1)S(1)}, u32[]{:S(2)}, u32[]{:S(2)}) collective-permute-start(bf16[128,768]{1,0:T(8,128)(2,1)} %own.1), channel_id=1, source_target_pairs={{0,1},{1,0},{2,3},{3,2},{4,5},{5,4},{6,7},{7,6},{8,9},{9,8},{10,11... | collective-permute-start | bytes 589832 | tf_op jit(solution)/shard_map/ppermute | solution.py:77
  9.2 17.0 %collective-permute-start.1 = (bf16[128,768]{1,0:T(8,128)(2,1)}, bf16[128,768]{1,0:T(8,128)(2,1)S(1)}, u32[]{:S(2)}, u32[]{:S(2)}) collective-permute-start(bf16[128,768]{1,0:T(8,128)(2,1)} %own.1), channel_id=1, source_target_pairs={{0,2},{2,0},{1,3},{3,1},{4,6},{6,4},{5,7},{7,5},{8,10},{10,8},{9,1... | collective-permute-start | bytes 589832 | tf_op jit(solution)/shard_map/ppermute | solution.py:77
  9.2 15.6 %collective-permute-start.4 = (bf16[96,896]{1,0:T(8,128)(2,1)}, bf16[96,896]{1,0:T(8,128)(2,1)}, u32[]{:S(2)}, u32[]{:S(2)}) collective-permute-start(bf16[96,896]{1,0:T(8,128)(2,1)} %shard_map.263.refs_0_), channel_id=1, source_target_pairs={{0,8},{4,12},{8,16},{12,20},{16,24},{20,28},{24,0},{28,4},{1,9},{5... | collective-permute-start | bytes 516104 | tf_op jit(solution)/shard_map/ppermute | solution.py:82
  11.1 15.9 %collective-permute-start.17 = (bf16[96,1536]{1,0:T(8,128)(2,1)S(1)}, bf16[96,1536]{1,0:T(8,128)(2,1)S(1)}, u32[]{:S(2)}, u32[]{:S(2)}) collective-permute-start(bf16[96,1536]{1,0:T(8,128)(2,1)S(1)} %shard_map.266.refs_0_), channel_id=1, source_target_pairs={{0,4},{4,0},{8,12},{12,8},{16,20},{20,16},{24,28},{28,24},{1,5},{5... | collective-permute-start | bytes 884744 | tf_op jit(solution)/shard_map/ppermute | solution.py:82
  12.8 9.1 %collective-permute-start.8 = (bf16[96,896]{1,0:T(8,128)(2,1)}, bf16[96,896]{1,0:T(8,128)(2,1)}, u32[]{:S(2)}, u32[]{:S(2)}) collective-permute-start(bf16[96,896]{1,0:T(8,128)(2,1)} %collective-permute-done.3.refs_1_), channel_id=1, source_target_pairs={{0,24},{4,28},{8,0},{12,4},{16,8},{20,12},{24,16},{28,20},{1,25},{... | collective-permute-start | bytes 516104 | tf_op jit(solution)/shard_map/ppermute | solution.py:82
  18.2 10.0 %collective-permute-start.2 = (bf16[128,768]{1,0:T(8,128)(2,1)S(1)}, bf16[128,768]{1,0:T(8,128)(2,1)S(1)}, u32[]{:S(2)}, u32[]{:S(2)}) collective-permute-start(bf16[128,768]{1,0:T(8,128)(2,1)S(1)} %collective-permute-done.tok1), channel_id=1, source_target_pairs={{0,2},{2,0},{1,3},{3,1},{4,6},{6,4},{5,7},{7,5},{8,10},{10,8},{9,1... | collective-permute-start | bytes 589832 | tf_op jit(solution)/shard_map/ppermute | solution.py:77
  21.9 8.9 %collective-permute-start.16 = (bf16[96,1536]{1,0:T(8,128)(2,1)S(1)}, bf16[96,1536]{1,0:T(8,128)(2,1)S(1)}, u32[]{:S(2)}, u32[]{:S(2)}) collective-permute-start(bf16[96,1536]{1,0:T(8,128)(2,1)S(1)} %shard_map.266.refs_0_), channel_id=1, source_target_pairs={{0,24},{4,28},{8,0},{12,4},{16,8},{20,12},{24,16},{28,20},{1,25},{... | collective-permute-start | bytes 884744 | tf_op jit(solution)/shard_map/ppermute | solution.py:82
  26.2 9.8 %collective-permute-start.6 = (bf16[96,896]{1,0:T(8,128)(2,1)}, bf16[96,896]{1,0:T(8,128)(2,1)}, u32[]{:S(2)}, u32[]{:S(2)}) collective-permute-start(bf16[96,896]{1,0:T(8,128)(2,1)} %collective-permute-done.3.refs_1_), channel_id=1, source_target_pairs={{0,4},{4,0},{8,12},{12,8},{16,20},{20,16},{24,28},{28,24},{1,5},{5... | collective-permute-start | bytes 516104 | tf_op jit(solution)/shard_map/ppermute | solution.py:82
  26.9 11.6 %collective-permute-start.5 = (bf16[96,896]{1,0:T(8,128)(2,1)}, bf16[96,896]{1,0:T(8,128)(2,1)}, u32[]{:S(2)}, u32[]{:S(2)}) collective-permute-start(bf16[96,896]{1,0:T(8,128)(2,1)} %collective-permute-done.4.refs_3_), channel_id=1, source_target_pairs={{0,4},{4,0},{8,12},{12,8},{16,20},{20,16},{24,28},{28,24},{1,5},{5... | collective-permute-start | bytes 516104 | tf_op jit(solution)/shard_map/ppermute | solution.py:82
  28.9 11.5 %collective-permute-start.9 = (bf16[96,896]{1,0:T(8,128)(2,1)}, bf16[96,896]{1,0:T(8,128)(2,1)}, u32[]{:S(2)}, u32[]{:S(2)}) collective-permute-start(bf16[96,896]{1,0:T(8,128)(2,1)} %collective-permute-done.8.refs_6_), channel_id=1, source_target_pairs={{0,4},{4,0},{8,12},{12,8},{16,20},{20,16},{24,28},{28,24},{1,5},{5... | collective-permute-start | bytes 516104 | tf_op jit(solution)/shard_map/ppermute | solution.py:82
  30.8 16.3 %collective-permute-start.18 = (bf16[96,1536]{1,0:T(8,128)(2,1)S(1)}, bf16[96,1536]{1,0:T(8,128)(2,1)S(1)}, u32[]{:S(2)}, u32[]{:S(2)}) collective-permute-start(bf16[96,1536]{1,0:T(8,128)(2,1)S(1)} %collective-permute-done.17.refs_5_), channel_id=1, source_target_pairs={{0,8},{4,12},{8,16},{12,20},{16,24},{20,28},{24,0},{28,4},{1,9},{5... | collective-permute-start | bytes 884744 | tf_op jit(solution)/shard_map/ppermute | solution.py:82
  33.3 21.7 %collective-permute-start.19 = (bf16[96,1536]{1,0:T(8,128)(2,1)S(1)}, bf16[96,1536]{1,0:T(8,128)(2,1)S(1)}, u32[]{:S(2)}, u32[]{:S(2)}) collective-permute-start(bf16[96,1536]{1,0:T(8,128)(2,1)S(1)} %shard_map.266.refs_0_), channel_id=1, source_target_pairs={{0,8},{4,12},{8,16},{12,20},{16,24},{20,28},{24,0},{28,4},{1,9},{5... | collective-permute-start | bytes 884744 | tf_op jit(solution)/shard_map/ppermute | solution.py:82
  36.0 17.5 %collective-permute-start.21 = (bf16[96,1536]{1,0:T(8,128)(2,1)S(1)}, bf16[96,1536]{1,0:T(8,128)(2,1)S(1)}, u32[]{:S(2)}, u32[]{:S(2)}) collective-permute-start(bf16[96,1536]{1,0:T(8,128)(2,1)S(1)} %collective-permute-done.16.refs_1_), channel_id=1, source_target_pairs={{0,24},{4,28},{8,0},{12,4},{16,8},{20,12},{24,16},{28,20},{1,25},{... | collective-permute-start | bytes 884744 | tf_op jit(solution)/shard_map/ppermute | solution.py:82
  45.8 11.1 %collective-permute-start.13 = (bf16[768,192]{1,0:T(8,128)(2,1)S(1)}, bf16[768,192]{1,0:T(8,128)(2,1)S(1)}, u32[]{:S(2)}, u32[]{:S(2)}) collective-permute-start(bf16[768,192]{1,0:T(8,128)(2,1)S(1)} %get-tuple-element.89.wo0.wo), channel_id=1, source_target_pairs={{0,1},{1,0},{2,3},{3,2},{4,5},{5,4},{6,7},{7,6},{8,9},{9,8},{10,11... | collective-permute-start | bytes 884744 | tf_op jit(solution)/shard_map/ppermute | solution.py:77
  46.0 13.7 %collective-permute-start.20 = (bf16[96,1536]{1,0:T(8,128)(2,1)S(1)}, bf16[96,1536]{1,0:T(8,128)(2,1)S(1)}, u32[]{:S(2)}, u32[]{:S(2)}) collective-permute-start(bf16[96,1536]{1,0:T(8,128)(2,1)S(1)} %collective-permute-done.16.refs_1_), channel_id=1, source_target_pairs={{0,4},{4,0},{8,12},{12,8},{16,20},{20,16},{24,28},{28,24},{1,5},{5... | collective-permute-start | bytes 884744 | tf_op jit(solution)/shard_map/ppermute | solution.py:82
  47.1 12.6 %collective-permute-start.10 = (bf16[512,192]{1,0:T(8,128)(2,1)S(1)}, bf16[512,192]{1,0:T(8,128)(2,1)S(1)}, u32[]{:S(2)}, u32[]{:S(2)}) collective-permute-start(bf16[512,192]{1,0:T(8,128)(2,1)S(1)} %get-tuple-element.87.mixed0.mixed), channel_id=1, source_target_pairs={{0,1},{1,0},{2,3},{3,2},{4,5},{5,4},{6,7},{7,6},{8,9},{9,8},{10,11... | collective-permute-start | bytes 589832 | tf_op jit(solution)/shard_map/ppermute | solution.py:77
  53.5 8.9 %collective-permute-start.22 = (bf16[96,1536]{1,0:T(8,128)(2,1)S(1)}, bf16[96,1536]{1,0:T(8,128)(2,1)S(1)}, u32[]{:S(2)}, u32[]{:S(2)}) collective-permute-start(bf16[96,1536]{1,0:T(8,128)(2,1)S(1)} %collective-permute-done.21.refs_6_), channel_id=1, source_target_pairs={{0,4},{4,0},{8,12},{12,8},{16,20},{20,16},{24,28},{28,24},{1,5},{5... | collective-permute-start | bytes 884744 | tf_op jit(solution)/shard_map/ppermute | solution.py:82
  70.2 11.6 %collective-permute-start.26 = (bf16[256,768]{1,0:T(8,128)(2,1)S(1)}, bf16[256,768]{1,0:T(8,128)(2,1)S(1)}, u32[]{:S(2)}, u32[]{:S(2)}) collective-permute-start(bf16[256,768]{1,0:T(8,128)(2,1)S(1)} %get-tuple-element.156), channel_id=1, source_target_pairs={{0,1},{1,0},{2,3},{3,2},{4,5},{5,4},{6,7},{7,6},{8,9},{9,8},{10,11... | collective-permute-start | bytes 1179656 | tf_op jit(solution)/shard_map/ppermute | solution.py:77
  70.8 9.1 %collective-permute-start.28 = (bf16[96,1536]{1,0:T(8,128)(2,1)S(1)}, bf16[96,1536]{1,0:T(8,128)(2,1)S(1)}, u32[]{:S(2)}, u32[]{:S(2)}) collective-permute-start(bf16[96,1536]{1,0:T(8,128)(2,1)S(1)} %get-tuple-element.108), channel_id=1, source_target_pairs={{0,24},{4,28},{8,0},{12,4},{16,8},{20,12},{24,16},{28,20},{1,25},{... | collective-permute-start | bytes 884744 | tf_op jit(solution)/shard_map/ppermute | solution.py:82
  70.8 9.1 %collective-permute-start.27 = (bf16[96,1536]{1,0:T(8,128)(2,1)S(1)}, bf16[96,1536]{1,0:T(8,128)(2,1)S(1)}, u32[]{:S(2)}, u32[]{:S(2)}) collective-permute-start(bf16[96,1536]{1,0:T(8,128)(2,1)S(1)} %get-tuple-element.107), channel_id=1, source_target_pairs={{0,4},{4,0},{8,12},{12,8},{16,20},{20,16},{24,28},{28,24},{1,5},{5... | collective-permute-start | bytes 884744 | tf_op jit(solution)/shard_map/ppermute | solution.py:82
  82.5 13.4 %collective-permute-start.34 = (bf16[96,1536]{1,0:T(8,128)(2,1)S(1)}, bf16[96,1536]{1,0:T(8,128)(2,1)S(1)}, u32[]{:S(2)}, u32[]{:S(2)}) collective-permute-start(bf16[96,1536]{1,0:T(8,128)(2,1)S(1)} %get-tuple-element.124), channel_id=1, source_target_pairs={{0,4},{4,0},{8,12},{12,8},{16,20},{20,16},{24,28},{28,24},{1,5},{5... | collective-permute-start | bytes 884744 | tf_op jit(solution)/shard_map/ppermute | solution.py:82
  84.1 11.8 %collective-permute-start.35 = (bf16[96,1536]{1,0:T(8,128)(2,1)S(1)}, bf16[96,1536]{1,0:T(8,128)(2,1)S(1)}, u32[]{:S(2)}, u32[]{:S(2)}) collective-permute-start(bf16[96,1536]{1,0:T(8,128)(2,1)S(1)} %get-tuple-element.125), channel_id=1, source_target_pairs={{0,24},{4,28},{8,0},{12,4},{16,8},{20,12},{24,16},{28,20},{1,25},{... | collective-permute-start | bytes 884744 | tf_op jit(solution)/shard_map/ppermute | solution.py:82
  84.3 10.4 %collective-permute-start.23 = (bf16[256,768]{1,0:T(8,128)(2,1)S(1)}, bf16[256,768]{1,0:T(8,128)(2,1)S(1)}, u32[]{:S(2)}, u32[]{:S(2)}) collective-permute-start(bf16[256,768]{1,0:T(8,128)(2,1)S(1)} %get-tuple-element.102), channel_id=1, source_target_pairs={{0,2},{2,0},{1,3},{3,1},{4,6},{6,4},{5,7},{7,5},{8,10},{10,8},{9,1... | collective-permute-start | bytes 1179656 | tf_op jit(solution)/shard_map/ppermute | solution.py:77
  92.9 11.8 %collective-permute-start.43 = (bf16[96,1536]{1,0:T(8,128)(2,1)S(1)}, bf16[96,1536]{1,0:T(8,128)(2,1)S(1)}, u32[]{:S(2)}, u32[]{:S(2)}) collective-permute-start(bf16[96,1536]{1,0:T(8,128)(2,1)S(1)} %add_convert_fusion.2), channel_id=1, source_target_pairs={{0,8},{4,12},{8,16},{12,20},{16,24},{20,28},{24,0},{28,4},{1,9},{5... | collective-permute-start | bytes 884744 | tf_op jit(solution)/shard_map/ppermute | solution.py:82
  94.8 14.0 %collective-permute-start.24 = (bf16[128,768]{1,0:T(8,128)(2,1)S(1)}, bf16[128,768]{1,0:T(8,128)(2,1)S(1)}, u32[]{:S(2)}, u32[]{:S(2)}) collective-permute-start(bf16[128,768]{1,0:T(8,128)(2,1)S(1)} %slice.37), channel_id=1, source_target_pairs={{0,1},{1,0},{2,3},{3,2},{4,5},{5,4},{6,7},{7,6},{8,9},{9,8},{10,11... | collective-permute-start | bytes 589832 | tf_op jit(solution)/shard_map/ppermute | solution.py:77
  96.2 11.1 %collective-permute-start.37 = (bf16[96,896]{1,0:T(8,128)(2,1)S(1)}, bf16[96,896]{1,0:T(8,128)(2,1)S(1)}, u32[]{:S(2)}, u32[]{:S(2)}) collective-permute-start(bf16[96,896]{1,0:T(8,128)(2,1)S(1)} %get-tuple-element.131), channel_id=1, source_target_pairs={{0,24},{4,28},{8,0},{12,4},{16,8},{20,12},{24,16},{28,20},{1,25},{... | collective-permute-start | bytes 516104 | tf_op jit(solution)/shard_map/ppermute | solution.py:82
  98.8 9.3 %collective-permute-start.38 = (bf16[96,896]{1,0:T(8,128)(2,1)S(1)}, bf16[96,896]{1,0:T(8,128)(2,1)S(1)}, u32[]{:S(2)}, u32[]{:S(2)}) collective-permute-start(bf16[96,896]{1,0:T(8,128)(2,1)S(1)} %get-tuple-element.133), channel_id=1, source_target_pairs={{0,4},{4,0},{8,12},{12,8},{16,20},{20,16},{24,28},{28,24},{1,5},{5... | collective-permute-start | bytes 516104 | tf_op jit(solution)/shard_map/ppermute | solution.py:82
  104.8 14.8 %collective-permute-start.45 = (bf16[96,1536]{1,0:T(8,128)(2,1)S(1)}, bf16[96,1536]{1,0:T(8,128)(2,1)S(1)}, u32[]{:S(2)}, u32[]{:S(2)}) collective-permute-start(bf16[96,1536]{1,0:T(8,128)(2,1)S(1)} %add_convert_fusion), channel_id=1, source_target_pairs={{0,8},{4,12},{8,16},{12,20},{16,24},{20,28},{24,0},{28,4},{1,9},{5... | collective-permute-start | bytes 884744 | tf_op jit(solution)/shard_map/ppermute | solution.py:82
  104.9 12.0 %collective-permute-start.31 = (bf16[128,768]{1,0:T(8,128)(2,1)S(1)}, bf16[128,768]{1,0:T(8,128)(2,1)S(1)}, u32[]{:S(2)}, u32[]{:S(2)}) collective-permute-start(bf16[128,768]{1,0:T(8,128)(2,1)S(1)} %slice.36), channel_id=1, source_target_pairs={{0,1},{1,0},{2,3},{3,2},{4,5},{5,4},{6,7},{7,6},{8,9},{9,8},{10,11... | collective-permute-start | bytes 589832 | tf_op jit(solution)/shard_map/ppermute | solution.py:77
  108.2 10.1 %collective-permute-start.39 = (bf16[96,896]{1,0:T(8,128)(2,1)S(1)}, bf16[96,896]{1,0:T(8,128)(2,1)S(1)}, u32[]{:S(2)}, u32[]{:S(2)}) collective-permute-start(bf16[96,896]{1,0:T(8,128)(2,1)S(1)} %add_convert_fusion.5), channel_id=1, source_target_pairs={{0,8},{4,12},{8,16},{12,20},{16,24},{20,28},{24,0},{28,4},{1,9},{5... | collective-permute-start | bytes 516104 | tf_op jit(solution)/shard_map/ppermute | solution.py:82
  108.9 11.7 %collective-permute-start.44 = (bf16[96,1536]{1,0:T(8,128)(2,1)S(1)}, bf16[96,1536]{1,0:T(8,128)(2,1)S(1)}, u32[]{:S(2)}, u32[]{:S(2)}) collective-permute-start(bf16[96,1536]{1,0:T(8,128)(2,1)S(1)} %add_convert_fusion.1), channel_id=1, source_target_pairs={{0,4},{4,0},{8,12},{12,8},{16,20},{20,16},{24,28},{28,24},{1,5},{5... | collective-permute-start | bytes 884744 | tf_op jit(solution)/shard_map/ppermute | solution.py:82
  (22 other events, 172.2 us)
